TPU v7x, 128 devices: a whole 4x4x4 slice. The times are simulated.
128 devices in a mesh: gx: 16 (over x, y), gy: 8 (over z, core).
Axes of the slice: x: 4, y: 4, z: 4, core: 2. Of those that a mesh axis runs over, the one named last changes fastest.
Arguments:
- state: bfloat16 [64, 24, 192, 256], P('gx', 'gy'), may hold values from -1 to 1
- weights: bfloat16 [64, 24, 9, 256, 256], P('gx', 'gy'), may hold values from -0.125 to 0.125
- drive: bfloat16 [2, 64, 24, 192, 256], P(None, 'gx', 'gy'), may hold values from -6 to 6
- leak: float32 [64, 24, 256], P('gx', 'gy'), may hold values from 0.1 to 1
- link_dev: int32 [16, 8, 12, 3], P(None, 'gy'), may hold values from 0 to 15, all different within a row; in each aligned block of 12 rows (0 to 11, 12 to 23, ..., all dimensions but the last counted through in order) at most 4 rows name the same one
- link_blk: int32 [16, 8, 12, 3], P(None, 'gy'), may hold values from 0 to 11
- offsets: int32 [5, 2], replicated, may hold values from -1 to 1, as said below
- gram_prev: float32 [64, 24, 256, 256], P('gx', 'gy'), may hold values from -6 to 6
Outputs:
- final_state: bfloat16 [64, 24, 192, 256], P('gx', 'gy')
- gram: float32 [64, 24, 256, 256], P('gx', 'gy')
Inputs may be any that keep to these rules, and one draw needn't show every extreme that they name: `link_dev`: the 3 sources of one block lie on different indices of gx; among the blocks of one device at most 4 sources lie on any one index of gx, and exactly 4 on some. Five distinct offsets.
All inputs are finite; a program needn't handle non-finite values.
Results may differ from a plain program's by a relative error of at most 0.0046.
Values may be sent and summed in bfloat16 or wider, within the bound.
No kernel may reach another device: no remote copies, remote signals or barrier semaphores. Data moves between devices by JAX's collectives and lax.ppermute only.
A program may use at most 192 MiB of HBM per device.

v0:
```python
import jax
import jax.numpy as jnp
from jax import lax
from jax.sharding import PartitionSpec as P


def padded(x, sides, width):
    for axis, dim in sides:
        size, length = (lax.axis_size(axis), x.shape[dim])
        up = [(i, (i + 1) % size) for i in range(size - 1)]
        down = [(j, i) for i, j in up]
        last = lax.slice_in_dim(x, length - width, length, axis=dim)
        first = lax.slice_in_dim(x, 0, width, axis=dim)
        before = lax.ppermute(last, axis, up)
        after = lax.ppermute(first, axis, down)
        x = jnp.concatenate([before, x, after], axis=dim)
    return x


def shards(state, weights, drive, leak, link_dev, link_blk, offsets, gram_prev):
    grid_rows, grid_cols, batch_cols, units = state.shape
    nblocks = grid_rows * grid_cols
    nlinks = link_dev.shape[-1]
    nstencil = offsets.shape[0]
    gx_size = lax.axis_size("gx")
    own_index = lax.axis_index("gx")
    all_dev = link_dev[:, 0].reshape(gx_size, nblocks * nlinks)
    all_blk = link_blk[:, 0].reshape(gx_size, nblocks * nlinks)
    my_dev = lax.dynamic_index_in_dim(all_dev, own_index, 0, keepdims=False)
    my_blk = lax.dynamic_index_in_dim(all_blk, own_index, 0, keepdims=False)
    w_long = weights[:, :, nstencil : nstencil + nlinks].reshape(nblocks, nlinks, units, units)
    current = state
    gram = gram_prev
    for step_id in range(drive.shape[0]):
        extended = padded(current, (("gx", 0), ("gy", 1)), 1)
        preact = jnp.zeros((grid_rows, grid_cols, batch_cols, units), jnp.float32)
        for offset_id in range(nstencil):
            zero = jnp.zeros((), jnp.int32)
            start_r = 1 + offsets[offset_id, 0]
            start_c = 1 + offsets[offset_id, 1]
            nearby = lax.dynamic_slice(
                extended, (start_r, start_c, zero, zero), (grid_rows, grid_cols, batch_cols, units)
            )
            preact = preact + jnp.einsum(
                "rcsu,rcuv->rcsv",
                nearby,
                weights[:, :, offset_id],
                preferred_element_type=jnp.float32,
            )
        flat_state = current.reshape(nblocks, batch_cols, units)
        whole = lax.all_gather(flat_state[None], "gx", axis=0, tiled=True)
        picked = whole.reshape(gx_size * nblocks, batch_cols, units)[my_dev * nblocks + my_blk]
        picked = picked.reshape(nblocks, nlinks, batch_cols, units)
        distant = jnp.einsum("blsu,bluv->bsv", picked, w_long, preferred_element_type=jnp.float32)
        preact = preact + distant.reshape(grid_rows, grid_cols, batch_cols, units)
        preact = preact + jnp.einsum(
            "rcsu,rcuv->rcsv",
            drive[step_id],
            weights[:, :, nstencil + nlinks],
            preferred_element_type=jnp.float32,
        )
        rate = leak[:, :, None, :]
        current = ((1.0 - rate) * current.astype(jnp.float32) + rate * jnp.tanh(preact)).astype(
            jnp.bfloat16
        )
        gram = gram + jnp.einsum(
            "rcsu,rcsv->rcuv", current, current, preferred_element_type=jnp.float32
        )
    return (current, gram)


def solution(mesh):
    return jax.shard_map(
        shards,
        mesh=mesh,
        in_specs=(
            P("gx", "gy", None, None),
            P("gx", "gy", None, None, None),
            P(None, "gx", "gy", None, None),
            P("gx", "gy", None),
            P(None, "gy", None, None),
            P(None, "gy", None, None),
            P(),
            P("gx", "gy", None, None),
        ),
        out_specs=(P("gx", "gy", None, None), P("gx", "gy", None, None)),
        check_vma=False,
    )
```

profile of v0, /device:TPU:12, one launch (start us, length us, event | category | flops | bytes accessed | tf_op | source)
XLA Modules:
  0.0 306.5 jit_solution(16424521632391896462)
XLA Ops:
  11.4 3.5 %collective-permute-start = (bf16[1,3,192,256]{3,2,1,0:T(8,128)(2,1)S(1)}, bf16[1,3,192,256]{3,2,1,0:T(8,128)(2,1)S(1)}, u32[]{:S(2)}, u32[]{:S(2)}) collective-permute-start(bf16[1,3,192,256]{3,2,1,0:T(8,128)(2,1)S(1)} %get-tuple-element.9), channel_id=1, source_target_pairs={{0,8},{8,16},{16,24},{24,32},{32,40},{40,48},{48,56},{56,64},{64,7... | collective-permute-start | bytes 884744 | tf_op jit(solution)/shard_map/ppermute | solution.py:14
  29.1 5.2 %slice.116 = bf16[4,3,3,256,256]{4,3,2,1,0:T(8,128)(2,1)} slice(bf16[4,3,9,256,256]{4,3,2,1,0:T(8,128)(2,1)} %param.9), slice={[0:4], [0:3], [5:8], [0:256], [0:256]} | slice | bytes 9437184 | tf_op jit(solution)/shard_map/slice | solution.py:31
  37.6 3.3 %fusion.2 = f32[4,3,192,256]{3,2,1,0:T(8,128)} fusion(bf16[4,3,9,256,256]{4,3,2,1,0:T(8,128)(2,1)} %param.9, bf16[2,4,3,192,256]{4,3,2,1,0:T(8,128)(2,1)S(1)} %copy-done.16), kind=kOutput, calls=%fused_computation.9 | convolution fusion | flops 301989888 | bytes 5111808 | tf_op jit(solution)/shard_map/rcsu,rcuv->rcsv/dot_general | solution.py:56
  42.6 3.4 %fusion.14 = f32[4,3,192,256]{3,2,1,0:T(8,128)} fusion(bf16[4,3,9,256,256]{4,3,2,1,0:T(8,128)(2,1)} %param.9, bf16[6,5,192,256]{3,2,1,0:T(8,128)(2,1)S(1)} %pad_maximum_fusion, s32[]{:T(128)S(6)} %select_n.62, s32[]{:T(128)S(6)} %select_n.63), kind=kOutput, calls=%fused_computation.17 | convolution fusion | flops 301989888 | bytes 5111816 | tf_op jit(solution)/shard_map/rcsu,rcuv->rcsv/dot_general | solution.py:44
  46.0 3.3 %fusion.18 = f32[4,3,192,256]{3,2,1,0:T(8,128)} fusion(bf16[4,3,9,256,256]{4,3,2,1,0:T(8,128)(2,1)} %param.9, bf16[6,5,192,256]{3,2,1,0:T(8,128)(2,1)S(1)} %pad_maximum_fusion, s32[]{:T(128)S(6)} %select_n.60, s32[]{:T(128)S(6)} %select_n.61), kind=kOutput, calls=%fused_computation.21 | convolution fusion | flops 301989888 | bytes 5111816 | tf_op jit(solution)/shard_map/rcsu,rcuv->rcsv/dot_general | solution.py:44
  49.3 3.3 %fusion.22 = f32[4,3,192,256]{3,2,1,0:T(8,128)} fusion(bf16[4,3,9,256,256]{4,3,2,1,0:T(8,128)(2,1)} %param.9, bf16[6,5,192,256]{3,2,1,0:T(8,128)(2,1)S(1)} %pad_maximum_fusion, s32[]{:T(128)S(6)} %select_n.58, s32[]{:T(128)S(6)} %select_n.59), kind=kOutput, calls=%fused_computation.25 | convolution fusion | flops 301989888 | bytes 5111816 | tf_op jit(solution)/shard_map/rcsu,rcuv->rcsv/dot_general | solution.py:44
  52.5 3.5 %fusion.26 = f32[4,3,192,256]{3,2,1,0:T(8,128)} fusion(bf16[4,3,9,256,256]{4,3,2,1,0:T(8,128)(2,1)} %param.9, bf16[6,5,192,256]{3,2,1,0:T(8,128)(2,1)S(1)} %pad_maximum_fusion, s32[]{:T(128)S(6)} %select_n.56, s32[]{:T(128)S(6)} %select_n.57), kind=kOutput, calls=%fused_computation.29 | convolution fusion | flops 301989888 | bytes 5111816 | tf_op jit(solution)/shard_map/rcsu,rcuv->rcsv/dot_general | solution.py:44
  56.0 77.2 %all-gather.3.cloned.1.call-done = bf16[16,12,192,256]{3,2,1,0:T(8,128)(2,1)} async-done(((bf16[1,12,192,256]{3,2,1,0:T(8,128)(2,1)}), bf16[16,12,192,256]{3,2,1,0:T(8,128)(2,1)}) %all-gather.3.cloned.1.call-update) | async-done | bytes 18874384 | tf_op jit(solution)/shard_map/all_gather | solution.py:51
  133.2 9.3 %gather_fusion = bf16[36,192,256]{2,1,0:T(8,128)(2,1)} fusion(bf16[192,192,256]{2,1,0:T(8,128)(2,1)} %bitcast.111, s32[1024]{0:T(1024)S(1)} %pad_clamp_fusion), kind=kCustom, calls=%fused_computation | custom fusion | bytes 7078032 | tf_op jit(solution)/shard_map/gather | solution.py:52
  142.5 4.6 %fusion.69 = f32[12,192,256,1]{2,1,3,0:T(8,128)S(1)} fusion(bf16[12,3,192,256]{3,2,1,0:T(8,128)(2,1)} %bitcast.107, bf16[12,3,256,256]{3,2,1,0:T(8,128)(2,1)} %bitcast.104), kind=kOutput, calls=%fused_computation.82 | convolution fusion | flops 905969664 | bytes 10616832 | tf_op jit(solution)/shard_map/blsu,bluv->bsv/dot_general | solution.py:54
  149.6 3.7 %add_convert_fusion.1 = bf16[4,3,192,256]{3,2,1,0:T(8,128)(2,1)} fusion(f32[4,3,192,256]{3,2,1,0:T(8,128)S(1)} %copy-done.14, f32[4,3,192,256]{3,2,1,0:T(8,128)S(1)} %bitcast.110, f32[4,3,192,256]{3,2,1,0:T(8,128)S(1)} %copy-done.5, f32[4,3,192,256]{3,2,1,0:T(8,128)S(1)} %copy-done.6, f32[4,3,192,256]{3,2,1,0:T(8,128)S(1)} %copy-done.8, ...), kind=kOutput, calls=%fused_computation.6 | convolution fusion | flops 308477952 | bytes 19300360 | tf_op jit(solution)/shard_map/rcsu,rcuv->rcsv/dot_general | solution.py:44
  154.6 3.1 %collective-permute-start.4 = (bf16[1,3,192,256]{3,2,1,0:T(8,128)(2,1)S(1)}, bf16[1,3,192,256]{3,2,1,0:T(8,128)(2,1)S(1)}, u32[]{:S(2)}, u32[]{:S(2)}) collective-permute-start(bf16[1,3,192,256]{3,2,1,0:T(8,128)(2,1)S(1)} %get-tuple-element.6), channel_id=1, source_target_pairs={{0,8},{8,16},{16,24},{24,32},{32,40},{40,48},{48,56},{56,64},{64,7... | collective-permute-start | bytes 884744 | tf_op jit(solution)/shard_map/ppermute | solution.py:14
  157.7 2.7 collective-permute-start.5
  160.5 4.8 %collective-permute-done.4 = bf16[1,3,192,256]{3,2,1,0:T(8,128)(2,1)S(1)} collective-permute-done((bf16[1,3,192,256]{3,2,1,0:T(8,128)(2,1)S(1)}, bf16[1,3,192,256]{3,2,1,0:T(8,128)(2,1)S(1)}, u32[]{:S(2)}, u32[]{:S(2)}) %collective-permute-start.4) | collective-permute-done | bytes 294944 | tf_op jit(solution)/shard_map/ppermute | solution.py:14
  165.3 2.8 collective-permute-done.5
  171.1 3.4 %fusion = f32[4,3,192,256]{3,2,1,0:T(8,128)} fusion(bf16[4,3,9,256,256]{4,3,2,1,0:T(8,128)(2,1)} %param.9, bf16[2,4,3,192,256]{4,3,2,1,0:T(8,128)(2,1)S(1)} %copy-done.17), kind=kOutput, calls=%fused_computation.7 | convolution fusion | flops 301989888 | bytes 5111808 | tf_op jit(solution)/shard_map/rcsu,rcuv->rcsv/dot_general | solution.py:56
  177.2 3.0 fusion.12
  180.2 3.3 %fusion.16 = f32[4,3,192,256]{3,2,1,0:T(8,128)} fusion(bf16[4,3,9,256,256]{4,3,2,1,0:T(8,128)(2,1)} %param.9, bf16[6,5,192,256]{3,2,1,0:T(8,128)(2,1)S(1)} %pad_maximum_fusion.1, s32[]{:T(128)S(6)} %select_n.60, s32[]{:T(128)S(6)} %select_n.61), kind=kOutput, calls=%fused_computation.19 | convolution fusion | flops 301989888 | bytes 5111816 | tf_op jit(solution)/shard_map/rcsu,rcuv->rcsv/dot_general | solution.py:44
  183.5 3.3 %fusion.20 = f32[4,3,192,256]{3,2,1,0:T(8,128)} fusion(bf16[4,3,9,256,256]{4,3,2,1,0:T(8,128)(2,1)} %param.9, bf16[6,5,192,256]{3,2,1,0:T(8,128)(2,1)S(1)} %pad_maximum_fusion.1, s32[]{:T(128)S(6)} %select_n.58, s32[]{:T(128)S(6)} %select_n.59), kind=kOutput, calls=%fused_computation.23 | convolution fusion | flops 301989888 | bytes 5111816 | tf_op jit(solution)/shard_map/rcsu,rcuv->rcsv/dot_general | solution.py:44
  186.8 3.3 %fusion.24 = f32[4,3,192,256]{3,2,1,0:T(8,128)} fusion(bf16[4,3,9,256,256]{4,3,2,1,0:T(8,128)(2,1)} %param.9, bf16[6,5,192,256]{3,2,1,0:T(8,128)(2,1)S(1)} %pad_maximum_fusion.1, s32[]{:T(128)S(6)} %select_n.56, s32[]{:T(128)S(6)} %select_n.57), kind=kOutput, calls=%fused_computation.27 | convolution fusion | flops 301989888 | bytes 5111816 | tf_op jit(solution)/shard_map/rcsu,rcuv->rcsv/dot_general | solution.py:44
  190.2 87.9 %all-gather.5.cloned.1.call-done = bf16[16,12,192,256]{3,2,1,0:T(8,128)(2,1)} async-done(((bf16[1,12,192,256]{3,2,1,0:T(8,128)(2,1)}), bf16[16,12,192,256]{3,2,1,0:T(8,128)(2,1)}) %all-gather.5.cloned.1.call-update) | async-done | bytes 18874384 | tf_op jit(solution)/shard_map/all_gather | solution.py:51
  278.0 9.4 %gather_fusion.1 = bf16[36,192,256]{2,1,0:T(8,128)(2,1)} fusion(bf16[192,192,256]{2,1,0:T(8,128)(2,1)} %bitcast.112, s32[1024]{0:T(1024)} %copy-done.24), kind=kCustom, calls=%fused_computation.1 | custom fusion | bytes 7078032 | tf_op jit(solution)/shard_map/gather | solution.py:52
  287.4 4.6 %fusion.70 = f32[12,192,256,1]{2,1,3,0:T(8,128)S(1)} fusion(bf16[12,3,192,256]{3,2,1,0:T(8,128)(2,1)} %bitcast.106, bf16[12,3,256,256]{3,2,1,0:T(8,128)(2,1)} %bitcast.105), kind=kOutput, calls=%fused_computation.83 | convolution fusion | flops 905969664 | bytes 10616832 | tf_op jit(solution)/shard_map/blsu,bluv->bsv/dot_general | solution.py:54
  293.6 3.4 %add_convert_fusion = bf16[4,3,192,256]{3,2,1,0:T(8,128)(2,1)S(1)} fusion(f32[4,3,192,256]{3,2,1,0:T(8,128)S(1)} %copy-done.13, f32[4,3,192,256]{3,2,1,0:T(8,128)S(1)} %bitcast.109, f32[4,3,192,256]{3,2,1,0:T(8,128)S(1)} %fusion.12, f32[4,3,192,256]{3,2,1,0:T(8,128)S(1)} %copy-done.2, f32[4,3,192,256]{3,2,1,0:T(8,128)S(1)} %copy-done.4, ...), kind=kOutput, calls=%fused_computation.5 | convolution fusion | flops 308477952 | bytes 19292168 | tf_op jit(solution)/shard_map/rcsu,rcuv->rcsv/dot_general | solution.py:44
  (87 shorter events, 23.7 us)
Async XLA Ops:
  7.2 7.8 %copy-start.20 = (f32[4,3,256]{2,0,1:T(4,128)S(1)}, f32[4,3,256]{2,0,1:T(4,128)}, u32[]{:S(2)}) copy-start(f32[4,3,256]{2,0,1:T(4,128)} %param.11) | copy-start | bytes 36868
  7.2 7.8 %copy-start.21 = (s32[5,2]{0,1:T(2,128)S(1)}, s32[5,2]{0,1:T(2,128)}, u32[]{:S(2)}) copy-start(s32[5,2]{0,1:T(2,128)} %param.14) | copy-start | bytes 124
  7.2 21.8 %copy-start.22 = (s32[16,1,12,3]{0,1,3,2:T(1,128)S(1)}, s32[16,1,12,3]{0,1,3,2:T(1,128)}, u32[]{:S(2)}) copy-start(s32[16,1,12,3]{0,1,3,2:T(1,128)} %param.12) | copy-start | bytes 6916
  7.2 21.8 %copy-start.23 = (s32[16,1,12,3]{0,1,3,2:T(1,128)S(1)}, s32[16,1,12,3]{0,1,3,2:T(1,128)}, u32[]{:S(2)}) copy-start(s32[16,1,12,3]{0,1,3,2:T(1,128)} %param.13) | copy-start | bytes 6916
  7.2 126.0 %all-gather.3.cloned.1.call-start = ((), (), s32[]{:S(2)}) async-start(), calls=%async_computation | async-start | bytes 20054016 | tf_op jit(solution)/shard_map/all_gather | solution.py:51
  7.9 270.1 %all-gather.5.cloned.1.call-start = ((), (), s32[]{:S(2)}) async-start(), calls=%async_computation.1 | async-start | bytes 20054016 | tf_op jit(solution)/shard_map/all_gather | solution.py:51
  9.1 25.6 %collective-permute-start.1 = (bf16[1,3,192,256]{3,2,1,0:T(8,128)(2,1)S(1)}, bf16[1,3,192,256]{3,2,1,0:T(8,128)(2,1)S(1)}, u32[]{:S(2)}, u32[]{:S(2)}) collective-permute-start(bf16[1,3,192,256]{3,2,1,0:T(8,128)(2,1)S(1)} %get-tuple-element.8), channel_id=1, source_target_pairs={{8,0},{16,8},{24,16},{32,24},{40,32},{48,40},{56,48},{64,56},{72,6... | collective-permute-start | bytes 884744 | tf_op jit(solution)/shard_map/ppermute | solution.py:15
  11.4 23.1 %collective-permute-start = (bf16[1,3,192,256]{3,2,1,0:T(8,128)(2,1)S(1)}, bf16[1,3,192,256]{3,2,1,0:T(8,128)(2,1)S(1)}, u32[]{:S(2)}, u32[]{:S(2)}) collective-permute-start(bf16[1,3,192,256]{3,2,1,0:T(8,128)(2,1)S(1)} %get-tuple-element.9), channel_id=1, source_target_pairs={{0,8},{8,16},{16,24},{24,32},{32,40},{40,48},{48,56},{56,64},{64,7... | collective-permute-start | bytes 884744 | tf_op jit(solution)/shard_map/ppermute | solution.py:14
  28.9 118.2 %copy-start.18 = (f32[4,3,256]{2,1,0:T(4,128)}, f32[4,3,256]{2,1,0:T(4,128)S(1)}, u32[]{:S(2)}) copy-start(f32[4,3,256]{2,1,0:T(4,128)S(1)} %copy.36) | copy-start | bytes 36868
  34.8 6.2 %collective-permute-start.2 = (bf16[6,1,192,256]{3,2,1,0:T(8,128)(2,1)S(1)}, bf16[6,1,192,256]{3,2,1,0:T(8,128)(2,1)S(1)}, u32[]{:S(2)}, u32[]{:S(2)}) collective-permute-start(bf16[6,1,192,256]{3,2,1,0:T(8,128)(2,1)S(1)} %get-tuple-element.4), channel_id=1, source_target_pairs={{0,1},{1,2},{2,3},{3,4},{4,5},{5,6},{6,7},{8,9},{9,10},{10,11},{11... | collective-permute-start | bytes 1769480 | tf_op jit(solution)/shard_map/ppermute | solution.py:14
  36.3 6.0 %collective-permute-start.3 = (bf16[6,1,192,256]{3,2,1,0:T(8,128)(2,1)S(1)}, bf16[6,1,192,256]{3,2,1,0:T(8,128)(2,1)S(1)}, u32[]{:S(2)}, u32[]{:S(2)}) collective-permute-start(bf16[6,1,192,256]{3,2,1,0:T(8,128)(2,1)S(1)} %get-tuple-element.5), channel_id=1, source_target_pairs={{1,0},{2,1},{3,2},{4,3},{5,4},{6,5},{7,6},{9,8},{10,9},{11,10},{12... | collective-permute-start | bytes 1769480 | tf_op jit(solution)/shard_map/ppermute | solution.py:15
  37.6 95.6 %copy-start.24 = (s32[1024]{0:T(1024)}, s32[1024]{0:T(1024)S(1)}, u32[]{:S(2)}) copy-start(s32[1024]{0:T(1024)S(1)} %pad_clamp_fusion) | copy-start | bytes 12292
  142.4 6.2 %copy-start.8 = (f32[4,3,192,256]{3,2,1,0:T(8,128)S(1)}, f32[4,3,192,256]{3,2,1,0:T(8,128)}, u32[]{:S(2)}) copy-start(f32[4,3,192,256]{3,2,1,0:T(8,128)} %fusion.26) | copy-start | bytes 7077892
  142.5 6.4 %copy-start.10 = (bf16[4,3,192,256]{3,2,1,0:T(8,128)(2,1)S(1)}, bf16[4,3,192,256]{3,2,1,0:T(8,128)(2,1)}, u32[]{:S(2)}) copy-start(bf16[4,3,192,256]{3,2,1,0:T(8,128)(2,1)} %param.8) | copy-start | bytes 3538948
  142.5 7.2 %copy-start.14 = (f32[4,3,192,256]{3,2,1,0:T(8,128)S(1)}, f32[4,3,192,256]{3,2,1,0:T(8,128)}, u32[]{:S(2)}) copy-start(f32[4,3,192,256]{3,2,1,0:T(8,128)} %fusion.2) | copy-start | bytes 7077892
  153.3 14.8 %copy-start = (bf16[4,3,192,256]{3,2,1,0:T(8,128)(2,1)S(1)}, bf16[4,3,192,256]{3,2,1,0:T(8,128)(2,1)}, u32[]{:S(2)}) copy-start(bf16[4,3,192,256]{3,2,1,0:T(8,128)(2,1)} %add_convert_fusion.1) | copy-start | bytes 3538948
  153.4 17.7 %copy-start.17 = (bf16[2,4,3,192,256]{4,3,2,1,0:T(8,128)(2,1)S(1)}, bf16[2,4,3,192,256]{4,3,2,1,0:T(8,128)(2,1)}, u32[]{:S(2)}) copy-start(bf16[2,4,3,192,256]{4,3,2,1,0:T(8,128)(2,1)} %param.10) | copy-start | bytes 7077892
  154.6 10.7 %collective-permute-start.4 = (bf16[1,3,192,256]{3,2,1,0:T(8,128)(2,1)S(1)}, bf16[1,3,192,256]{3,2,1,0:T(8,128)(2,1)S(1)}, u32[]{:S(2)}, u32[]{:S(2)}) collective-permute-start(bf16[1,3,192,256]{3,2,1,0:T(8,128)(2,1)S(1)} %get-tuple-element.6), channel_id=1, source_target_pairs={{0,8},{8,16},{16,24},{24,32},{32,40},{40,48},{48,56},{56,64},{64,7... | collective-permute-start | bytes 884744 | tf_op jit(solution)/shard_map/ppermute | solution.py:14
  157.7 10.4 %collective-permute-start.5 = (bf16[1,3,192,256]{3,2,1,0:T(8,128)(2,1)S(1)}, bf16[1,3,192,256]{3,2,1,0:T(8,128)(2,1)S(1)}, u32[]{:S(2)}, u32[]{:S(2)}) collective-permute-start(bf16[1,3,192,256]{3,2,1,0:T(8,128)(2,1)S(1)} %get-tuple-element.7), channel_id=1, source_target_pairs={{8,0},{16,8},{24,16},{32,24},{40,32},{48,40},{56,48},{64,56},{72,6... | collective-permute-start | bytes 884744 | tf_op jit(solution)/shard_map/ppermute | solution.py:15
  168.2 8.5 %collective-permute-start.6 = (bf16[6,1,192,256]{3,2,1,0:T(8,128)(2,1)S(1)}, bf16[6,1,192,256]{3,2,1,0:T(8,128)(2,1)S(1)}, u32[]{:S(2)}, u32[]{:S(2)}) collective-permute-start(bf16[6,1,192,256]{3,2,1,0:T(8,128)(2,1)S(1)} %get-tuple-element.2), channel_id=1, source_target_pairs={{0,1},{1,2},{2,3},{3,4},{4,5},{5,6},{6,7},{8,9},{9,10},{10,11},{11... | collective-permute-start | bytes 1769480 | tf_op jit(solution)/shard_map/ppermute | solution.py:14
  169.6 7.2 %collective-permute-start.7 = (bf16[6,1,192,256]{3,2,1,0:T(8,128)(2,1)S(1)}, bf16[6,1,192,256]{3,2,1,0:T(8,128)(2,1)S(1)}, u32[]{:S(2)}, u32[]{:S(2)}) collective-permute-start(bf16[6,1,192,256]{3,2,1,0:T(8,128)(2,1)S(1)} %get-tuple-element.3), channel_id=1, source_target_pairs={{1,0},{2,1},{3,2},{4,3},{5,4},{6,5},{7,6},{9,8},{10,9},{11,10},{12... | collective-permute-start | bytes 1769480 | tf_op jit(solution)/shard_map/ppermute | solution.py:15
  177.2 9.6 %copy-start.1 = (bf16[6,5,192,256]{3,2,1,0:T(8,128)(2,1)}, bf16[6,5,192,256]{3,2,1,0:T(8,128)(2,1)S(1)}, u32[]{:S(2)}) copy-start(bf16[6,5,192,256]{3,2,1,0:T(8,128)(2,1)S(1)} %pad_maximum_fusion.1) | copy-start | bytes 8847364
  287.4 6.2 %copy-start.13 = (f32[4,3,192,256]{3,2,1,0:T(8,128)S(1)}, f32[4,3,192,256]{3,2,1,0:T(8,128)}, u32[]{:S(2)}) copy-start(f32[4,3,192,256]{3,2,1,0:T(8,128)} %fusion) | copy-start | bytes 7077892
  287.4 6.2 %copy-start.19 = (f32[4,3,256]{2,1,0:T(4,128)S(1)}, f32[4,3,256]{2,1,0:T(4,128)}, u32[]{:S(2)}) copy-start(f32[4,3,256]{2,1,0:T(4,128)} %copy-done.18) | copy-start | bytes 36868
  (11 other events, 47.9 us)
Sparse Core Ops, SparseCore 0:
  10.2 122.8 all-gather.2
  153.5 124.4 all-gather.4
where the time goes:
time: 310 us; the launch traced here: 307 us
  waiting for transfers between devices  175 us (56%)
  matrix products  54.1 us (17%)
  local copies, waits for them, and re-layouts  31.5 us (10%)
  between operations  27.7 us (9%)
  starting transfers between devices  17.3 us (6%)
    all_gather x2, waiting for transfers between devices, shards(): whole = lax.all_gather(flat_state[None], 'gx', axis=0, tiled=True)  165 us
    dot_general x10, matrix products, shards(): jnp.einsum('rcsu,rcuv->rcsv', nearby, weights[:, :, offset_id], preferred...  33.4 us
    gather x2, local copies, waits for them, and re-layouts, shards(): whole.reshape(gx_size * nblocks, batch_cols, units)  18.7 us
    ppermute x4, starting transfers between devices, padded(): before = lax.ppermute(last, axis, up)  9.37 us
    dot_general x2, matrix products, shards(): jnp.einsum('blsu,bluv->bsv', picked, w_long, preferred_element_type=jnp.f...  9.28 us
    ppermute x4, starting transfers between devices, padded(): after = lax.ppermute(first, axis, down)  7.87 us
    dot_general x2, matrix products, shards(): jnp.einsum('rcsu,rcuv->rcsv', drive[step_id], weights[:, :, nstencil + nl...  6.69 us
  transfers between devices with their start and end apart: 10, of which 5 were waited for; matrix products, arithmetic and copies ran while one was open for 15% of the time, Pallas kernels for 0%

commit v1 on v0

v1 whole, which is shorter than its diff:
```python
import functools

import jax
import jax.numpy as jnp
from jax import lax
from jax.experimental import pallas as pl
from jax.experimental.pallas import tpu as pltpu
from jax.sharding import Mesh, PartitionSpec as P

VMEM_BYTES = 56 * 1024 * 1024
ANY = pl.BlockSpec(memory_space=pl.ANY)
SMEM = pl.BlockSpec(memory_space=pltpu.SMEM)
VMEM = pl.BlockSpec(memory_space=pltpu.VMEM)
RING = 4


def plan_kernel(dims, pos, dev, blk, offs, send, near, far, count, seen):
    rows, cols, nlinks, nstencil, cap, ngx, ngy = dims
    nblk = rows * cols
    me, band = pos[0], pos[1]
    mine = (me // RING, me % RING)
    dests = [me]
    dests += [((mine[0] + way) % RING) * RING + mine[1] for way in range(1, RING)]
    dests += [mine[0] * RING + (mine[1] + way) % RING for way in range(1, RING)]

    @pl.loop(0, ngx)
    def _(i):
        for n in range(len(dests)):
            seen[n, i] = 0

    for half in range(2):
        for kind in range(2 * RING):
            count[half, kind] = 0
        for way in range(RING - 1):
            for rel in range(RING):
                for i in range(cap):
                    send[half, way, rel, i] = 0

    @pl.loop(0, nblk)
    def _(q):
        for l in range(nlinks):
            for n, dest in enumerate(dests):
                d = dev[dest, 0, q, l]
                at = (d // RING, d % RING)
                i = seen[n, d]
                seen[n, d] = i + 1
                i = jnp.minimum(i, cap - 1)
                if n:
                    half, way = (n - 1) // (RING - 1), (n - 1) % (RING - 1)

                    @pl.when(at[half] == mine[half])
                    def _(half=half, way=way, at=at, i=i, dest=dest):
                        rel = (at[1 - half] - mine[1 - half] + RING) % RING
                        send[half, way, rel, i] = blk[dest, 0, q, l]

                    continue
                for half in range(2):
                    way = (at[half] - mine[half] + RING) % RING
                    rel = (at[1 - half] - mine[1 - half] + RING) % RING
                    own = blk[me, 0, q, l]
                    upper = (rel == RING // 2) & (own >= nblk // 2)
                    kind = jnp.where(way == 0, jnp.where(upper, 2 * RING - 1, rel), RING + way - 1)
                    place = jnp.where(way == 0, jnp.where(upper, own - nblk // 2, own), rel * cap + i)
                    k = count[half, kind]
                    far[half, kind, jnp.minimum(k, RING * cap - 1)] = place * 64 + q * nlinks + l
                    count[half, kind] = k + 1

    side = nblk + 2 * cols
    swap = band % 2
    left, right = side + (1 - swap) * (rows + 2), side + swap * (rows + 2)
    void = side + 2 * (rows + 2)

    @pl.loop(0, rows)
    def _(r0):
        for c0 in range(cols):
            for k in range(nstencil):
                r, t = r0 + offs[k, 0], c0 + offs[k, 1]
                code = jnp.where(r < 0, nblk + t, jnp.where(r >= rows, nblk + cols + t, r * cols + t))
                code = jnp.where(t < 0, left + r + 1, jnp.where(t >= cols, right + r + 1, code))
                out = (r < 0) & (me == 0) | (r >= rows) & (me == ngx - 1)
                out = out | (t < 0) & (band == 0) | (t >= cols) & (band == ngy - 1)
                near[(r0 * cols + c0) * nstencil + k] = jnp.where(out, void, code)


def pack_kernel(cap, send, *refs):
    nsrc, nout = 2 * (RING + 1), 2 * (RING - 1)
    srcs, outs = refs[:nsrc], refs[nsrc : nsrc + nout]
    pool, slots, sem, osem = refs[nsrc + nout :]
    loads, at = [], 0
    for i, src in enumerate(srcs):
        half = i // (RING + 1)
        at = 0 if i % (RING + 1) == 0 else at
        n = src.shape[0]
        loads.append(pltpu.make_async_copy(src, pool.at[half, pl.ds(at, n)], sem.at[i]))
        at += n
    for c in loads:
        c.start()
    nblk = srcs[0].shape[0]
    puts = []
    for half in range(2):
        for c in loads[half * (RING + 1) : (half + 1) * (RING + 1)]:
            c.wait()
        for way in range(RING - 1):
            n = half * (RING - 1) + way
            for rel in range(RING):
                for i in range(cap):
                    slots[n, rel * cap + i] = pool[half, rel * nblk + send[half, way, rel, i]]
            puts.append(pltpu.make_async_copy(slots.at[n], outs[n], osem.at[n]))
            puts[-1].start()
    for c in puts:
        c.wait()


def near_kernel(dims, nrim, grams, t, near, own_ref, *refs):
    nblk, nstencil, nsrc = dims
    rims, refs = refs[: len(nrim)], list(refs[len(nrim) :])
    w_ref, drive_ref = refs[:2]
    refs = refs[2:]
    gram_ref = refs.pop(0) if grams else None
    pre_ref = refs.pop(0)
    gram_out = refs.pop(0) if grams else None
    pool, wst, wdr, dr, pre, *refs = refs
    gin, gout = (refs.pop(0), refs.pop(0)) if grams else (None, None)
    sem, osem = refs
    units = own_ref.shape[-1]
    copies, at = [pltpu.make_async_copy(own_ref, pool.at[pl.ds(0, nblk)], sem.at[nblk])], nblk
    for i, n in enumerate(nrim):
        copies.append(pltpu.make_async_copy(rims[i], pool.at[pl.ds(at, n)], sem.at[nblk + i + 1]))
        at += n

    def ins(q):
        yield pltpu.make_async_copy(w_ref.at[q, pl.ds(0, nstencil)], wst.at[q], sem.at[q])
        yield pltpu.make_async_copy(w_ref.at[q, nsrc], wdr.at[q], sem.at[q])
        yield pltpu.make_async_copy(drive_ref.at[t, q], dr.at[q], sem.at[q])
        if grams:
            yield pltpu.make_async_copy(gram_ref.at[q], gin.at[q], sem.at[q])

    def puts(q):
        yield pltpu.make_async_copy(pre.at[q], pre_ref.at[q], osem.at[q])
        if grams:
            yield pltpu.make_async_copy(gout.at[q], gram_out.at[q], osem.at[q])

    for c in copies:
        c.start()

    @pl.loop(0, nblk)
    def _(q):
        for c in ins(q):
            c.start()

    pool[at] = jnp.zeros_like(pool[at])
    for c in copies:
        c.wait()

    @pl.loop(0, nblk)
    def _(q):
        for c in ins(q):
            c.wait()
        lhs = jnp.concatenate([pool[near[q * nstencil + k]] for k in range(nstencil)] + [dr[q]], axis=1)
        w = jnp.concatenate([wst[q].reshape(nstencil * units, units), wdr[q]], axis=0)
        pre[q] = jnp.dot(lhs, w, preferred_element_type=jnp.float32)
        if grams:
            x = pool[q]
            gout[q] = gin[q] + lax.dot_general(x, x, (((0,), (0,)), ((), ())), preferred_element_type=jnp.float32)
        for c in puts(q):
            c.start()

    @pl.loop(0, nblk)
    def _(q):
        for c in puts(q):
            c.wait()


def far_kernel(dims, last, far, count, *refs):
    nblk, h, nstencil, nlinks = dims
    nin = 4 * RING
    bufs, refs = refs[:nin], list(refs[nin:])
    own_ref, w_ref, pre_ref, leak_ref = refs[:4]
    refs = refs[4:]
    gram_ref = refs.pop(0) if last else None
    nout = 2 if last else 3
    outs, refs = refs[:nout], refs[nout:]
    got, old, wl, pre, new, *refs = refs
    gin, gout = (refs.pop(0), refs.pop(0)) if last else (None, None)
    sem, osem = refs

    for half in range(2):
        for kind in range(2 * RING):
            src = bufs[half * 2 * RING + kind]

            @pl.loop(0, count[half, kind])
            def _(n, half=half, kind=kind, src=src):
                e = far[half, kind, n]
                to = got.at[e % 64, pl.ds(half * h, h)]
                pltpu.make_async_copy(src.at[e // 64], to, sem.at[nblk]).start()

    def ins(q):
        yield pltpu.make_async_copy(own_ref.at[q], old.at[q], sem.at[q])
        yield pltpu.make_async_copy(w_ref.at[q, pl.ds(nstencil, nlinks)], wl.at[q], sem.at[q])
        yield pltpu.make_async_copy(pre_ref.at[q], pre.at[q], sem.at[q])
        if last:
            yield pltpu.make_async_copy(gram_ref.at[q], gin.at[q], sem.at[q])

    def puts(q):
        if last:
            yield pltpu.make_async_copy(new.at[q], outs[0].at[q], osem.at[q])
            yield pltpu.make_async_copy(gout.at[q], outs[1].at[q], osem.at[q])
        else:
            yield pltpu.make_async_copy(new.at[q, pl.ds(0, h)], outs[0].at[q], osem.at[q])
            yield pltpu.make_async_copy(new.at[q, pl.ds(h, h)], outs[1].at[q], osem.at[q])
            yield pltpu.make_async_copy(new.at[q], outs[2].at[q], osem.at[q])

    @pl.loop(0, nblk)
    def _(q):
        for c in ins(q):
            c.start()

    pltpu.make_async_copy(got, got, sem.at[nblk]).wait()

    @pl.loop(0, nblk)
    def _(q):
        for c in ins(q):
            c.wait()
        lhs = jnp.concatenate([got[q * nlinks + l] for l in range(nlinks)], axis=1)
        units = lhs.shape[-1] // nlinks
        w = wl[q].reshape(nlinks * units, units)
        total = pre[q] + jnp.dot(lhs, w, preferred_element_type=jnp.float32)
        rate = leak_ref[pl.ds(q, 1), :]
        fresh = ((1.0 - rate) * old[q].astype(jnp.float32) + rate * jnp.tanh(total)).astype(jnp.bfloat16)
        new[q] = fresh
        if last:
            gout[q] = gin[q] + lax.dot_general(
                fresh, fresh, (((0,), (0,)), ((), ())), preferred_element_type=jnp.float32
            )
        for c in puts(q):
            c.start()

    @pl.loop(0, nblk)
    def _(q):
        for c in puts(q):
            c.wait()


def after(x, *done):
    return lax.optimization_barrier((x, *done))[0]


def shards(state, weights, drive, leak, link_dev, link_blk, offsets, gram_prev):
    rows, cols, seq, units = state.shape
    nblk = rows * cols
    nlinks = link_dev.shape[-1]
    nstencil = offsets.shape[0]
    ngx = RING * RING
    cap = 4
    slots = RING * cap
    steps = drive.shape[0]
    gx = ("x", "y")
    gy = ("z", "core")
    ny = lax.axis_size(gy)
    nsrc = nstencil + nlinks
    bf16 = jnp.bfloat16
    f32 = jnp.float32
    h = seq // 2
    params = pltpu.CompilerParams(vmem_limit_bytes=VMEM_BYTES)
    kinds = 2 * RING
    pos = jnp.stack([lax.axis_index(gx), lax.axis_index(gy)]).astype(jnp.int32)
    send, near, far, count = pl.pallas_call(
        functools.partial(plan_kernel, (rows, cols, nlinks, nstencil, cap, ngx, ny)),
        out_shape=(
            jax.ShapeDtypeStruct((2, RING - 1, RING, cap), jnp.int32),
            jax.ShapeDtypeStruct((nblk * nstencil,), jnp.int32),
            jax.ShapeDtypeStruct((2, kinds, slots), jnp.int32),
            jax.ShapeDtypeStruct((2, kinds), jnp.int32),
        ),
        in_specs=[SMEM] * 4,
        out_specs=(SMEM,) * 4,
        scratch_shapes=[pltpu.SMEM((2 * RING - 1, ngx), jnp.int32)],
        name="plan",
    )(pos, link_dev, link_blk, offsets)

    state = state.reshape(nblk, seq, units)
    weights = weights.reshape(nblk, nsrc + 1, units, units)
    drive = drive.reshape(steps, nblk, seq, units)
    leak = leak.reshape(nblk, units)
    gram = gram_prev.reshape(nblk, units, units)

    def shift(x, axis, k):
        return lax.ppermute(x, axis, [(i, (i - k) % RING) for i in range(RING)])

    def ring(x, k):
        return lax.ppermute(x, gx, [(i, (i + k) % ngx) for i in range(ngx)])

    def first(a, b, full):
        grid = full.reshape(rows, cols, seq, units)
        above, below = ring(grid[rows - 1], 1), ring(grid[0], -1)
        a1 = after(a, above, below)
        y1, y3 = shift(a1, "y", 1), shift(a1, "y", 3)
        x1, x3 = shift(b, "x", 1), shift(b, "x", 3)
        m = nblk // 2
        y2l, y2u = shift(y1[:m], "y", 1), shift(y3[m:], "y", 3)
        x2l, x2u = shift(x1[:m], "x", 1), shift(x3[m:], "x", 3)
        return [a, y1, y2l, y2u, y3], [b, x1, x2l, x2u, x3], above, below

    def pack(a, b):
        return pl.pallas_call(
            functools.partial(pack_kernel, cap),
            out_shape=[jax.ShapeDtypeStruct((slots, h, units), bf16)] * (2 * (RING - 1)),
            in_specs=[SMEM] + [ANY] * (len(a) + len(b)),
            out_specs=[ANY] * (2 * (RING - 1)),
            scratch_shapes=[
                pltpu.VMEM((2, RING * nblk, h, units), bf16),
                pltpu.VMEM((2 * (RING - 1), slots, h, units), bf16),
                pltpu.SemaphoreType.DMA((len(a) + len(b),)),
                pltpu.SemaphoreType.DMA((2 * (RING - 1),)),
            ],
            compiler_params=params,
            name="pack",
        )(send, *a, *b)

    def second(packed, full, above, below):
        pa, pb = packed[: RING - 1], packed[RING - 1 :]
        x1, x3 = shift(pa[2], "x", 1), shift(pa[0], "x", 3)
        y1, y3 = shift(pb[2], "y", 1), shift(pb[0], "y", 3)
        done = (x1, x3, y1, y3)
        x2, y2 = shift(after(pa[1], *done), "x", 2), shift(after(pb[1], *done), "y", 2)
        grid = full.reshape(rows, cols, seq, units)
        tall = lambda c: jnp.concatenate([above[c : c + 1], grid[:, c], below[c : c + 1]], axis=0)
        even = lax.axis_index("core") == 0
        chip, step = jnp.where(even, tall(cols - 1), tall(0)), jnp.where(even, tall(0), tall(cols - 1))
        core = lax.ppermute(after(chip, *done), gy, [(i, i + 1 - 2 * (i % 2)) for i in range(ny)])
        side = lax.ppermute(after(step, *done), gy, [(i, (i - 1 + 2 * (i % 2)) % ny) for i in range(ny)])
        return [x1, x2, x3], [y1, y2, y3], [above, below, core, side]

    def products(t, full, rim, gram):
        nrim = tuple(r.shape[0] for r in rim)
        args = [near, full, *rim, weights, drive]
        outs = [jax.ShapeDtypeStruct((nblk, seq, units), f32)]
        scratch = [
            pltpu.VMEM((nblk + sum(nrim) + 1, seq, units), bf16),
            pltpu.VMEM((nblk, nstencil, units, units), bf16),
            pltpu.VMEM((nblk, units, units), bf16),
            pltpu.VMEM((nblk, seq, units), bf16),
            pltpu.VMEM((nblk, seq, units), f32),
        ]
        if gram is not None:
            args.append(gram)
            outs.append(jax.ShapeDtypeStruct((nblk, units, units), f32))
            scratch += [pltpu.VMEM((nblk, units, units), f32)] * 2
        scratch += [pltpu.SemaphoreType.DMA((nblk + 1 + len(nrim),)), pltpu.SemaphoreType.DMA((nblk,))]
        return pl.pallas_call(
            functools.partial(near_kernel, (nblk, nstencil, nsrc), nrim, gram is not None, t),
            out_shape=outs,
            in_specs=[SMEM] + [ANY] * (len(args) - 1),
            out_specs=[ANY] * len(outs),
            scratch_shapes=scratch,
            compiler_params=params,
            name="near",
        )(*args)

    def finish(a, b, ga, gb, full, pre, gram, last):
        args = [far, count]
        for x, g in ((a, ga), (b, gb)):
            args += [*x[:3], x[4], *g, x[3]]
        args += [full, weights, pre, leak]
        in_specs = [SMEM] * 2 + [ANY] * (len(args) - 3) + [VMEM]
        scratch = [
            pltpu.VMEM((nblk * nlinks, seq, units), bf16),
            pltpu.VMEM((nblk, seq, units), bf16),
            pltpu.VMEM((nblk, nlinks, units, units), bf16),
            pltpu.VMEM((nblk, seq, units), f32),
            pltpu.VMEM((nblk, seq, units), bf16),
        ]
        if last:
            args.append(gram)
            in_specs.append(ANY)
            outs = [jax.ShapeDtypeStruct((nblk, seq, units), bf16), jax.ShapeDtypeStruct((nblk, units, units), f32)]
            scratch += [pltpu.VMEM((nblk, units, units), f32)] * 2
        else:
            outs = [jax.ShapeDtypeStruct((nblk, n, units), bf16) for n in (h, h, seq)]
        scratch += [pltpu.SemaphoreType.DMA((nblk + 1,)), pltpu.SemaphoreType.DMA((nblk,))]
        return pl.pallas_call(
            functools.partial(far_kernel, (nblk, h, nstencil, nlinks), last),
            out_shape=outs,
            in_specs=in_specs,
            out_specs=[ANY] * len(outs),
            scratch_shapes=scratch,
            compiler_params=params,
            name="far",
        )(*args)

    own_a, own_b, full = state[:, :h], state[:, h:], state
    for t in range(steps):
        a, b, above, below = first(own_a, own_b, full)
        packed = pack(a, b)
        ga, gb, rim = second(packed, full, above, below)
        res = products(t, full, rim, gram if t else None)
        pre = res[0]
        if t:
            gram = res[1]
        res = finish(a, b, ga, gb, full, pre, gram, t == steps - 1)
        if t < steps - 1:
            own_a, own_b, full = res
    final, gram = res
    return final.reshape(rows, cols, seq, units), gram.reshape(rows, cols, units, units)


def solution(mesh):
    grid = Mesh(mesh.devices.reshape(4, 4, 4, 2), ("x", "y", "z", "core"))
    gx, gy = ("x", "y"), ("z", "core")
    return jax.shard_map(
        shards,
        mesh=grid,
        in_specs=(
            P(gx, gy, None, None),
            P(gx, gy, None, None, None),
            P(None, gx, gy, None, None),
            P(gx, gy, None),
            P(None, gy, None, None),
            P(None, gy, None, None),
            P(),
            P(gx, gy, None, None),
        ),
        out_specs=(P(gx, gy, None, None), P(gx, gy, None, None)),
        check_vma=False,
    )
```

time: 310 us -> 221 us (0.71)
  waiting for transfers between devices: 175 us -> 72.6 us
  Pallas kernels: 0 us -> 55.9 us
  starting transfers between devices: 17.3 us -> 71.7 us
  matrix products: 54.1 us -> 0 us
  between operations: 27.7 us -> 1.32 us
  local copies, waits for them, and re-layouts: 31.5 us -> 13.9 us
    all_gather x2 -> x0, waiting for transfers between devices: 165 us -> none  [shards(): whole = lax.all_gather(flat_state[None], 'gx', axis=0, tiled=True)]
    ppermute x8 -> x36, waiting for transfers between devices: 8.95 us -> 72.6 us  [the longest x28 48 us: shift(): return lax.ppermute(x, axis, [(i, (i - k) % RING) for i in range(RING)])]
    pallas_call x0 -> x7, Pallas kernels: none -> 55.9 us  [the longest x2 18.2 us: finish(): pl.pallas_call(functools.partial(far_kernel, (nblk, h, nstencil, nlinks),...]
    ppermute x8 -> x36, starting transfers between devices: 17.2 us -> 71.7 us  [the longest x28 58 us: shift(): return lax.ppermute(x, axis, [(i, (i - k) % RING) for i in range(RING)])]
    dot_general x16 -> x0, matrix products: 54.1 us -> none  [the longest x10 33.4 us: shards(): jnp.einsum('rcsu,rcuv->rcsv', nearby, weights[:, :, offset_id], preferred...]
    gather x2 -> x0, local copies, waits for them, and re-layouts: 18.7 us -> none  [shards(): whole.reshape(gx_size * nblocks, batch_cols, units)]
    slice x5 -> x14, local copies, waits for them, and re-layouts: 8.31 us -> 4.52 us  [the longest x4 1.61 us: first(): y2l, y2u = (shift(y1[:m], 'y', 1), shift(y3[m:], 'y', 3))]
    unnamed x53 -> x90, local copies, waits for them, and re-layouts: 4.47 us -> 7.45 us
  transfers between devices with their start and end apart: 10 -> 36, of which waited for: 5 -> 18; matrix products, arithmetic and copies ran while one was open for 15% -> 4% of each run, Pallas kernels for 0% -> 13%
where the time goes in v1:
time: 221 us; the launch traced here: 217 us
  waiting for transfers between devices  72.6 us (33%)
  starting transfers between devices  71.7 us (32%)
  Pallas kernels  55.9 us (25%)
  local copies, waits for them, and re-layouts  13.9 us (6%)
    ppermute x28, starting transfers between devices, shift(): return lax.ppermute(x, axis, [(i, (i - k) % RING) for i in range(RING)])  58 us
    ppermute x28, waiting for transfers between devices, shift(): return lax.ppermute(x, axis, [(i, (i - k) % RING) for i in range(RING)])  48 us
    pallas_call x2, Pallas kernels, finish(): pl.pallas_call(functools.partial(far_kernel, (nblk, h, nstencil, nlinks),...  18.2 us
    pallas_call x2, Pallas kernels, products(): pl.pallas_call(functools.partial(near_kernel, (nblk, nstencil, nsrc), nri...  16.7 us
    ppermute x2, waiting for transfers between devices, second(): lax.ppermute(after(step, *done), gy, [(i, (i - 1 + 2 * (i % 2)) % ny) for...  14.7 us
    pallas_call x1, Pallas kernels, shards(): pl.pallas_call(functools.partial(plan_kernel, (rows, cols, nlinks, nstenc...  11.3 us
    ppermute x4, waiting for transfers between devices, ring(): return lax.ppermute(x, gx, [(i, (i + k) % ngx) for i in range(ngx)])  9.89 us
    pallas_call x2, Pallas kernels, pack(): pl.pallas_call(functools.partial(pack_kernel, cap), out_shape=[jax.ShapeD...  9.64 us
  transfers between devices with their start and end apart: 36, of which 18 were waited for; matrix products, arithmetic and copies ran while one was open for 4% of the time, Pallas kernels for 13%

profile of v1, /device:TPU:12, one launch (start us, length us, event | category | flops | bytes accessed | tf_op | source)
XLA Modules:
  0.0 217.3 jit_solution(5664917623787989867)
XLA Ops:
  6.1 4.5 %collective-permute-done.1.refs_1_ = bf16[3,192,256]{2,1,0:T(8,128)(2,1)S(1)} collective-permute-done((bf16[3,192,256]{2,1,0:T(8,128)(2,1)S(1)}, bf16[3,192,256]{2,1,0:T(8,128)(2,1)S(1)}, u32[]{:S(2)}, u32[]{:S(2)}) %collective-permute-start.1) | collective-permute-done | bytes 294944 | tf_op jit(solution)/shard_map/ppermute | solution.py:291
  12.5 5.1 %collective-permute-start.2 = (bf16[12,96,256]{2,1,0:T(8,128)(2,1)S(1)}, bf16[12,96,256]{2,1,0:T(8,128)(2,1)S(1)}, u32[]{:S(2)}, u32[]{:S(2)}) collective-permute-start(bf16[12,96,256]{2,1,0:T(8,128)(2,1)S(1)} %get-tuple-element.37.refs_0_), channel_id=1, source_target_pairs={{0,24},{8,0},{16,8},{24,16},{1,25},{9,1},{17,9},{25,17},{2,26},{10... | collective-permute-start | bytes 1769480 | tf_op jit(solution)/shard_map/ppermute | solution.py:288
  22.2 5.9 %collective-permute-done.4.refs_4_.refs_3_ = bf16[12,96,256]{2,1,0:T(8,128)(2,1)S(1)} collective-permute-done((bf16[12,96,256]{2,1,0:T(8,128)(2,1)S(1)}, bf16[12,96,256]{2,1,0:T(8,128)(2,1)S(1)}, u32[]{:S(2)}, u32[]{:S(2)}) %collective-permute-start.4) | collective-permute-done | bytes 589856 | tf_op jit(solution)/shard_map/ppermute | solution.py:288
  35.6 11.3 %plan.1 = (s32[2,3,4,4]{3,2,1,0:T(4,128)}, s32[60]{0:T(128)}, s32[2,8,16]{2,1,0:T(8,128)}, s32[2,8]{1,0:T(2,128)}) custom-call(s32[2]{0:T(128)} %pad_add_fusion.pos, s32[16,1,12,3]{3,2,1,0:T(8,128)} %copy.16.dev, s32[16,1,12,3]{3,2,1,0:T(8,128)} %copy.17.blk, s32[5,2]{1,0:T(8,128)} %copy.18.offs), custom_call_target="tpu_custom_call" | custom-call | tf_op jit(solution)/shard_map/plan/pallas_call | solution.py:267
  47.0 4.8 %pack.2 = (bf16[16,96,256]{2,1,0:T(8,128)(2,1)}, bf16[16,96,256]{2,1,0:T(8,128)(2,1)}, bf16[16,96,256]{2,1,0:T(8,128)(2,1)}, bf16[16,96,256]{2,1,0:T(8,128)(2,1)...) custom-call(s32[2,3,4,4]{3,2,1,0:T(4,128)} %get-tuple-element.38.send, bf16[12,96,256]{2,1,0:T(8,128)(2,1)} %copy-done.3, ...), custom_call_target="tpu_custom_call" | custom-call | tf_op jit(solution)/shard_map/pack/pallas_call | solution.py:305
  57.3 10.3 %collective-permute-done.10.refs_4_ = bf16[16,96,256]{2,1,0:T(8,128)(2,1)S(1)} collective-permute-done((bf16[16,96,256]{2,1,0:T(8,128)(2,1)}, bf16[16,96,256]{2,1,0:T(8,128)(2,1)S(1)}, u32[]{:S(2)}, u32[]{:S(2)}) %collective-permute-start.10) | collective-permute-done | bytes 786464 | tf_op jit(solution)/shard_map/ppermute | solution.py:288
  74.0 3.4 %collective-permute-start.14 = (bf16[16,96,256]{2,1,0:T(8,128)(2,1)}, bf16[16,96,256]{2,1,0:T(8,128)(2,1)S(1)}, u32[]{:S(2)}, u32[]{:S(2)}) collective-permute-start(bf16[16,96,256]{2,1,0:T(8,128)(2,1)} %get-tuple-element.44), channel_id=1, source_target_pairs={{0,64},{32,96},{64,0},{96,32},{1,65},{33,97},{65,1},{97,33},{2,66}... | collective-permute-start | bytes 2359304 | tf_op jit(solution)/shard_map/ppermute | solution.py:288
  80.8 4.1 %collective-permute-start.17 = (bf16[6,192,256]{2,1,0:T(8,128)(2,1)}, bf16[6,192,256]{2,1,0:T(8,128)(2,1)S(1)}, u32[]{:S(2)}, u32[]{:S(2)}) collective-permute-start(bf16[6,192,256]{2,1,0:T(8,128)(2,1)} %get-tuple-element.49), channel_id=1, source_target_pairs={{0,7},{1,2},{2,1},{3,4},{4,3},{5,6},{6,5},{7,0},{8,15},{9,10},{10,... | collective-permute-start | bytes 1769480 | tf_op jit(solution)/shard_map/ppermute | solution.py:331
  85.5 7.2 %collective-permute-done.17.refs_3_ = bf16[6,192,256]{2,1,0:T(8,128)(2,1)S(1)} collective-permute-done((bf16[6,192,256]{2,1,0:T(8,128)(2,1)}, bf16[6,192,256]{2,1,0:T(8,128)(2,1)S(1)}, u32[]{:S(2)}, u32[]{:S(2)}) %collective-permute-start.17) | collective-permute-done | bytes 589856 | tf_op jit(solution)/shard_map/ppermute | solution.py:331
  93.5 7.5 %near.2.refs_18_ = f32[12,192,256]{2,1,0:T(8,128)} custom-call(s32[60]{0:T(128)} %get-tuple-element.47.near, bf16[12,192,256]{2,1,0:T(8,128)(2,1)} %bitcast.33, bf16[3,192,256]{2,1,0:T(8,128)(2,1)} %copy-done.20, bf16[3,192,256]{2,1,0:T(8,128)(2,1)} %copy-done.18, bf16[6,192,256]{2,1,0:T(8,128)(2,1)} %copy-done.33, bf16[6,192,256]{2,1,0:T(8,128)(2,1)} %copy-done.35, ...), custom_call_target="tpu_custom_call" | custom-call | tf_op jit(solution)/shard_map/near/pallas_call | solution.py:350
  101.9 7.6 %far.2 = (bf16[12,96,256]{2,1,0:T(8,128)(2,1)}, bf16[12,96,256]{2,1,0:T(8,128)(2,1)}, bf16[12,192,256]{2,1,0:T(8,128)(2,1)}) custom-call(s32[2,8,16]{2,1,0:T(8,128)} %get-tuple-element.35.far, s32[2,8]{1,0:T(2,128)} %get-tuple-element.36.count, bf16[12,96,256]{2,1,0:T(8,128)(2,1)} %copy-done.3, bf16[12,96,256]{2,1,0:T(8,128)(2,1)} %copy-done.7, ...), custom_call_target="tpu_custom_call" | custom-call | tf_op jit(solution)/shard_map/far/pallas_call | solution.py:381
  115.2 3.6 %collective-permute-done.19.refs_1_ = bf16[3,192,256]{2,1,0:T(8,128)(2,1)S(1)} collective-permute-done((bf16[3,192,256]{2,1,0:T(8,128)(2,1)S(1)}, bf16[3,192,256]{2,1,0:T(8,128)(2,1)S(1)}, u32[]{:S(2)}, u32[]{:S(2)}) %collective-permute-start.19) | collective-permute-done | bytes 294944 | tf_op jit(solution)/shard_map/ppermute | solution.py:291
  120.6 5.3 %collective-permute-start.20 = (bf16[12,96,256]{2,1,0:T(8,128)(2,1)S(1)}, bf16[12,96,256]{2,1,0:T(8,128)(2,1)S(1)}, u32[]{:S(2)}, u32[]{:S(2)}) collective-permute-start(bf16[12,96,256]{2,1,0:T(8,128)(2,1)S(1)} %copy-done.12), channel_id=1, source_target_pairs={{0,24},{8,0},{16,8},{24,16},{1,25},{9,1},{17,9},{25,17},{2,26},{10... | collective-permute-start | bytes 1769480 | tf_op jit(solution)/shard_map/ppermute | solution.py:288
  129.1 5.6 %collective-permute-done.22.refs_4_.refs_3_ = bf16[12,96,256]{2,1,0:T(8,128)(2,1)S(1)} collective-permute-done((bf16[12,96,256]{2,1,0:T(8,128)(2,1)S(1)}, bf16[12,96,256]{2,1,0:T(8,128)(2,1)S(1)}, u32[]{:S(2)}, u32[]{:S(2)}) %collective-permute-start.22) | collective-permute-done | bytes 589856 | tf_op jit(solution)/shard_map/ppermute | solution.py:288
  134.8 4.3 %collective-permute-start.21 = (bf16[6,96,256]{2,1,0:T(8,128)(2,1)S(1)}, bf16[6,96,256]{2,1,0:T(8,128)(2,1)S(1)}, u32[]{:S(2)}, u32[]{:S(2)}) collective-permute-start(bf16[6,96,256]{2,1,0:T(8,128)(2,1)S(1)} %slice.128), channel_id=1, source_target_pairs={{0,24},{8,0},{16,8},{24,16},{1,25},{9,1},{17,9},{25,17},{2,26},{10... | collective-permute-start | bytes 884744 | tf_op jit(solution)/shard_map/ppermute | solution.py:288
  139.2 4.5 %collective-permute-done.23.refs_3_.refs_7_ = bf16[6,96,256]{2,1,0:T(8,128)(2,1)S(1)} collective-permute-done((bf16[6,96,256]{2,1,0:T(8,128)(2,1)S(1)}, bf16[6,96,256]{2,1,0:T(8,128)(2,1)S(1)}, u32[]{:S(2)}, u32[]{:S(2)}) %collective-permute-start.23) | collective-permute-done | bytes 294944 | tf_op jit(solution)/shard_map/ppermute | solution.py:288
  145.1 4.8 %pack.3 = (bf16[16,96,256]{2,1,0:T(8,128)(2,1)}, bf16[16,96,256]{2,1,0:T(8,128)(2,1)}, bf16[16,96,256]{2,1,0:T(8,128)(2,1)}, bf16[16,96,256]{2,1,0:T(8,128)(2,1)...) custom-call(s32[2,3,4,4]{3,2,1,0:T(4,128)} %get-tuple-element.38.send, ...), custom_call_target="tpu_custom_call" | custom-call | tf_op jit(solution)/shard_map/pack/pallas_call | solution.py:305
  155.4 9.7 %collective-permute-done.28.refs_4_ = bf16[16,96,256]{2,1,0:T(8,128)(2,1)S(1)} collective-permute-done((bf16[16,96,256]{2,1,0:T(8,128)(2,1)}, bf16[16,96,256]{2,1,0:T(8,128)(2,1)S(1)}, u32[]{:S(2)}, u32[]{:S(2)}) %collective-permute-start.28) | collective-permute-done | bytes 786464 | tf_op jit(solution)/shard_map/ppermute | solution.py:288
  168.8 9.7 %collective-permute-start.32 = (bf16[16,96,256]{2,1,0:T(8,128)(2,1)S(1)}, bf16[16,96,256]{2,1,0:T(8,128)(2,1)S(1)}, u32[]{:S(2)}, u32[]{:S(2)}) collective-permute-start(bf16[16,96,256]{2,1,0:T(8,128)(2,1)S(1)} %copy-done.42), channel_id=1, source_target_pairs={{0,64},{32,96},{64,0},{96,32},{1,65},{33,97},{65,1},{97,33},{2,66}... | collective-permute-start | bytes 2359304 | tf_op jit(solution)/shard_map/ppermute | solution.py:288
  178.4 4.1 %collective-permute-start.33 = (bf16[16,96,256]{2,1,0:T(8,128)(2,1)S(1)}, bf16[16,96,256]{2,1,0:T(8,128)(2,1)S(1)}, u32[]{:S(2)}, u32[]{:S(2)}) collective-permute-start(bf16[16,96,256]{2,1,0:T(8,128)(2,1)S(1)} %copy-done.41), channel_id=1, source_target_pairs={{0,16},{8,24},{16,0},{24,8},{1,17},{9,25},{17,1},{25,9},{2,18},{10... | collective-permute-start | bytes 2359304 | tf_op jit(solution)/shard_map/ppermute | solution.py:288
  182.8 4.9 %collective-permute-start.35 = (bf16[6,192,256]{2,1,0:T(8,128)(2,1)S(1)}, bf16[6,192,256]{2,1,0:T(8,128)(2,1)S(1)}, u32[]{:S(2)}, u32[]{:S(2)}) collective-permute-start(bf16[6,192,256]{2,1,0:T(8,128)(2,1)S(1)} %get-tuple-element.63), channel_id=1, source_target_pairs={{0,7},{1,2},{2,1},{3,4},{4,3},{5,6},{6,5},{7,0},{8,15},{9,10},{10,... | collective-permute-start | bytes 1769480 | tf_op jit(solution)/shard_map/ppermute | solution.py:331
  187.7 7.6 %collective-permute-done.35.refs_3_ = bf16[6,192,256]{2,1,0:T(8,128)(2,1)S(1)} collective-permute-done((bf16[6,192,256]{2,1,0:T(8,128)(2,1)S(1)}, bf16[6,192,256]{2,1,0:T(8,128)(2,1)S(1)}, u32[]{:S(2)}, u32[]{:S(2)}) %collective-permute-start.35) | collective-permute-done | bytes 589856 | tf_op jit(solution)/shard_map/ppermute | solution.py:331
  196.1 9.2 %near.3 = (f32[12,192,256]{2,1,0:T(8,128)}, f32[12,256,256]{2,1,0:T(8,128)}) custom-call(s32[60]{0:T(128)} %get-tuple-element.47.near, bf16[12,192,256]{2,1,0:T(8,128)(2,1)} %get-tuple-element.51.own_ref.refs_16_, bf16[3,192,256]{2,1,0:T(8,128)(2,1)} %copy-done.23, bf16[3,192,256]{2,1,0:T(8,128)(2,1)} %copy-done.22, bf16[6,192,256]{2,1,0:T(8,128)(2,1)} %copy-done.34, ...), custom_call_target="tpu_custom_call" | custom-call | tf_op jit(solution)/shard_map/near/pallas_call | solution.py:350
  206.5 10.7 %far.3 = (bf16[12,192,256]{2,1,0:T(8,128)(2,1)}, f32[12,256,256]{2,1,0:T(8,128)}) custom-call(s32[2,8,16]{2,1,0:T(8,128)} %get-tuple-element.35.far, s32[2,8]{1,0:T(2,128)} %get-tuple-element.36.count, bf16[12,96,256]{2,1,0:T(8,128)(2,1)} %get-tuple-element.52.refs_0_, bf16[12,96,256]{2,1,0:T(8,128)(2,1)} %copy-done.11, bf16[6,96,256]{2,1,0:T(8,128)(2,1)} %copy-done.17, ...), custom_call_target="tpu_custom_call" | custom-call | tf_op jit(solution)/shard_map/far/pallas_call | solution.py:381
  (166 shorter events, 60.3 us)
Async XLA Ops:
  4.0 14.6 %collective-permute-start.8 = (bf16[12,96,256]{2,1,0:T(8,128)(2,1)S(1)}, bf16[12,96,256]{2,1,0:T(8,128)(2,1)S(1)}, u32[]{:S(2)}, u32[]{:S(2)}) collective-permute-start(bf16[12,96,256]{2,1,0:T(8,128)(2,1)S(1)} %get-tuple-element.78.refs_5_.refs_8_), channel_id=1, source_target_pairs={{0,32},{32,64},{64,96},{96,0},{1,33},{33,65},{65,97},{97,1},{2,34}... | collective-permute-start | bytes 1769480 | tf_op jit(solution)/shard_map/ppermute | solution.py:288
  5.3 15.3 %collective-permute-start.6 = (bf16[12,96,256]{2,1,0:T(8,128)(2,1)S(1)}, bf16[12,96,256]{2,1,0:T(8,128)(2,1)S(1)}, u32[]{:S(2)}, u32[]{:S(2)}) collective-permute-start(bf16[12,96,256]{2,1,0:T(8,128)(2,1)S(1)} %get-tuple-element.78.refs_5_.refs_8_), channel_id=1, source_target_pairs={{0,96},{32,0},{64,32},{96,64},{1,97},{33,1},{65,33},{97,65},{2,98}... | collective-permute-start | bytes 1769480 | tf_op jit(solution)/shard_map/ppermute | solution.py:288
  12.1 16.1 %collective-permute-start.4 = (bf16[12,96,256]{2,1,0:T(8,128)(2,1)S(1)}, bf16[12,96,256]{2,1,0:T(8,128)(2,1)S(1)}, u32[]{:S(2)}, u32[]{:S(2)}) collective-permute-start(bf16[12,96,256]{2,1,0:T(8,128)(2,1)S(1)} %get-tuple-element.37.refs_0_), channel_id=1, source_target_pairs={{0,8},{8,16},{16,24},{24,0},{1,9},{9,17},{17,25},{25,1},{2,10},{10... | collective-permute-start | bytes 1769480 | tf_op jit(solution)/shard_map/ppermute | solution.py:288
  12.5 16.4 %collective-permute-start.2 = (bf16[12,96,256]{2,1,0:T(8,128)(2,1)S(1)}, bf16[12,96,256]{2,1,0:T(8,128)(2,1)S(1)}, u32[]{:S(2)}, u32[]{:S(2)}) collective-permute-start(bf16[12,96,256]{2,1,0:T(8,128)(2,1)S(1)} %get-tuple-element.37.refs_0_), channel_id=1, source_target_pairs={{0,24},{8,0},{16,8},{24,16},{1,25},{9,1},{17,9},{25,17},{2,26},{10... | collective-permute-start | bytes 1769480 | tf_op jit(solution)/shard_map/ppermute | solution.py:288
  19.4 27.6 %collective-permute-start.9 = (bf16[6,96,256]{2,1,0:T(8,128)(2,1)}, bf16[6,96,256]{2,1,0:T(8,128)(2,1)}, u32[]{:S(2)}, u32[]{:S(2)}) collective-permute-start(bf16[6,96,256]{2,1,0:T(8,128)(2,1)} %slice.123), channel_id=1, source_target_pairs={{0,32},{32,64},{64,96},{96,0},{1,33},{33,65},{65,97},{97,1},{2,34}... | collective-permute-start | bytes 884744 | tf_op jit(solution)/shard_map/ppermute | solution.py:288
  21.4 25.6 %collective-permute-start.7 = (bf16[6,96,256]{2,1,0:T(8,128)(2,1)}, bf16[6,96,256]{2,1,0:T(8,128)(2,1)}, u32[]{:S(2)}, u32[]{:S(2)}) collective-permute-start(bf16[6,96,256]{2,1,0:T(8,128)(2,1)} %slice.122), channel_id=1, source_target_pairs={{0,96},{32,0},{64,32},{96,64},{1,97},{33,1},{65,33},{97,65},{2,98}... | collective-permute-start | bytes 884744 | tf_op jit(solution)/shard_map/ppermute | solution.py:288
  28.9 18.1 %collective-permute-start.5 = (bf16[6,96,256]{2,1,0:T(8,128)(2,1)}, bf16[6,96,256]{2,1,0:T(8,128)(2,1)}, u32[]{:S(2)}, u32[]{:S(2)}) collective-permute-start(bf16[6,96,256]{2,1,0:T(8,128)(2,1)} %slice.120), channel_id=1, source_target_pairs={{0,8},{8,16},{16,24},{24,0},{1,9},{9,17},{17,25},{25,1},{2,10},{10... | collective-permute-start | bytes 884744 | tf_op jit(solution)/shard_map/ppermute | solution.py:288
  29.7 17.3 %collective-permute-start.3 = (bf16[6,96,256]{2,1,0:T(8,128)(2,1)}, bf16[6,96,256]{2,1,0:T(8,128)(2,1)}, u32[]{:S(2)}, u32[]{:S(2)}) collective-permute-start(bf16[6,96,256]{2,1,0:T(8,128)(2,1)} %slice.119), channel_id=1, source_target_pairs={{0,24},{8,0},{16,8},{24,16},{1,25},{9,1},{17,9},{25,17},{2,26},{10... | collective-permute-start | bytes 884744 | tf_op jit(solution)/shard_map/ppermute | solution.py:288
  51.9 15.7 %collective-permute-start.10 = (bf16[16,96,256]{2,1,0:T(8,128)(2,1)}, bf16[16,96,256]{2,1,0:T(8,128)(2,1)S(1)}, u32[]{:S(2)}, u32[]{:S(2)}) collective-permute-start(bf16[16,96,256]{2,1,0:T(8,128)(2,1)} %get-tuple-element.39), channel_id=1, source_target_pairs={{0,96},{32,0},{64,32},{96,64},{1,97},{33,1},{65,33},{97,65},{2,98}... | collective-permute-start | bytes 2359304 | tf_op jit(solution)/shard_map/ppermute | solution.py:288
  52.5 17.7 %collective-permute-start.11 = (bf16[16,96,256]{2,1,0:T(8,128)(2,1)}, bf16[16,96,256]{2,1,0:T(8,128)(2,1)S(1)}, u32[]{:S(2)}, u32[]{:S(2)}) collective-permute-start(bf16[16,96,256]{2,1,0:T(8,128)(2,1)} %get-tuple-element.41), channel_id=1, source_target_pairs={{0,32},{32,64},{64,96},{96,0},{1,33},{33,65},{65,97},{97,1},{2,34}... | collective-permute-start | bytes 2359304 | tf_op jit(solution)/shard_map/ppermute | solution.py:288
  54.0 18.0 %collective-permute-start.12 = (bf16[16,96,256]{2,1,0:T(8,128)(2,1)}, bf16[16,96,256]{2,1,0:T(8,128)(2,1)}, u32[]{:S(2)}, u32[]{:S(2)}) collective-permute-start(bf16[16,96,256]{2,1,0:T(8,128)(2,1)} %get-tuple-element.42), channel_id=1, source_target_pairs={{0,24},{8,0},{16,8},{24,16},{1,25},{9,1},{17,9},{25,17},{2,26},{10... | collective-permute-start | bytes 2359304 | tf_op jit(solution)/shard_map/ppermute | solution.py:288
  57.2 16.8 %collective-permute-start.13 = (bf16[16,96,256]{2,1,0:T(8,128)(2,1)}, bf16[16,96,256]{2,1,0:T(8,128)(2,1)}, u32[]{:S(2)}, u32[]{:S(2)}) collective-permute-start(bf16[16,96,256]{2,1,0:T(8,128)(2,1)} %get-tuple-element.43), channel_id=1, source_target_pairs={{0,8},{8,16},{16,24},{24,0},{1,9},{9,17},{17,25},{25,1},{2,10},{10... | collective-permute-start | bytes 2359304 | tf_op jit(solution)/shard_map/ppermute | solution.py:288
  74.0 27.0 %collective-permute-start.14 = (bf16[16,96,256]{2,1,0:T(8,128)(2,1)}, bf16[16,96,256]{2,1,0:T(8,128)(2,1)S(1)}, u32[]{:S(2)}, u32[]{:S(2)}) collective-permute-start(bf16[16,96,256]{2,1,0:T(8,128)(2,1)} %get-tuple-element.44), channel_id=1, source_target_pairs={{0,64},{32,96},{64,0},{96,32},{1,65},{33,97},{65,1},{97,33},{2,66}... | collective-permute-start | bytes 2359304 | tf_op jit(solution)/shard_map/ppermute | solution.py:288
  77.5 23.6 %collective-permute-start.15 = (bf16[16,96,256]{2,1,0:T(8,128)(2,1)}, bf16[16,96,256]{2,1,0:T(8,128)(2,1)}, u32[]{:S(2)}, u32[]{:S(2)}) collective-permute-start(bf16[16,96,256]{2,1,0:T(8,128)(2,1)} %get-tuple-element.46), channel_id=1, source_target_pairs={{0,16},{8,24},{16,0},{24,8},{1,17},{9,25},{17,1},{25,9},{2,18},{10... | collective-permute-start | bytes 2359304 | tf_op jit(solution)/shard_map/ppermute | solution.py:288
  113.2 13.5 %collective-permute-start.26 = (bf16[12,96,256]{2,1,0:T(8,128)(2,1)S(1)}, bf16[12,96,256]{2,1,0:T(8,128)(2,1)S(1)}, u32[]{:S(2)}, u32[]{:S(2)}) collective-permute-start(bf16[12,96,256]{2,1,0:T(8,128)(2,1)S(1)} %copy-done.13), channel_id=1, source_target_pairs={{0,32},{32,64},{64,96},{96,0},{1,33},{33,65},{65,97},{97,1},{2,34}... | collective-permute-start | bytes 1769480 | tf_op jit(solution)/shard_map/ppermute | solution.py:288
  114.1 13.7 %collective-permute-start.24 = (bf16[12,96,256]{2,1,0:T(8,128)(2,1)S(1)}, bf16[12,96,256]{2,1,0:T(8,128)(2,1)S(1)}, u32[]{:S(2)}, u32[]{:S(2)}) collective-permute-start(bf16[12,96,256]{2,1,0:T(8,128)(2,1)S(1)} %copy-done.13), channel_id=1, source_target_pairs={{0,96},{32,0},{64,32},{96,64},{1,97},{33,1},{65,33},{97,65},{2,98}... | collective-permute-start | bytes 1769480 | tf_op jit(solution)/shard_map/ppermute | solution.py:288
  119.2 15.4 %collective-permute-start.22 = (bf16[12,96,256]{2,1,0:T(8,128)(2,1)S(1)}, bf16[12,96,256]{2,1,0:T(8,128)(2,1)S(1)}, u32[]{:S(2)}, u32[]{:S(2)}) collective-permute-start(bf16[12,96,256]{2,1,0:T(8,128)(2,1)S(1)} %copy-done.12), channel_id=1, source_target_pairs={{0,8},{8,16},{16,24},{24,0},{1,9},{9,17},{17,25},{25,1},{2,10},{10... | collective-permute-start | bytes 1769480 | tf_op jit(solution)/shard_map/ppermute | solution.py:288
  120.6 14.1 %collective-permute-start.20 = (bf16[12,96,256]{2,1,0:T(8,128)(2,1)S(1)}, bf16[12,96,256]{2,1,0:T(8,128)(2,1)S(1)}, u32[]{:S(2)}, u32[]{:S(2)}) collective-permute-start(bf16[12,96,256]{2,1,0:T(8,128)(2,1)S(1)} %copy-done.12), channel_id=1, source_target_pairs={{0,24},{8,0},{16,8},{24,16},{1,25},{9,1},{17,9},{25,17},{2,26},{10... | collective-permute-start | bytes 1769480 | tf_op jit(solution)/shard_map/ppermute | solution.py:288
  150.0 15.1 %collective-permute-start.28 = (bf16[16,96,256]{2,1,0:T(8,128)(2,1)}, bf16[16,96,256]{2,1,0:T(8,128)(2,1)S(1)}, u32[]{:S(2)}, u32[]{:S(2)}) collective-permute-start(bf16[16,96,256]{2,1,0:T(8,128)(2,1)} %get-tuple-element.54), channel_id=1, source_target_pairs={{0,96},{32,0},{64,32},{96,64},{1,97},{33,1},{65,33},{97,65},{2,98}... | collective-permute-start | bytes 2359304 | tf_op jit(solution)/shard_map/ppermute | solution.py:288
  150.4 17.5 %collective-permute-start.29 = (bf16[16,96,256]{2,1,0:T(8,128)(2,1)}, bf16[16,96,256]{2,1,0:T(8,128)(2,1)S(1)}, u32[]{:S(2)}, u32[]{:S(2)}) collective-permute-start(bf16[16,96,256]{2,1,0:T(8,128)(2,1)} %get-tuple-element.56), channel_id=1, source_target_pairs={{0,32},{32,64},{64,96},{96,0},{1,33},{33,65},{65,97},{97,1},{2,34}... | collective-permute-start | bytes 2359304 | tf_op jit(solution)/shard_map/ppermute | solution.py:288
  152.1 15.8 %collective-permute-start.30 = (bf16[16,96,256]{2,1,0:T(8,128)(2,1)}, bf16[16,96,256]{2,1,0:T(8,128)(2,1)S(1)}, u32[]{:S(2)}, u32[]{:S(2)}) collective-permute-start(bf16[16,96,256]{2,1,0:T(8,128)(2,1)} %get-tuple-element.57), channel_id=1, source_target_pairs={{0,24},{8,0},{16,8},{24,16},{1,25},{9,1},{17,9},{25,17},{2,26},{10... | collective-permute-start | bytes 2359304 | tf_op jit(solution)/shard_map/ppermute | solution.py:288
  155.3 13.5 %collective-permute-start.31 = (bf16[16,96,256]{2,1,0:T(8,128)(2,1)}, bf16[16,96,256]{2,1,0:T(8,128)(2,1)S(1)}, u32[]{:S(2)}, u32[]{:S(2)}) collective-permute-start(bf16[16,96,256]{2,1,0:T(8,128)(2,1)} %get-tuple-element.58), channel_id=1, source_target_pairs={{0,8},{8,16},{16,24},{24,0},{1,9},{9,17},{17,25},{25,1},{2,10},{10... | collective-permute-start | bytes 2359304 | tf_op jit(solution)/shard_map/ppermute | solution.py:288
  168.8 36.5 %collective-permute-start.32 = (bf16[16,96,256]{2,1,0:T(8,128)(2,1)S(1)}, bf16[16,96,256]{2,1,0:T(8,128)(2,1)S(1)}, u32[]{:S(2)}, u32[]{:S(2)}) collective-permute-start(bf16[16,96,256]{2,1,0:T(8,128)(2,1)S(1)} %copy-done.42), channel_id=1, source_target_pairs={{0,64},{32,96},{64,0},{96,32},{1,65},{33,97},{65,1},{97,33},{2,66}... | collective-permute-start | bytes 2359304 | tf_op jit(solution)/shard_map/ppermute | solution.py:288
  178.4 26.9 %collective-permute-start.33 = (bf16[16,96,256]{2,1,0:T(8,128)(2,1)S(1)}, bf16[16,96,256]{2,1,0:T(8,128)(2,1)S(1)}, u32[]{:S(2)}, u32[]{:S(2)}) collective-permute-start(bf16[16,96,256]{2,1,0:T(8,128)(2,1)S(1)} %copy-done.41), channel_id=1, source_target_pairs={{0,16},{8,24},{16,0},{24,8},{1,17},{9,25},{17,1},{25,9},{2,18},{10... | collective-permute-start | bytes 2359304 | tf_op jit(solution)/shard_map/ppermute | solution.py:288
  (55 other events, 725.4 us)

commit v2 on v1

--- a/solution.py
+++ b/solution.py
@@ -12,16 +12,17 @@
 SMEM = pl.BlockSpec(memory_space=pltpu.SMEM)
 VMEM = pl.BlockSpec(memory_space=pltpu.VMEM)
 RING = 4
-
-
-def plan_kernel(dims, pos, dev, blk, offs, send, near, far, count, seen):
+BITS, MASK = 2, RING - 1
+
+
+def plan_kernel(dims, pos, dev, blk, offs, send, near, far, count, beside, nbeside, seen):
     rows, cols, nlinks, nstencil, cap, ngx, ngy = dims
     nblk = rows * cols
     me, band = pos[0], pos[1]
-    mine = (me // RING, me % RING)
+    mine = (me >> BITS, me & MASK)
     dests = [me]
-    dests += [((mine[0] + way) % RING) * RING + mine[1] for way in range(1, RING)]
-    dests += [mine[0] * RING + (mine[1] + way) % RING for way in range(1, RING)]
+    dests += [((mine[0] + way) & MASK) * RING + mine[1] for way in range(1, RING)]
+    dests += [mine[0] * RING + ((mine[1] + way) & MASK) for way in range(1, RING)]
 
     @pl.loop(0, ngx)
     def _(i):
@@ -41,7 +42,7 @@
         for l in range(nlinks):
             for n, dest in enumerate(dests):
                 d = dev[dest, 0, q, l]
-                at = (d // RING, d % RING)
+                at = (d >> BITS, d & MASK)
                 i = seen[n, d]
                 seen[n, d] = i + 1
                 i = jnp.minimum(i, cap - 1)
@@ -50,13 +51,13 @@
 
                     @pl.when(at[half] == mine[half])
                     def _(half=half, way=way, at=at, i=i, dest=dest):
-                        rel = (at[1 - half] - mine[1 - half] + RING) % RING
+                        rel = (at[1 - half] - mine[1 - half]) & MASK
                         send[half, way, rel, i] = blk[dest, 0, q, l]
 
                     continue
                 for half in range(2):
-                    way = (at[half] - mine[half] + RING) % RING
-                    rel = (at[1 - half] - mine[1 - half] + RING) % RING
+                    way = (at[half] - mine[half]) & MASK
+                    rel = (at[1 - half] - mine[1 - half]) & MASK
                     own = blk[me, 0, q, l]
                     upper = (rel == RING // 2) & (own >= nblk // 2)
                     kind = jnp.where(way == 0, jnp.where(upper, 2 * RING - 1, rel), RING + way - 1)
@@ -65,10 +66,9 @@
                     far[half, kind, jnp.minimum(k, RING * cap - 1)] = place * 64 + q * nlinks + l
                     count[half, kind] = k + 1
 
-    side = nblk + 2 * cols
-    swap = band % 2
-    left, right = side + (1 - swap) * (rows + 2), side + swap * (rows + 2)
-    void = side + 2 * (rows + 2)
+    swap = band & 1
+    void = nblk + 2 * cols
+    nbeside[0] = 0
 
     @pl.loop(0, rows)
     def _(r0):
@@ -76,10 +76,19 @@
             for k in range(nstencil):
                 r, t = r0 + offs[k, 0], c0 + offs[k, 1]
                 code = jnp.where(r < 0, nblk + t, jnp.where(r >= rows, nblk + cols + t, r * cols + t))
-                code = jnp.where(t < 0, left + r + 1, jnp.where(t >= cols, right + r + 1, code))
                 out = (r < 0) & (me == 0) | (r >= rows) & (me == ngx - 1)
-                out = out | (t < 0) & (band == 0) | (t >= cols) & (band == ngy - 1)
-                near[(r0 * cols + c0) * nstencil + k] = jnp.where(out, void, code)
+                left, right = t < 0, t >= cols
+                term = (r0 * cols + c0) * nstencil + k
+                near[term] = jnp.where(out | left | right, void, code)
+                if c0 in (0, cols - 1):
+                    out = out | left & (band == 0) | right & (band == ngy - 1)
+
+                    @pl.when((left | right) & jnp.logical_not(out))
+                    def _(left=left, r=r, c0=c0, k=k):
+                        n = nbeside[0]
+                        which = jnp.where(left, 1 - swap, swap)
+                        beside[n] = (((r0 * cols + c0) * 8 + k) * 64) + which * (rows + 2) + r + 1
+                        nbeside[0] = n + 1
 
 
 def pack_kernel(cap, send, *refs):
@@ -171,18 +180,34 @@
             c.wait()
 
 
-def far_kernel(dims, last, far, count, *refs):
+def far_kernel(dims, last, far, count, beside, nbeside, *refs):
     nblk, h, nstencil, nlinks = dims
     nin = 4 * RING
     bufs, refs = refs[:nin], list(refs[nin:])
-    own_ref, w_ref, pre_ref, leak_ref = refs[:4]
-    refs = refs[4:]
+    core_ref, side_ref, own_ref, w_ref, pre_ref, leak_ref = refs[:6]
+    refs = refs[6:]
     gram_ref = refs.pop(0) if last else None
     nout = 2 if last else 3
     outs, refs = refs[:nout], refs[nout:]
-    got, old, wl, pre, new, *refs = refs
+    got, cols, wb, old, wl, pre, new, *refs = refs
     gin, gout = (refs.pop(0), refs.pop(0)) if last else (None, None)
-    sem, osem = refs
+    sem, osem, bsem = refs
+    tall = core_ref.shape[0]
+    whole = [
+        pltpu.make_async_copy(pre_ref, pre, sem.at[nblk + 1]),
+        pltpu.make_async_copy(core_ref, cols.at[pl.ds(0, tall)], sem.at[nblk + 2]),
+        pltpu.make_async_copy(side_ref, cols.at[pl.ds(tall, tall)], sem.at[nblk + 3]),
+    ]
+    for c in whole:
+        c.start()
+
+    def weight(n):
+        e = beside[n]
+        return pltpu.make_async_copy(w_ref.at[e >> 9, (e >> 6) & 7], wb.at[n], bsem.at[n])
+
+    @pl.loop(0, nbeside[0])
+    def _(n):
+        weight(n).start()
 
     for half in range(2):
         for kind in range(2 * RING):
@@ -191,13 +216,12 @@
             @pl.loop(0, count[half, kind])
             def _(n, half=half, kind=kind, src=src):
                 e = far[half, kind, n]
-                to = got.at[e % 64, pl.ds(half * h, h)]
-                pltpu.make_async_copy(src.at[e // 64], to, sem.at[nblk]).start()
+                to = got.at[e & 63, pl.ds(half * h, h)]
+                pltpu.make_async_copy(src.at[e >> 6], to, sem.at[nblk]).start()
 
     def ins(q):
         yield pltpu.make_async_copy(own_ref.at[q], old.at[q], sem.at[q])
         yield pltpu.make_async_copy(w_ref.at[q, pl.ds(nstencil, nlinks)], wl.at[q], sem.at[q])
-        yield pltpu.make_async_copy(pre_ref.at[q], pre.at[q], sem.at[q])
         if last:
             yield pltpu.make_async_copy(gram_ref.at[q], gin.at[q], sem.at[q])
 
@@ -214,6 +238,15 @@
     def _(q):
         for c in ins(q):
             c.start()
+
+    for c in whole:
+        c.wait()
+
+    @pl.loop(0, nbeside[0])
+    def _(n):
+        weight(n).wait()
+        e = beside[n]
+        pre[e >> 9] += jnp.dot(cols[e & 63], wb[n], preferred_element_type=jnp.float32)
 
     pltpu.make_async_copy(got, got, sem.at[nblk]).wait()
 
@@ -264,16 +297,18 @@
     params = pltpu.CompilerParams(vmem_limit_bytes=VMEM_BYTES)
     kinds = 2 * RING
     pos = jnp.stack([lax.axis_index(gx), lax.axis_index(gy)]).astype(jnp.int32)
-    send, near, far, count = pl.pallas_call(
+    send, near, far, count, beside, nbeside = pl.pallas_call(
         functools.partial(plan_kernel, (rows, cols, nlinks, nstencil, cap, ngx, ny)),
         out_shape=(
             jax.ShapeDtypeStruct((2, RING - 1, RING, cap), jnp.int32),
             jax.ShapeDtypeStruct((nblk * nstencil,), jnp.int32),
             jax.ShapeDtypeStruct((2, kinds, slots), jnp.int32),
             jax.ShapeDtypeStruct((2, kinds), jnp.int32),
+            jax.ShapeDtypeStruct((rows * nstencil,), jnp.int32),
+            jax.ShapeDtypeStruct((1,), jnp.int32),
         ),
         in_specs=[SMEM] * 4,
-        out_specs=(SMEM,) * 4,
+        out_specs=(SMEM,) * 6,
         scratch_shapes=[pltpu.SMEM((2 * RING - 1, ngx), jnp.int32)],
         name="plan",
     )(pos, link_dev, link_blk, offsets)
@@ -292,14 +327,15 @@
 
     def first(a, b, full):
         grid = full.reshape(rows, cols, seq, units)
-        above, below = ring(grid[rows - 1], 1), ring(grid[0], -1)
-        a1 = after(a, above, below)
-        y1, y3 = shift(a1, "y", 1), shift(a1, "y", 3)
+        y1, y3 = shift(a, "y", 1), shift(a, "y", 3)
         x1, x3 = shift(b, "x", 1), shift(b, "x", 3)
         m = nblk // 2
-        y2l, y2u = shift(y1[:m], "y", 1), shift(y3[m:], "y", 3)
-        x2l, x2u = shift(x1[:m], "x", 1), shift(x3[m:], "x", 3)
-        return [a, y1, y2l, y2u, y3], [b, x1, x2l, x2u, x3], above, below
+        done = (y1, y3, x1, x3, count)
+        y2l, y2u = shift(after(y1[:m], *done), "y", 1), shift(after(y3[m:], *done), "y", 3)
+        x2l, x2u = shift(after(x1[:m], *done), "x", 1), shift(after(x3[m:], *done), "x", 3)
+        above, below = ring(after(grid[rows - 1], *done), 1), ring(after(grid[0], *done), -1)
+        a = [after(a, above, below), y1, y2l, y2u, y3]
+        return a, [b, x1, x2l, x2u, x3], above, below
 
     def pack(a, b):
         return pl.pallas_call(
@@ -329,7 +365,7 @@
         chip, step = jnp.where(even, tall(cols - 1), tall(0)), jnp.where(even, tall(0), tall(cols - 1))
         core = lax.ppermute(after(chip, *done), gy, [(i, i + 1 - 2 * (i % 2)) for i in range(ny)])
         side = lax.ppermute(after(step, *done), gy, [(i, (i - 1 + 2 * (i % 2)) % ny) for i in range(ny)])
-        return [x1, x2, x3], [y1, y2, y3], [above, below, core, side]
+        return [x1, x2, x3], [y1, y2, y3], core, side
 
     def products(t, full, rim, gram):
         nrim = tuple(r.shape[0] for r in rim)
@@ -357,14 +393,16 @@
             name="near",
         )(*args)
 
-    def finish(a, b, ga, gb, full, pre, gram, last):
-        args = [far, count]
+    def finish(a, b, ga, gb, core, side, full, pre, gram, last):
+        args = [far, count, beside, nbeside]
         for x, g in ((a, ga), (b, gb)):
             args += [*x[:3], x[4], *g, x[3]]
-        args += [full, weights, pre, leak]
-        in_specs = [SMEM] * 2 + [ANY] * (len(args) - 3) + [VMEM]
+        args += [core, side, full, weights, pre, leak]
+        in_specs = [SMEM] * 4 + [ANY] * (len(args) - 5) + [VMEM]
         scratch = [
             pltpu.VMEM((nblk * nlinks, seq, units), bf16),
+            pltpu.VMEM((2 * (rows + 2), seq, units), bf16),
+            pltpu.VMEM((rows * nstencil, units, units), bf16),
             pltpu.VMEM((nblk, seq, units), bf16),
             pltpu.VMEM((nblk, nlinks, units, units), bf16),
             pltpu.VMEM((nblk, seq, units), f32),
@@ -377,7 +415,7 @@
             scratch += [pltpu.VMEM((nblk, units, units), f32)] * 2
         else:
             outs = [jax.ShapeDtypeStruct((nblk, n, units), bf16) for n in (h, h, seq)]
-        scratch += [pltpu.SemaphoreType.DMA((nblk + 1,)), pltpu.SemaphoreType.DMA((nblk,))]
+        scratch += [pltpu.SemaphoreType.DMA((n,)) for n in (nblk + 4, nblk, rows * nstencil)]
         return pl.pallas_call(
             functools.partial(far_kernel, (nblk, h, nstencil, nlinks), last),
             out_shape=outs,
@@ -392,12 +430,12 @@
     for t in range(steps):
         a, b, above, below = first(own_a, own_b, full)
         packed = pack(a, b)
-        ga, gb, rim = second(packed, full, above, below)
-        res = products(t, full, rim, gram if t else None)
+        ga, gb, core, side = second(packed, full, above, below)
+        res = products(t, after(full, packed[0]), [above, below], gram if t else None)
         pre = res[0]
         if t:
             gram = res[1]
-        res = finish(a, b, ga, gb, full, pre, gram, t == steps - 1)
+        res = finish(a, b, ga, gb, core, side, full, pre, gram, t == steps - 1)
         if t < steps - 1:
             own_a, own_b, full = res
     final, gram = res

time: 221 us -> 198 us (0.90)
  starting transfers between devices: 71.7 us -> 59.3 us
  waiting for transfers between devices: 72.6 us -> 63.6 us
    ppermute x2, waiting for transfers between devices: 14.7 us -> 0.01 us  [second(): lax.ppermute(after(step, *done), gy, [(i, (i - 1 + 2 * (i % 2)) % ny) for...]
    ppermute x28, starting transfers between devices: 58 us -> 45.4 us  [shift(): return lax.ppermute(x, axis, [(i, (i - k) % RING) for i in range(RING)])]
    ppermute x28, waiting for transfers between devices: 48 us -> 57.3 us  [shift(): return lax.ppermute(x, axis, [(i, (i - k) % RING) for i in range(RING)])]
    ppermute x4, waiting for transfers between devices: 9.89 us -> 6.26 us  [ring(): return lax.ppermute(x, gx, [(i, (i + k) % ngx) for i in range(ngx)])]
    pallas_call x2, Pallas kernels: 18.2 us -> 21.5 us  [finish(): pl.pallas_call(functools.partial(far_kernel, (nblk, h, nstencil, nlinks),...]
    unnamed x90 -> x82, local copies, waits for them, and re-layouts: 7.45 us -> 7.85 us
  transfers between devices with their start and end apart: 36 -> 36, of which waited for: 18 -> 19; matrix products, arithmetic and copies ran while one was open for 4% -> 5% of each run, Pallas kernels for 13% -> 13%
where the time goes in v2:
time: 198 us; the launch traced here: 196 us
  waiting for transfers between devices  63.6 us (32%)
  starting transfers between devices  59.3 us (30%)
  Pallas kernels  56.8 us (29%)
  local copies, waits for them, and re-layouts  13.3 us (7%)
    ppermute x28, waiting for transfers between devices, shift(): return lax.ppermute(x, axis, [(i, (i - k) % RING) for i in range(RING)])  57.3 us
    ppermute x28, starting transfers between devices, shift(): return lax.ppermute(x, axis, [(i, (i - k) % RING) for i in range(RING)])  45.4 us
    pallas_call x2, Pallas kernels, finish(): pl.pallas_call(functools.partial(far_kernel, (nblk, h, nstencil, nlinks),...  21.5 us
    pallas_call x2, Pallas kernels, products(): pl.pallas_call(functools.partial(near_kernel, (nblk, nstencil, nsrc), nri...  16 us
    pallas_call x2, Pallas kernels, pack(): pl.pallas_call(functools.partial(pack_kernel, cap), out_shape=[jax.ShapeD...  9.64 us
    pallas_call x1, Pallas kernels, shards(): pl.pallas_call(functools.partial(plan_kernel, (rows, cols, nlinks, nstenc...  9.63 us
    ppermute x2, starting transfers between devices, second(): lax.ppermute(after(step, *done), gy, [(i, (i - 1 + 2 * (i % 2)) % ny) for...  8.13 us
    unnamed x82, local copies, waits for them, and re-layouts  7.85 us
  transfers between devices with their start and end apart: 36, of which 19 were waited for; matrix products, arithmetic and copies ran while one was open for 5% of the time, Pallas kernels for 13%

profile of v2, /device:TPU:12, one launch (start us, length us, event | category | flops | bytes accessed | tf_op | source)
XLA Modules:
  0.0 196.0 jit_solution(15025472185779167896)
XLA Ops:
  10.5 9.6 %plan.1 = (s32[2,3,4,4]{3,2,1,0:T(4,128)}, s32[60]{0:T(128)}, s32[2,8,16]{2,1,0:T(8,128)}, s32[2,8]{1,0:T(2,128)}, s32[20]{0:T(128)}, /*index=5*/s32[1]{0:T(128)}) custom-call(s32[2]{0:T(128)} %pad_add_fusion.pos, s32[16,1,12,3]{3,2,1,0:T(8,128)} %copy.16.dev, s32[16,1,12,3]{3,2,1,0:T(8,128)} %copy.17.blk, s32[5,2]{1,0:T(8,128)} %copy.18.offs), custom_call_target="tpu_custom_call" | custom-call | tf_op jit(solution)/shard_map/plan/pallas_call | solution.py:300
  25.0 3.8 %collective-permute-start.6 = (bf16[6,96,256]{2,1,0:T(8,128)(2,1)S(1)}, bf16[6,96,256]{2,1,0:T(8,128)(2,1)S(1)}, u32[]{:S(2)}, u32[]{:S(2)}) collective-permute-start(bf16[6,96,256]{2,1,0:T(8,128)(2,1)S(1)} %slice.120), channel_id=1, source_target_pairs={{0,24},{8,0},{16,8},{24,16},{1,25},{9,1},{17,9},{25,17},{2,26},{10... | collective-permute-start | bytes 884744 | tf_op jit(solution)/shard_map/ppermute | solution.py:323
  30.4 4.2 %collective-permute-done.5.refs_1_ = bf16[3,192,256]{2,1,0:T(8,128)(2,1)S(1)} collective-permute-done((bf16[3,192,256]{2,1,0:T(8,128)(2,1)S(1)}, bf16[3,192,256]{2,1,0:T(8,128)(2,1)S(1)}, u32[]{:S(2)}, u32[]{:S(2)}) %collective-permute-start.5) | collective-permute-done | bytes 294944 | tf_op jit(solution)/shard_map/ppermute | solution.py:326
  34.5 3.4 %collective-permute-done.6.refs_2_ = bf16[6,96,256]{2,1,0:T(8,128)(2,1)S(1)} collective-permute-done((bf16[6,96,256]{2,1,0:T(8,128)(2,1)S(1)}, bf16[6,96,256]{2,1,0:T(8,128)(2,1)S(1)}, u32[]{:S(2)}, u32[]{:S(2)}) %collective-permute-start.6) | collective-permute-done | bytes 294944 | tf_op jit(solution)/shard_map/ppermute | solution.py:323
  38.9 4.8 %pack.2 = (bf16[16,96,256]{2,1,0:T(8,128)(2,1)}, bf16[16,96,256]{2,1,0:T(8,128)(2,1)}, bf16[16,96,256]{2,1,0:T(8,128)(2,1)}, bf16[16,96,256]{2,1,0:T(8,128)(2,1)...) custom-call(s32[2,3,4,4]{3,2,1,0:T(4,128)} %get-tuple-element.59.send, bf16[12,96,256]{2,1,0:T(8,128)(2,1)} %copy-done.3, ...), custom_call_target="tpu_custom_call" | custom-call | tf_op jit(solution)/shard_map/pack/pallas_call | solution.py:341
  48.3 12.4 %collective-permute-done.10.refs_4_ = bf16[16,96,256]{2,1,0:T(8,128)(2,1)S(1)} collective-permute-done((bf16[16,96,256]{2,1,0:T(8,128)(2,1)}, bf16[16,96,256]{2,1,0:T(8,128)(2,1)S(1)}, u32[]{:S(2)}, u32[]{:S(2)}) %collective-permute-start.10) | collective-permute-done | bytes 786464 | tf_op jit(solution)/shard_map/ppermute | solution.py:323
  60.7 3.3 %collective-permute-done.12.refs_12_ = bf16[16,96,256]{2,1,0:T(8,128)(2,1)S(1)} collective-permute-done((bf16[16,96,256]{2,1,0:T(8,128)(2,1)}, bf16[16,96,256]{2,1,0:T(8,128)(2,1)S(1)}, u32[]{:S(2)}, u32[]{:S(2)}) %collective-permute-start.12) | collective-permute-done | bytes 786464 | tf_op jit(solution)/shard_map/ppermute | solution.py:323
  64.0 4.1 %collective-permute-done.13.refs_14_ = bf16[16,96,256]{2,1,0:T(8,128)(2,1)} collective-permute-done((bf16[16,96,256]{2,1,0:T(8,128)(2,1)}, bf16[16,96,256]{2,1,0:T(8,128)(2,1)}, u32[]{:S(2)}, u32[]{:S(2)}) %collective-permute-start.13) | collective-permute-done | bytes 786464 | tf_op jit(solution)/shard_map/ppermute | solution.py:323
  68.4 4.7 %collective-permute-start.15 = (bf16[16,96,256]{2,1,0:T(8,128)(2,1)}, bf16[16,96,256]{2,1,0:T(8,128)(2,1)}, u32[]{:S(2)}, u32[]{:S(2)}) collective-permute-start(bf16[16,96,256]{2,1,0:T(8,128)(2,1)} %get-tuple-element.70), channel_id=1, source_target_pairs={{0,16},{8,24},{16,0},{24,8},{1,17},{9,25},{17,1},{25,9},{2,18},{10... | collective-permute-start | bytes 2359304 | tf_op jit(solution)/shard_map/ppermute | solution.py:323
  74.2 4.1 %collective-permute-start.17 = (bf16[6,192,256]{2,1,0:T(8,128)(2,1)S(1)}, bf16[6,192,256]{2,1,0:T(8,128)(2,1)S(1)}, u32[]{:S(2)}, u32[]{:S(2)}) collective-permute-start(bf16[6,192,256]{2,1,0:T(8,128)(2,1)S(1)} %get-tuple-element.72), channel_id=1, source_target_pairs={{0,7},{1,2},{2,1},{3,4},{4,3},{5,6},{6,5},{7,0},{8,15},{9,10},{10,... | collective-permute-start | bytes 1769480 | tf_op jit(solution)/shard_map/ppermute | solution.py:367
  78.9 7.2 %near.2.refs_20_ = f32[12,192,256]{2,1,0:T(8,128)} custom-call(s32[60]{0:T(128)} %get-tuple-element.73.near, bf16[12,192,256]{2,1,0:T(8,128)(2,1)} %bitcast.34, bf16[3,192,256]{2,1,0:T(8,128)(2,1)} %copy-done.18, bf16[3,192,256]{2,1,0:T(8,128)(2,1)} %copy-done.21, bf16[12,9,256,256]{3,2,1,0:T(8,128)(2,1)} %bitcast.29, bf16[2,12,192,256]{3,2,1,0:T(8,128)(2,1)} %bitcast.37), custom_call_target="tpu_custom_call" | custom-call | tf_op jit(solution)/shard_map/near/pallas_call | solution.py:386
  87.7 9.2 %far.2 = (bf16[12,96,256]{2,1,0:T(8,128)(2,1)}, bf16[12,96,256]{2,1,0:T(8,128)(2,1)}, bf16[12,192,256]{2,1,0:T(8,128)(2,1)}) custom-call(s32[2,8,16]{2,1,0:T(8,128)} %get-tuple-element.51.far, s32[2,8]{1,0:T(2,128)} %get-tuple-element.52.count, s32[20]{0:T(128)} %get-tuple-element.53.beside, s32[1]{0:T(128)} %get-tuple-element.54.nbeside, ...), custom_call_target="tpu_custom_call" | custom-call | tf_op jit(solution)/shard_map/far/pallas_call | solution.py:419
  102.9 8.2 %collective-permute-done.19.refs_4_.refs_3_ = bf16[12,96,256]{2,1,0:T(8,128)(2,1)S(1)} collective-permute-done((bf16[12,96,256]{2,1,0:T(8,128)(2,1)}, bf16[12,96,256]{2,1,0:T(8,128)(2,1)S(1)}, u32[]{:S(2)}, u32[]{:S(2)}) %collective-permute-start.19) | collective-permute-done | bytes 589856 | tf_op jit(solution)/shard_map/ppermute | solution.py:323
  115.3 3.2 %collective-permute-start.23 = (bf16[3,192,256]{2,1,0:T(8,128)(2,1)S(1)}, bf16[3,192,256]{2,1,0:T(8,128)(2,1)S(1)}, u32[]{:S(2)}, u32[]{:S(2)}) collective-permute-start(bf16[3,192,256]{2,1,0:T(8,128)(2,1)S(1)} %get-tuple-element.79), channel_id=1, source_target_pairs={{0,120},{8,0},{16,8},{24,16},{32,24},{40,32},{48,40},{56,48},{64,5... | collective-permute-start | bytes 884744 | tf_op jit(solution)/shard_map/ppermute | solution.py:326
  118.5 3.5 %collective-permute-start.24 = (bf16[6,96,256]{2,1,0:T(8,128)(2,1)S(1)}, bf16[6,96,256]{2,1,0:T(8,128)(2,1)S(1)}, u32[]{:S(2)}, u32[]{:S(2)}) collective-permute-start(bf16[6,96,256]{2,1,0:T(8,128)(2,1)S(1)} %slice.128), channel_id=1, source_target_pairs={{0,24},{8,0},{16,8},{24,16},{1,25},{9,1},{17,9},{25,17},{2,26},{10... | collective-permute-start | bytes 884744 | tf_op jit(solution)/shard_map/ppermute | solution.py:323
  131.8 4.8 %pack.3 = (bf16[16,96,256]{2,1,0:T(8,128)(2,1)}, bf16[16,96,256]{2,1,0:T(8,128)(2,1)}, bf16[16,96,256]{2,1,0:T(8,128)(2,1)}, bf16[16,96,256]{2,1,0:T(8,128)(2,1)...) custom-call(s32[2,3,4,4]{3,2,1,0:T(4,128)} %get-tuple-element.59.send, ...), custom_call_target="tpu_custom_call" | custom-call | tf_op jit(solution)/shard_map/pack/pallas_call | solution.py:341
  137.5 4.2 %collective-permute-start.30 = (bf16[16,96,256]{2,1,0:T(8,128)(2,1)}, bf16[16,96,256]{2,1,0:T(8,128)(2,1)S(1)}, u32[]{:S(2)}, u32[]{:S(2)}) collective-permute-start(bf16[16,96,256]{2,1,0:T(8,128)(2,1)} %get-tuple-element.88), channel_id=1, source_target_pairs={{0,24},{8,0},{16,8},{24,16},{1,25},{9,1},{17,9},{25,17},{2,26},{10... | collective-permute-start | bytes 2359304 | tf_op jit(solution)/shard_map/ppermute | solution.py:323
  142.4 8.7 %collective-permute-done.28.refs_4_ = bf16[16,96,256]{2,1,0:T(8,128)(2,1)S(1)} collective-permute-done((bf16[16,96,256]{2,1,0:T(8,128)(2,1)}, bf16[16,96,256]{2,1,0:T(8,128)(2,1)S(1)}, u32[]{:S(2)}, u32[]{:S(2)}) %collective-permute-start.28) | collective-permute-done | bytes 786464 | tf_op jit(solution)/shard_map/ppermute | solution.py:323
  152.3 3.3 %collective-permute-done.31.refs_14_ = bf16[16,96,256]{2,1,0:T(8,128)(2,1)S(1)} collective-permute-done((bf16[16,96,256]{2,1,0:T(8,128)(2,1)}, bf16[16,96,256]{2,1,0:T(8,128)(2,1)S(1)}, u32[]{:S(2)}, u32[]{:S(2)}) %collective-permute-start.31) | collective-permute-done | bytes 786464 | tf_op jit(solution)/shard_map/ppermute | solution.py:323
  155.6 4.1 %collective-permute-done.29.refs_6_ = bf16[16,96,256]{2,1,0:T(8,128)(2,1)S(1)} collective-permute-done((bf16[16,96,256]{2,1,0:T(8,128)(2,1)}, bf16[16,96,256]{2,1,0:T(8,128)(2,1)S(1)}, u32[]{:S(2)}, u32[]{:S(2)}) %collective-permute-start.29) | collective-permute-done | bytes 786464 | tf_op jit(solution)/shard_map/ppermute | solution.py:323
  159.7 6.7 %collective-permute-start.32 = (bf16[16,96,256]{2,1,0:T(8,128)(2,1)}, bf16[16,96,256]{2,1,0:T(8,128)(2,1)S(1)}, u32[]{:S(2)}, u32[]{:S(2)}) collective-permute-start(bf16[16,96,256]{2,1,0:T(8,128)(2,1)} %get-tuple-element.90), channel_id=1, source_target_pairs={{0,64},{32,96},{64,0},{96,32},{1,65},{33,97},{65,1},{97,33},{2,66}... | collective-permute-start | bytes 2359304 | tf_op jit(solution)/shard_map/ppermute | solution.py:323
  169.1 4.0 %collective-permute-start.35 = (bf16[6,192,256]{2,1,0:T(8,128)(2,1)S(1)}, bf16[6,192,256]{2,1,0:T(8,128)(2,1)S(1)}, u32[]{:S(2)}, u32[]{:S(2)}) collective-permute-start(bf16[6,192,256]{2,1,0:T(8,128)(2,1)S(1)} %get-tuple-element.94), channel_id=1, source_target_pairs={{0,7},{1,2},{2,1},{3,4},{4,3},{5,6},{6,5},{7,0},{8,15},{9,10},{10,... | collective-permute-start | bytes 1769480 | tf_op jit(solution)/shard_map/ppermute | solution.py:367
  173.1 8.8 %near.3 = (f32[12,192,256]{2,1,0:T(8,128)}, f32[12,256,256]{2,1,0:T(8,128)}) custom-call(s32[60]{0:T(128)} %get-tuple-element.73.near, bf16[12,192,256]{2,1,0:T(8,128)(2,1)} %get-tuple-element.95.own_ref.refs_18_, bf16[3,192,256]{2,1,0:T(8,128)(2,1)} %copy-done.20, bf16[3,192,256]{2,1,0:T(8,128)(2,1)} %copy-done.22, bf16[12,9,256,256]{3,2,1,0:T(8,128)(2,1)} %bitcast.31, ...), custom_call_target="tpu_custom_call" | custom-call | tf_op jit(solution)/shard_map/near/pallas_call | solution.py:386
  183.5 12.3 %far.3 = (bf16[12,192,256]{2,1,0:T(8,128)(2,1)}, f32[12,256,256]{2,1,0:T(8,128)}) custom-call(s32[2,8,16]{2,1,0:T(8,128)} %get-tuple-element.51.far, s32[2,8]{1,0:T(2,128)} %get-tuple-element.52.count, s32[20]{0:T(128)} %get-tuple-element.53.beside, s32[1]{0:T(128)} %get-tuple-element.54.nbeside, bf16[12,96,256]{2,1,0:T(8,128)(2,1)} %get-tuple-element.80.refs_0_, ...), custom_call_target="tpu_custom_call" | custom-call | tf_op jit(solution)/shard_map/far/pallas_call | solution.py:419
  (158 shorter events, 51.8 us)
Async XLA Ops:
  2.1 18.1 %collective-permute-start.1 = (bf16[12,96,256]{2,1,0:T(8,128)(2,1)S(1)}, bf16[12,96,256]{2,1,0:T(8,128)(2,1)S(1)}, u32[]{:S(2)}, u32[]{:S(2)}) collective-permute-start(bf16[12,96,256]{2,1,0:T(8,128)(2,1)S(1)} %get-tuple-element.57.refs_0_), channel_id=1, source_target_pairs={{0,8},{8,16},{16,24},{24,0},{1,9},{9,17},{17,25},{25,1},{2,10},{10... | collective-permute-start | bytes 1769480 | tf_op jit(solution)/shard_map/ppermute | solution.py:323
  3.7 16.5 %collective-permute-start = (bf16[12,96,256]{2,1,0:T(8,128)(2,1)S(1)}, bf16[12,96,256]{2,1,0:T(8,128)(2,1)S(1)}, u32[]{:S(2)}, u32[]{:S(2)}) collective-permute-start(bf16[12,96,256]{2,1,0:T(8,128)(2,1)S(1)} %get-tuple-element.57.refs_0_), channel_id=1, source_target_pairs={{0,24},{8,0},{16,8},{24,16},{1,25},{9,1},{17,9},{25,17},{2,26},{10... | collective-permute-start | bytes 1769480 | tf_op jit(solution)/shard_map/ppermute | solution.py:323
  4.2 16.0 %collective-permute-start.3 = (bf16[12,96,256]{2,1,0:T(8,128)(2,1)S(1)}, bf16[12,96,256]{2,1,0:T(8,128)(2,1)}, u32[]{:S(2)}, u32[]{:S(2)}) collective-permute-start(bf16[12,96,256]{2,1,0:T(8,128)(2,1)S(1)} %get-tuple-element.112.refs_5_.refs_8_), channel_id=1, source_target_pairs={{0,32},{32,64},{64,96},{96,0},{1,33},{33,65},{65,97},{97,1},{2,34}... | collective-permute-start | bytes 1769480 | tf_op jit(solution)/shard_map/ppermute | solution.py:323
  5.4 14.9 %collective-permute-start.2 = (bf16[12,96,256]{2,1,0:T(8,128)(2,1)S(1)}, bf16[12,96,256]{2,1,0:T(8,128)(2,1)}, u32[]{:S(2)}, u32[]{:S(2)}) collective-permute-start(bf16[12,96,256]{2,1,0:T(8,128)(2,1)S(1)} %get-tuple-element.112.refs_5_.refs_8_), channel_id=1, source_target_pairs={{0,96},{32,0},{64,32},{96,64},{1,97},{33,1},{65,33},{97,65},{2,98}... | collective-permute-start | bytes 1769480 | tf_op jit(solution)/shard_map/ppermute | solution.py:323
  25.0 12.9 %collective-permute-start.6 = (bf16[6,96,256]{2,1,0:T(8,128)(2,1)S(1)}, bf16[6,96,256]{2,1,0:T(8,128)(2,1)S(1)}, u32[]{:S(2)}, u32[]{:S(2)}) collective-permute-start(bf16[6,96,256]{2,1,0:T(8,128)(2,1)S(1)} %slice.120), channel_id=1, source_target_pairs={{0,24},{8,0},{16,8},{24,16},{1,25},{9,1},{17,9},{25,17},{2,26},{10... | collective-permute-start | bytes 884744 | tf_op jit(solution)/shard_map/ppermute | solution.py:323
  43.7 17.0 %collective-permute-start.10 = (bf16[16,96,256]{2,1,0:T(8,128)(2,1)}, bf16[16,96,256]{2,1,0:T(8,128)(2,1)S(1)}, u32[]{:S(2)}, u32[]{:S(2)}) collective-permute-start(bf16[16,96,256]{2,1,0:T(8,128)(2,1)} %get-tuple-element.63), channel_id=1, source_target_pairs={{0,96},{32,0},{64,32},{96,64},{1,97},{33,1},{65,33},{97,65},{2,98}... | collective-permute-start | bytes 2359304 | tf_op jit(solution)/shard_map/ppermute | solution.py:323
  45.6 18.4 %collective-permute-start.12 = (bf16[16,96,256]{2,1,0:T(8,128)(2,1)}, bf16[16,96,256]{2,1,0:T(8,128)(2,1)S(1)}, u32[]{:S(2)}, u32[]{:S(2)}) collective-permute-start(bf16[16,96,256]{2,1,0:T(8,128)(2,1)} %get-tuple-element.66), channel_id=1, source_target_pairs={{0,24},{8,0},{16,8},{24,16},{1,25},{9,1},{17,9},{25,17},{2,26},{10... | collective-permute-start | bytes 2359304 | tf_op jit(solution)/shard_map/ppermute | solution.py:323
  48.2 19.9 %collective-permute-start.13 = (bf16[16,96,256]{2,1,0:T(8,128)(2,1)}, bf16[16,96,256]{2,1,0:T(8,128)(2,1)}, u32[]{:S(2)}, u32[]{:S(2)}) collective-permute-start(bf16[16,96,256]{2,1,0:T(8,128)(2,1)} %get-tuple-element.67), channel_id=1, source_target_pairs={{0,8},{8,16},{16,24},{24,0},{1,9},{9,17},{17,25},{25,1},{2,10},{10... | collective-permute-start | bytes 2359304 | tf_op jit(solution)/shard_map/ppermute | solution.py:323
  48.2 19.9 %collective-permute-start.11 = (bf16[16,96,256]{2,1,0:T(8,128)(2,1)}, bf16[16,96,256]{2,1,0:T(8,128)(2,1)}, u32[]{:S(2)}, u32[]{:S(2)}) collective-permute-start(bf16[16,96,256]{2,1,0:T(8,128)(2,1)} %get-tuple-element.65), channel_id=1, source_target_pairs={{0,32},{32,64},{64,96},{96,0},{1,33},{33,65},{65,97},{97,1},{2,34}... | collective-permute-start | bytes 2359304 | tf_op jit(solution)/shard_map/ppermute | solution.py:323
  68.1 18.7 %collective-permute-start.14 = (bf16[16,96,256]{2,1,0:T(8,128)(2,1)}, bf16[16,96,256]{2,1,0:T(8,128)(2,1)S(1)}, u32[]{:S(2)}, u32[]{:S(2)}) collective-permute-start(bf16[16,96,256]{2,1,0:T(8,128)(2,1)} %get-tuple-element.68), channel_id=1, source_target_pairs={{0,64},{32,96},{64,0},{96,32},{1,65},{33,97},{65,1},{97,33},{2,66}... | collective-permute-start | bytes 2359304 | tf_op jit(solution)/shard_map/ppermute | solution.py:323
  68.4 18.7 %collective-permute-start.15 = (bf16[16,96,256]{2,1,0:T(8,128)(2,1)}, bf16[16,96,256]{2,1,0:T(8,128)(2,1)}, u32[]{:S(2)}, u32[]{:S(2)}) collective-permute-start(bf16[16,96,256]{2,1,0:T(8,128)(2,1)} %get-tuple-element.70), channel_id=1, source_target_pairs={{0,16},{8,24},{16,0},{24,8},{1,17},{9,25},{17,1},{25,9},{2,18},{10... | collective-permute-start | bytes 2359304 | tf_op jit(solution)/shard_map/ppermute | solution.py:323
  74.2 11.9 %collective-permute-start.17 = (bf16[6,192,256]{2,1,0:T(8,128)(2,1)S(1)}, bf16[6,192,256]{2,1,0:T(8,128)(2,1)S(1)}, u32[]{:S(2)}, u32[]{:S(2)}) collective-permute-start(bf16[6,192,256]{2,1,0:T(8,128)(2,1)S(1)} %get-tuple-element.72), channel_id=1, source_target_pairs={{0,7},{1,2},{2,1},{3,4},{4,3},{5,6},{6,5},{7,0},{8,15},{9,10},{10,... | collective-permute-start | bytes 1769480 | tf_op jit(solution)/shard_map/ppermute | solution.py:367
  97.0 14.1 %collective-permute-start.19 = (bf16[12,96,256]{2,1,0:T(8,128)(2,1)}, bf16[12,96,256]{2,1,0:T(8,128)(2,1)S(1)}, u32[]{:S(2)}, u32[]{:S(2)}) collective-permute-start(bf16[12,96,256]{2,1,0:T(8,128)(2,1)} %get-tuple-element.80.refs_0_), channel_id=1, source_target_pairs={{0,8},{8,16},{16,24},{24,0},{1,9},{9,17},{17,25},{25,1},{2,10},{10... | collective-permute-start | bytes 1769480 | tf_op jit(solution)/shard_map/ppermute | solution.py:323
  97.9 13.3 %collective-permute-start.18 = (bf16[12,96,256]{2,1,0:T(8,128)(2,1)}, bf16[12,96,256]{2,1,0:T(8,128)(2,1)S(1)}, u32[]{:S(2)}, u32[]{:S(2)}) collective-permute-start(bf16[12,96,256]{2,1,0:T(8,128)(2,1)} %get-tuple-element.80.refs_0_), channel_id=1, source_target_pairs={{0,24},{8,0},{16,8},{24,16},{1,25},{9,1},{17,9},{25,17},{2,26},{10... | collective-permute-start | bytes 1769480 | tf_op jit(solution)/shard_map/ppermute | solution.py:323
  99.8 12.7 %collective-permute-start.21 = (bf16[12,96,256]{2,1,0:T(8,128)(2,1)}, bf16[12,96,256]{2,1,0:T(8,128)(2,1)S(1)}, u32[]{:S(2)}, u32[]{:S(2)}) collective-permute-start(bf16[12,96,256]{2,1,0:T(8,128)(2,1)} %get-tuple-element.77.refs_5_.refs_8_), channel_id=1, source_target_pairs={{0,32},{32,64},{64,96},{96,0},{1,33},{33,65},{65,97},{97,1},{2,34}... | collective-permute-start | bytes 1769480 | tf_op jit(solution)/shard_map/ppermute | solution.py:323
  100.8 13.6 %collective-permute-start.20 = (bf16[12,96,256]{2,1,0:T(8,128)(2,1)}, bf16[12,96,256]{2,1,0:T(8,128)(2,1)S(1)}, u32[]{:S(2)}, u32[]{:S(2)}) collective-permute-start(bf16[12,96,256]{2,1,0:T(8,128)(2,1)} %get-tuple-element.77.refs_5_.refs_8_), channel_id=1, source_target_pairs={{0,96},{32,0},{64,32},{96,64},{1,97},{33,1},{65,33},{97,65},{2,98}... | collective-permute-start | bytes 1769480 | tf_op jit(solution)/shard_map/ppermute | solution.py:323
  136.6 14.5 %collective-permute-start.28 = (bf16[16,96,256]{2,1,0:T(8,128)(2,1)}, bf16[16,96,256]{2,1,0:T(8,128)(2,1)S(1)}, u32[]{:S(2)}, u32[]{:S(2)}) collective-permute-start(bf16[16,96,256]{2,1,0:T(8,128)(2,1)} %get-tuple-element.85), channel_id=1, source_target_pairs={{0,96},{32,0},{64,32},{96,64},{1,97},{33,1},{65,33},{97,65},{2,98}... | collective-permute-start | bytes 2359304 | tf_op jit(solution)/shard_map/ppermute | solution.py:323
  137.5 14.7 %collective-permute-start.30 = (bf16[16,96,256]{2,1,0:T(8,128)(2,1)}, bf16[16,96,256]{2,1,0:T(8,128)(2,1)S(1)}, u32[]{:S(2)}, u32[]{:S(2)}) collective-permute-start(bf16[16,96,256]{2,1,0:T(8,128)(2,1)} %get-tuple-element.88), channel_id=1, source_target_pairs={{0,24},{8,0},{16,8},{24,16},{1,25},{9,1},{17,9},{25,17},{2,26},{10... | collective-permute-start | bytes 2359304 | tf_op jit(solution)/shard_map/ppermute | solution.py:323
  141.8 13.8 %collective-permute-start.31 = (bf16[16,96,256]{2,1,0:T(8,128)(2,1)}, bf16[16,96,256]{2,1,0:T(8,128)(2,1)S(1)}, u32[]{:S(2)}, u32[]{:S(2)}) collective-permute-start(bf16[16,96,256]{2,1,0:T(8,128)(2,1)} %get-tuple-element.89), channel_id=1, source_target_pairs={{0,8},{8,16},{16,24},{24,0},{1,9},{9,17},{17,25},{25,1},{2,10},{10... | collective-permute-start | bytes 2359304 | tf_op jit(solution)/shard_map/ppermute | solution.py:323
  141.8 17.9 %collective-permute-start.29 = (bf16[16,96,256]{2,1,0:T(8,128)(2,1)}, bf16[16,96,256]{2,1,0:T(8,128)(2,1)S(1)}, u32[]{:S(2)}, u32[]{:S(2)}) collective-permute-start(bf16[16,96,256]{2,1,0:T(8,128)(2,1)} %get-tuple-element.87), channel_id=1, source_target_pairs={{0,32},{32,64},{64,96},{96,0},{1,33},{33,65},{65,97},{97,1},{2,34}... | collective-permute-start | bytes 2359304 | tf_op jit(solution)/shard_map/ppermute | solution.py:323
  159.7 22.3 %collective-permute-start.32 = (bf16[16,96,256]{2,1,0:T(8,128)(2,1)}, bf16[16,96,256]{2,1,0:T(8,128)(2,1)S(1)}, u32[]{:S(2)}, u32[]{:S(2)}) collective-permute-start(bf16[16,96,256]{2,1,0:T(8,128)(2,1)} %get-tuple-element.90), channel_id=1, source_target_pairs={{0,64},{32,96},{64,0},{96,32},{1,65},{33,97},{65,1},{97,33},{2,66}... | collective-permute-start | bytes 2359304 | tf_op jit(solution)/shard_map/ppermute | solution.py:323
  166.4 15.6 %collective-permute-start.33 = (bf16[16,96,256]{2,1,0:T(8,128)(2,1)S(1)}, bf16[16,96,256]{2,1,0:T(8,128)(2,1)S(1)}, u32[]{:S(2)}, u32[]{:S(2)}) collective-permute-start(bf16[16,96,256]{2,1,0:T(8,128)(2,1)S(1)} %copy-done.38), channel_id=1, source_target_pairs={{0,16},{8,24},{16,0},{24,8},{1,17},{9,25},{17,1},{25,9},{2,18},{10... | collective-permute-start | bytes 2359304 | tf_op jit(solution)/shard_map/ppermute | solution.py:323
  169.0 13.0 %collective-permute-start.34 = (bf16[6,192,256]{2,1,0:T(8,128)(2,1)S(1)}, bf16[6,192,256]{2,1,0:T(8,128)(2,1)S(1)}, u32[]{:S(2)}, u32[]{:S(2)}) collective-permute-start(bf16[6,192,256]{2,1,0:T(8,128)(2,1)S(1)} %get-tuple-element.93), channel_id=1, source_target_pairs={{0,1},{1,0},{2,3},{3,2},{4,5},{5,4},{6,7},{7,6},{8,9},{9,8},{10,11... | collective-permute-start | bytes 1769480 | tf_op jit(solution)/shard_map/ppermute | solution.py:366
  169.1 12.9 %collective-permute-start.35 = (bf16[6,192,256]{2,1,0:T(8,128)(2,1)S(1)}, bf16[6,192,256]{2,1,0:T(8,128)(2,1)S(1)}, u32[]{:S(2)}, u32[]{:S(2)}) collective-permute-start(bf16[6,192,256]{2,1,0:T(8,128)(2,1)S(1)} %get-tuple-element.94), channel_id=1, source_target_pairs={{0,7},{1,2},{2,1},{3,4},{4,3},{5,6},{6,5},{7,0},{8,15},{9,10},{10,... | collective-permute-start | bytes 1769480 | tf_op jit(solution)/shard_map/ppermute | solution.py:367
  (51 other events, 518.8 us)

commit v3 on v2

--- a/solution.py
+++ b/solution.py
@@ -250,23 +250,29 @@
 
     pltpu.make_async_copy(got, got, sem.at[nblk]).wait()
 
-    @pl.loop(0, nblk)
-    def _(q):
-        for c in ins(q):
-            c.wait()
-        lhs = jnp.concatenate([got[q * nlinks + l] for l in range(nlinks)], axis=1)
-        units = lhs.shape[-1] // nlinks
-        w = wl[q].reshape(nlinks * units, units)
-        total = pre[q] + jnp.dot(lhs, w, preferred_element_type=jnp.float32)
-        rate = leak_ref[pl.ds(q, 1), :]
-        fresh = ((1.0 - rate) * old[q].astype(jnp.float32) + rate * jnp.tanh(total)).astype(jnp.bfloat16)
-        new[q] = fresh
-        if last:
-            gout[q] = gin[q] + lax.dot_general(
-                fresh, fresh, (((0,), (0,)), ((), ())), preferred_element_type=jnp.float32
-            )
-        for c in puts(q):
-            c.start()
+    group = 3
+    units = wl.shape[-1]
+
+    @pl.loop(0, nblk // group)
+    def _(i):
+        qs = [i * group + j for j in range(group)]
+        for q in qs:
+            for c in ins(q):
+                c.wait()
+        fresh = []
+        for q in qs:
+            lhs = jnp.concatenate([got[q * nlinks + l] for l in range(nlinks)], axis=1)
+            w = wl[q].reshape(nlinks * units, units)
+            total = pre[q] + jnp.dot(lhs, w, preferred_element_type=jnp.float32)
+            rate = leak_ref[pl.ds(q, 1), :]
+            fresh.append(((1.0 - rate) * old[q].astype(jnp.float32) + rate * jnp.tanh(total)).astype(jnp.bfloat16))
+        for q, x in zip(qs, fresh):
+            new[q] = x
+            if last:
+                gout[q] = gin[q] + lax.dot_general(x, x, (((0,), (0,)), ((), ())), preferred_element_type=jnp.float32)
+        for q in qs:
+            for c in puts(q):
+                c.start()
 
     @pl.loop(0, nblk)
     def _(q):
@@ -353,19 +359,19 @@
             name="pack",
         )(send, *a, *b)
 
-    def second(packed, full, above, below):
+    def second(packed, full, above, below, work):
         pa, pb = packed[: RING - 1], packed[RING - 1 :]
         x1, x3 = shift(pa[2], "x", 1), shift(pa[0], "x", 3)
         y1, y3 = shift(pb[2], "y", 1), shift(pb[0], "y", 3)
-        done = (x1, x3, y1, y3)
-        x2, y2 = shift(after(pa[1], *done), "x", 2), shift(after(pb[1], *done), "y", 2)
+        res = work()
+        x2, y2 = shift(after(pa[1], x1, x3, res[0]), "x", 2), shift(after(pb[1], y1, y3, res[0]), "y", 2)
         grid = full.reshape(rows, cols, seq, units)
         tall = lambda c: jnp.concatenate([above[c : c + 1], grid[:, c], below[c : c + 1]], axis=0)
         even = lax.axis_index("core") == 0
         chip, step = jnp.where(even, tall(cols - 1), tall(0)), jnp.where(even, tall(0), tall(cols - 1))
-        core = lax.ppermute(after(chip, *done), gy, [(i, i + 1 - 2 * (i % 2)) for i in range(ny)])
-        side = lax.ppermute(after(step, *done), gy, [(i, (i - 1 + 2 * (i % 2)) % ny) for i in range(ny)])
-        return [x1, x2, x3], [y1, y2, y3], core, side
+        core = lax.ppermute(after(chip, res[0]), gy, [(i, i + 1 - 2 * (i % 2)) for i in range(ny)])
+        side = lax.ppermute(after(step, res[0]), gy, [(i, (i - 1 + 2 * (i % 2)) % ny) for i in range(ny)])
+        return [x1, x2, x3], [y1, y2, y3], core, side, res
 
     def products(t, full, rim, gram):
         nrim = tuple(r.shape[0] for r in rim)
@@ -430,8 +436,8 @@
     for t in range(steps):
         a, b, above, below = first(own_a, own_b, full)
         packed = pack(a, b)
-        ga, gb, core, side = second(packed, full, above, below)
-        res = products(t, after(full, packed[0]), [above, below], gram if t else None)
+        work = lambda: products(t, after(full, packed[0]), [above, below], gram if t else None)
+        ga, gb, core, side, res = second(packed, full, above, below, work)
         pre = res[0]
         if t:
             gram = res[1]

time: 198 us -> 197 us (level)
  waiting for transfers between devices: 63.6 us -> 57.5 us
  starting transfers between devices: 59.3 us -> 64.2 us
  local copies, waits for them, and re-layouts: 13.3 us -> 17.1 us
  Pallas kernels: 56.8 us -> 53.9 us
    ppermute x28, waiting for transfers between devices: 57.3 us -> 35.5 us  [shift(): return lax.ppermute(x, axis, [(i, (i - k) % RING) for i in range(RING)])]
    ppermute x4, waiting for transfers between devices: 0.01 us -> 14.5 us  [the longest x2 14.5 us: second(): lax.ppermute(after(step, res[0]), gy, [(i, (i - 1 + 2 * (i % 2)) % ny) fo...]
    ppermute x28, starting transfers between devices: 45.4 us -> 50.2 us  [shift(): return lax.ppermute(x, axis, [(i, (i - k) % RING) for i in range(RING)])]
    pallas_call x2, Pallas kernels: 21.5 us -> 18.4 us  [finish(): pl.pallas_call(functools.partial(far_kernel, (nblk, h, nstencil, nlinks),...]
    unnamed x82 -> x80, local copies, waits for them, and re-layouts: 7.85 us -> 7.88 us
  transfers between devices with their start and end apart: 36 -> 36, of which waited for: 19 -> 18; matrix products, arithmetic and copies ran while one was open for 5% -> 7% of each run, Pallas kernels for 13% -> 13%
where the time goes in v3:
time: 197 us; the launch traced here: 196 us
  starting transfers between devices  64.2 us (33%)
  waiting for transfers between devices  57.5 us (29%)
  Pallas kernels  53.9 us (27%)
  local copies, waits for them, and re-layouts  17.1 us (9%)
    ppermute x28, starting transfers between devices, shift(): return lax.ppermute(x, axis, [(i, (i - k) % RING) for i in range(RING)])  50.2 us
    ppermute x28, waiting for transfers between devices, shift(): return lax.ppermute(x, axis, [(i, (i - k) % RING) for i in range(RING)])  35.5 us
    pallas_call x2, Pallas kernels, finish(): pl.pallas_call(functools.partial(far_kernel, (nblk, h, nstencil, nlinks),...  18.4 us
    pallas_call x2, Pallas kernels, products(): pl.pallas_call(functools.partial(near_kernel, (nblk, nstencil, nsrc), nri...  16.1 us
    ppermute x2, waiting for transfers between devices, second(): lax.ppermute(after(step, res[0]), gy, [(i, (i - 1 + 2 * (i % 2)) % ny) fo...  14.5 us
    ppermute x2, starting transfers between devices, second(): lax.ppermute(after(step, res[0]), gy, [(i, (i - 1 + 2 * (i % 2)) % ny) fo...  9.9 us
    pallas_call x2, Pallas kernels, pack(): pl.pallas_call(functools.partial(pack_kernel, cap), out_shape=[jax.ShapeD...  9.72 us
    pallas_call x1, Pallas kernels, shards(): pl.pallas_call(functools.partial(plan_kernel, (rows, cols, nlinks, nstenc...  9.63 us
  transfers between devices with their start and end apart: 36, of which 18 were waited for; matrix products, arithmetic and copies ran while one was open for 7% of the time, Pallas kernels for 13%

profile of v3, /device:TPU:12, one launch (start us, length us, event | category | flops | bytes accessed | tf_op | source)
XLA Modules:
  0.0 195.7 jit_solution(18170674975555499683)
XLA Ops:
  10.6 9.6 %plan.1 = (s32[2,3,4,4]{3,2,1,0:T(4,128)}, s32[60]{0:T(128)}, s32[2,8,16]{2,1,0:T(8,128)}, s32[2,8]{1,0:T(2,128)}, s32[20]{0:T(128)}, /*index=5*/s32[1]{0:T(128)}) custom-call(s32[2]{0:T(128)} %pad_add_fusion.pos, s32[16,1,12,3]{3,2,1,0:T(8,128)} %copy.16.dev, s32[16,1,12,3]{3,2,1,0:T(8,128)} %copy.17.blk, s32[5,2]{1,0:T(8,128)} %copy.18.offs), custom_call_target="tpu_custom_call" | custom-call | tf_op jit(solution)/shard_map/plan/pallas_call | solution.py:306
  25.1 3.8 %collective-permute-start.6 = (bf16[6,96,256]{2,1,0:T(8,128)(2,1)S(1)}, bf16[6,96,256]{2,1,0:T(8,128)(2,1)S(1)}, u32[]{:S(2)}, u32[]{:S(2)}) collective-permute-start(bf16[6,96,256]{2,1,0:T(8,128)(2,1)S(1)} %slice.120), channel_id=1, source_target_pairs={{0,24},{8,0},{16,8},{24,16},{1,25},{9,1},{17,9},{25,17},{2,26},{10... | collective-permute-start | bytes 884744 | tf_op jit(solution)/shard_map/ppermute | solution.py:329
  30.4 4.2 %collective-permute-done.5.refs_1_ = bf16[3,192,256]{2,1,0:T(8,128)(2,1)S(1)} collective-permute-done((bf16[3,192,256]{2,1,0:T(8,128)(2,1)S(1)}, bf16[3,192,256]{2,1,0:T(8,128)(2,1)S(1)}, u32[]{:S(2)}, u32[]{:S(2)}) %collective-permute-start.5) | collective-permute-done | bytes 294944 | tf_op jit(solution)/shard_map/ppermute | solution.py:332
  34.6 3.4 %collective-permute-done.6.refs_2_ = bf16[6,96,256]{2,1,0:T(8,128)(2,1)S(1)} collective-permute-done((bf16[6,96,256]{2,1,0:T(8,128)(2,1)S(1)}, bf16[6,96,256]{2,1,0:T(8,128)(2,1)S(1)}, u32[]{:S(2)}, u32[]{:S(2)}) %collective-permute-start.6) | collective-permute-done | bytes 294944 | tf_op jit(solution)/shard_map/ppermute | solution.py:329
  39.0 4.8 %pack.2 = (bf16[16,96,256]{2,1,0:T(8,128)(2,1)}, bf16[16,96,256]{2,1,0:T(8,128)(2,1)}, bf16[16,96,256]{2,1,0:T(8,128)(2,1)}, bf16[16,96,256]{2,1,0:T(8,128)(2,1)...) custom-call(s32[2,3,4,4]{3,2,1,0:T(4,128)} %get-tuple-element.59.send, bf16[12,96,256]{2,1,0:T(8,128)(2,1)} %copy-done.3, ...), custom_call_target="tpu_custom_call" | custom-call | tf_op jit(solution)/shard_map/pack/pallas_call | solution.py:347
  48.4 7.2 %near.2.refs_20_ = f32[12,192,256]{2,1,0:T(8,128)} custom-call(s32[60]{0:T(128)} %get-tuple-element.66.near, bf16[12,192,256]{2,1,0:T(8,128)(2,1)} %bitcast.34, bf16[3,192,256]{2,1,0:T(8,128)(2,1)} %collective-permute-done.4.refs_0_, bf16[3,192,256]{2,1,0:T(8,128)(2,1)} %copy-done.19, bf16[12,9,256,256]{3,2,1,0:T(8,128)(2,1)} %bitcast.29, ...), custom_call_target="tpu_custom_call" | custom-call | tf_op jit(solution)/shard_map/near/pallas_call | solution.py:392
  56.6 5.0 %collective-permute-done.13.refs_12_ = bf16[16,96,256]{2,1,0:T(8,128)(2,1)S(1)} collective-permute-done((bf16[16,96,256]{2,1,0:T(8,128)(2,1)}, bf16[16,96,256]{2,1,0:T(8,128)(2,1)S(1)}, u32[]{:S(2)}, u32[]{:S(2)}) %collective-permute-start.13) | collective-permute-done | bytes 786464 | tf_op jit(solution)/shard_map/ppermute | solution.py:329
  61.5 3.5 %collective-permute-done.14.refs_14_ = bf16[16,96,256]{2,1,0:T(8,128)(2,1)S(1)} collective-permute-done((bf16[16,96,256]{2,1,0:T(8,128)(2,1)}, bf16[16,96,256]{2,1,0:T(8,128)(2,1)S(1)}, u32[]{:S(2)}, u32[]{:S(2)}) %collective-permute-start.14) | collective-permute-done | bytes 786464 | tf_op jit(solution)/shard_map/ppermute | solution.py:329
  68.4 4.8 %collective-permute-start.15 = (bf16[16,96,256]{2,1,0:T(8,128)(2,1)}, bf16[16,96,256]{2,1,0:T(8,128)(2,1)}, u32[]{:S(2)}, u32[]{:S(2)}) collective-permute-start(bf16[16,96,256]{2,1,0:T(8,128)(2,1)} %get-tuple-element.72), channel_id=1, source_target_pairs={{0,16},{8,24},{16,0},{24,8},{1,17},{9,25},{17,1},{25,9},{2,18},{10... | collective-permute-start | bytes 2359304 | tf_op jit(solution)/shard_map/ppermute | solution.py:329
  75.2 4.1 %collective-permute-start.17 = (bf16[6,192,256]{2,1,0:T(8,128)(2,1)S(1)}, bf16[6,192,256]{2,1,0:T(8,128)(2,1)S(1)}, u32[]{:S(2)}, u32[]{:S(2)}) collective-permute-start(bf16[6,192,256]{2,1,0:T(8,128)(2,1)S(1)} %get-tuple-element.74), channel_id=1, source_target_pairs={{0,7},{1,2},{2,1},{3,4},{4,3},{5,6},{6,5},{7,0},{8,15},{9,10},{10,... | collective-permute-start | bytes 1769480 | tf_op jit(solution)/shard_map/ppermute | solution.py:373
  79.9 6.9 %collective-permute-done.17.refs_17_ = bf16[6,192,256]{2,1,0:T(8,128)(2,1)S(1)} collective-permute-done((bf16[6,192,256]{2,1,0:T(8,128)(2,1)S(1)}, bf16[6,192,256]{2,1,0:T(8,128)(2,1)S(1)}, u32[]{:S(2)}, u32[]{:S(2)}) %collective-permute-start.17) | collective-permute-done | bytes 589856 | tf_op jit(solution)/shard_map/ppermute | solution.py:373
  87.9 8.4 %far.2 = (bf16[12,96,256]{2,1,0:T(8,128)(2,1)}, bf16[12,96,256]{2,1,0:T(8,128)(2,1)}, bf16[12,192,256]{2,1,0:T(8,128)(2,1)}) custom-call(s32[2,8,16]{2,1,0:T(8,128)} %get-tuple-element.51.far, s32[2,8]{1,0:T(2,128)} %get-tuple-element.52.count, s32[20]{0:T(128)} %get-tuple-element.53.beside, s32[1]{0:T(128)} %get-tuple-element.54.nbeside, ...), custom_call_target="tpu_custom_call" | custom-call | tf_op jit(solution)/shard_map/far/pallas_call | solution.py:425
  101.8 9.0 %collective-permute-done.19.refs_4_.refs_3_ = bf16[12,96,256]{2,1,0:T(8,128)(2,1)S(1)} collective-permute-done((bf16[12,96,256]{2,1,0:T(8,128)(2,1)}, bf16[12,96,256]{2,1,0:T(8,128)(2,1)S(1)}, u32[]{:S(2)}, u32[]{:S(2)}) %collective-permute-start.19) | collective-permute-done | bytes 589856 | tf_op jit(solution)/shard_map/ppermute | solution.py:329
  116.5 3.4 %collective-permute-start.24 = (bf16[6,96,256]{2,1,0:T(8,128)(2,1)S(1)}, bf16[6,96,256]{2,1,0:T(8,128)(2,1)S(1)}, u32[]{:S(2)}, u32[]{:S(2)}) collective-permute-start(bf16[6,96,256]{2,1,0:T(8,128)(2,1)S(1)} %slice.128), channel_id=1, source_target_pairs={{0,24},{8,0},{16,8},{24,16},{1,25},{9,1},{17,9},{25,17},{2,26},{10... | collective-permute-start | bytes 884744 | tf_op jit(solution)/shard_map/ppermute | solution.py:329
  119.9 3.3 %collective-permute-done.22.refs_0_ = bf16[3,192,256]{2,1,0:T(8,128)(2,1)S(1)} collective-permute-done((bf16[3,192,256]{2,1,0:T(8,128)(2,1)S(1)}, bf16[3,192,256]{2,1,0:T(8,128)(2,1)S(1)}, u32[]{:S(2)}, u32[]{:S(2)}) %collective-permute-start.22) | collective-permute-done | bytes 294944 | tf_op jit(solution)/shard_map/ppermute | solution.py:332
  130.7 4.9 %pack.3 = (bf16[16,96,256]{2,1,0:T(8,128)(2,1)}, bf16[16,96,256]{2,1,0:T(8,128)(2,1)}, bf16[16,96,256]{2,1,0:T(8,128)(2,1)}, bf16[16,96,256]{2,1,0:T(8,128)(2,1)...) custom-call(s32[2,3,4,4]{3,2,1,0:T(4,128)} %get-tuple-element.59.send, ...), custom_call_target="tpu_custom_call" | custom-call | tf_op jit(solution)/shard_map/pack/pallas_call | solution.py:347
  135.6 3.8 %collective-permute-start.31 = (bf16[16,96,256]{2,1,0:T(8,128)(2,1)}, bf16[16,96,256]{2,1,0:T(8,128)(2,1)S(1)}, u32[]{:S(2)}, u32[]{:S(2)}) collective-permute-start(bf16[16,96,256]{2,1,0:T(8,128)(2,1)} %get-tuple-element.91), channel_id=1, source_target_pairs={{0,24},{8,0},{16,8},{24,16},{1,25},{9,1},{17,9},{25,17},{2,26},{10... | collective-permute-start | bytes 2359304 | tf_op jit(solution)/shard_map/ppermute | solution.py:329
  141.6 9.0 %near.3 = (f32[12,192,256]{2,1,0:T(8,128)}, f32[12,256,256]{2,1,0:T(8,128)}) custom-call(s32[60]{0:T(128)} %get-tuple-element.66.near, bf16[12,192,256]{2,1,0:T(8,128)(2,1)} %get-tuple-element.88.own_ref.refs_18_, bf16[3,192,256]{2,1,0:T(8,128)(2,1)} %copy-done.20, bf16[3,192,256]{2,1,0:T(8,128)(2,1)} %copy-done.18, bf16[12,9,256,256]{3,2,1,0:T(8,128)(2,1)} %bitcast.31, ...), custom_call_target="tpu_custom_call" | custom-call | tf_op jit(solution)/shard_map/near/pallas_call | solution.py:392
  153.5 4.0 %collective-permute-done.29.refs_6_ = bf16[16,96,256]{2,1,0:T(8,128)(2,1)S(1)} collective-permute-done((bf16[16,96,256]{2,1,0:T(8,128)(2,1)}, bf16[16,96,256]{2,1,0:T(8,128)(2,1)S(1)}, u32[]{:S(2)}, u32[]{:S(2)}) %collective-permute-start.29) | collective-permute-done | bytes 786464 | tf_op jit(solution)/shard_map/ppermute | solution.py:329
  157.5 7.5 %collective-permute-start.30 = (bf16[16,96,256]{2,1,0:T(8,128)(2,1)S(1)}, bf16[16,96,256]{2,1,0:T(8,128)(2,1)S(1)}, u32[]{:S(2)}, u32[]{:S(2)}) collective-permute-start(bf16[16,96,256]{2,1,0:T(8,128)(2,1)S(1)} %copy-done.37), channel_id=1, source_target_pairs={{0,64},{32,96},{64,0},{96,32},{1,65},{33,97},{65,1},{97,33},{2,66}... | collective-permute-start | bytes 2359304 | tf_op jit(solution)/shard_map/ppermute | solution.py:329
  165.0 4.6 %collective-permute-start.33 = (bf16[16,96,256]{2,1,0:T(8,128)(2,1)S(1)}, bf16[16,96,256]{2,1,0:T(8,128)(2,1)S(1)}, u32[]{:S(2)}, u32[]{:S(2)}) collective-permute-start(bf16[16,96,256]{2,1,0:T(8,128)(2,1)S(1)} %copy-done.36), channel_id=1, source_target_pairs={{0,16},{8,24},{16,0},{24,8},{1,17},{9,25},{17,1},{25,9},{2,18},{10... | collective-permute-start | bytes 2359304 | tf_op jit(solution)/shard_map/ppermute | solution.py:329
  170.9 5.8 %collective-permute-start.35 = (bf16[6,192,256]{2,1,0:T(8,128)(2,1)S(1)}, bf16[6,192,256]{2,1,0:T(8,128)(2,1)S(1)}, u32[]{:S(2)}, u32[]{:S(2)}) collective-permute-start(bf16[6,192,256]{2,1,0:T(8,128)(2,1)S(1)} %get-tuple-element.96), channel_id=1, source_target_pairs={{0,7},{1,2},{2,1},{3,4},{4,3},{5,6},{6,5},{7,0},{8,15},{9,10},{10,... | collective-permute-start | bytes 1769480 | tf_op jit(solution)/shard_map/ppermute | solution.py:373
  176.7 7.6 %collective-permute-done.35.refs_17_ = bf16[6,192,256]{2,1,0:T(8,128)(2,1)S(1)} collective-permute-done((bf16[6,192,256]{2,1,0:T(8,128)(2,1)S(1)}, bf16[6,192,256]{2,1,0:T(8,128)(2,1)S(1)}, u32[]{:S(2)}, u32[]{:S(2)}) %collective-permute-start.35) | collective-permute-done | bytes 589856 | tf_op jit(solution)/shard_map/ppermute | solution.py:373
  185.6 10.0 %far.3 = (bf16[12,192,256]{2,1,0:T(8,128)(2,1)}, f32[12,256,256]{2,1,0:T(8,128)}) custom-call(s32[2,8,16]{2,1,0:T(8,128)} %get-tuple-element.51.far, s32[2,8]{1,0:T(2,128)} %get-tuple-element.52.count, s32[20]{0:T(128)} %get-tuple-element.53.beside, s32[1]{0:T(128)} %get-tuple-element.54.nbeside, bf16[12,96,256]{2,1,0:T(8,128)(2,1)} %get-tuple-element.80.refs_0_, ...), custom_call_target="tpu_custom_call" | custom-call | tf_op jit(solution)/shard_map/far/pallas_call | solution.py:425
  (156 shorter events, 55.8 us)
Async XLA Ops:
  2.1 18.2 %collective-permute-start.1 = (bf16[12,96,256]{2,1,0:T(8,128)(2,1)S(1)}, bf16[12,96,256]{2,1,0:T(8,128)(2,1)S(1)}, u32[]{:S(2)}, u32[]{:S(2)}) collective-permute-start(bf16[12,96,256]{2,1,0:T(8,128)(2,1)S(1)} %get-tuple-element.57.refs_0_), channel_id=1, source_target_pairs={{0,8},{8,16},{16,24},{24,0},{1,9},{9,17},{17,25},{25,1},{2,10},{10... | collective-permute-start | bytes 1769480 | tf_op jit(solution)/shard_map/ppermute | solution.py:329
  3.7 16.6 %collective-permute-start = (bf16[12,96,256]{2,1,0:T(8,128)(2,1)S(1)}, bf16[12,96,256]{2,1,0:T(8,128)(2,1)S(1)}, u32[]{:S(2)}, u32[]{:S(2)}) collective-permute-start(bf16[12,96,256]{2,1,0:T(8,128)(2,1)S(1)} %get-tuple-element.57.refs_0_), channel_id=1, source_target_pairs={{0,24},{8,0},{16,8},{24,16},{1,25},{9,1},{17,9},{25,17},{2,26},{10... | collective-permute-start | bytes 1769480 | tf_op jit(solution)/shard_map/ppermute | solution.py:329
  4.2 16.1 %collective-permute-start.3 = (bf16[12,96,256]{2,1,0:T(8,128)(2,1)S(1)}, bf16[12,96,256]{2,1,0:T(8,128)(2,1)}, u32[]{:S(2)}, u32[]{:S(2)}) collective-permute-start(bf16[12,96,256]{2,1,0:T(8,128)(2,1)S(1)} %get-tuple-element.112.refs_5_.refs_8_), channel_id=1, source_target_pairs={{0,32},{32,64},{64,96},{96,0},{1,33},{33,65},{65,97},{97,1},{2,34}... | collective-permute-start | bytes 1769480 | tf_op jit(solution)/shard_map/ppermute | solution.py:329
  5.4 15.0 %collective-permute-start.2 = (bf16[12,96,256]{2,1,0:T(8,128)(2,1)S(1)}, bf16[12,96,256]{2,1,0:T(8,128)(2,1)}, u32[]{:S(2)}, u32[]{:S(2)}) collective-permute-start(bf16[12,96,256]{2,1,0:T(8,128)(2,1)S(1)} %get-tuple-element.112.refs_5_.refs_8_), channel_id=1, source_target_pairs={{0,96},{32,0},{64,32},{96,64},{1,97},{33,1},{65,33},{97,65},{2,98}... | collective-permute-start | bytes 1769480 | tf_op jit(solution)/shard_map/ppermute | solution.py:329
  25.1 12.9 %collective-permute-start.6 = (bf16[6,96,256]{2,1,0:T(8,128)(2,1)S(1)}, bf16[6,96,256]{2,1,0:T(8,128)(2,1)S(1)}, u32[]{:S(2)}, u32[]{:S(2)}) collective-permute-start(bf16[6,96,256]{2,1,0:T(8,128)(2,1)S(1)} %slice.120), channel_id=1, source_target_pairs={{0,24},{8,0},{16,8},{24,16},{1,25},{9,1},{17,9},{25,17},{2,26},{10... | collective-permute-start | bytes 884744 | tf_op jit(solution)/shard_map/ppermute | solution.py:329
  43.9 17.7 %collective-permute-start.13 = (bf16[16,96,256]{2,1,0:T(8,128)(2,1)}, bf16[16,96,256]{2,1,0:T(8,128)(2,1)S(1)}, u32[]{:S(2)}, u32[]{:S(2)}) collective-permute-start(bf16[16,96,256]{2,1,0:T(8,128)(2,1)} %get-tuple-element.69), channel_id=1, source_target_pairs={{0,24},{8,0},{16,8},{24,16},{1,25},{9,1},{17,9},{25,17},{2,26},{10... | collective-permute-start | bytes 2359304 | tf_op jit(solution)/shard_map/ppermute | solution.py:329
  45.8 19.2 %collective-permute-start.14 = (bf16[16,96,256]{2,1,0:T(8,128)(2,1)}, bf16[16,96,256]{2,1,0:T(8,128)(2,1)S(1)}, u32[]{:S(2)}, u32[]{:S(2)}) collective-permute-start(bf16[16,96,256]{2,1,0:T(8,128)(2,1)} %get-tuple-element.71), channel_id=1, source_target_pairs={{0,8},{8,16},{16,24},{24,0},{1,9},{9,17},{17,25},{25,1},{2,10},{10... | collective-permute-start | bytes 2359304 | tf_op jit(solution)/shard_map/ppermute | solution.py:329
  46.0 19.0 %collective-permute-start.10 = (bf16[16,96,256]{2,1,0:T(8,128)(2,1)}, bf16[16,96,256]{2,1,0:T(8,128)(2,1)}, u32[]{:S(2)}, u32[]{:S(2)}) collective-permute-start(bf16[16,96,256]{2,1,0:T(8,128)(2,1)} %get-tuple-element.63), channel_id=1, source_target_pairs={{0,96},{32,0},{64,32},{96,64},{1,97},{33,1},{65,33},{97,65},{2,98}... | collective-permute-start | bytes 2359304 | tf_op jit(solution)/shard_map/ppermute | solution.py:329
  48.4 18.0 %collective-permute-start.11 = (bf16[16,96,256]{2,1,0:T(8,128)(2,1)}, bf16[16,96,256]{2,1,0:T(8,128)(2,1)}, u32[]{:S(2)}, u32[]{:S(2)}) collective-permute-start(bf16[16,96,256]{2,1,0:T(8,128)(2,1)} %get-tuple-element.65), channel_id=1, source_target_pairs={{0,32},{32,64},{64,96},{96,0},{1,33},{33,65},{65,97},{97,1},{2,34}... | collective-permute-start | bytes 2359304 | tf_op jit(solution)/shard_map/ppermute | solution.py:329
  66.3 20.5 %collective-permute-start.12 = (bf16[16,96,256]{2,1,0:T(8,128)(2,1)}, bf16[16,96,256]{2,1,0:T(8,128)(2,1)S(1)}, u32[]{:S(2)}, u32[]{:S(2)}) collective-permute-start(bf16[16,96,256]{2,1,0:T(8,128)(2,1)} %get-tuple-element.68), channel_id=1, source_target_pairs={{0,64},{32,96},{64,0},{96,32},{1,65},{33,97},{65,1},{97,33},{2,66}... | collective-permute-start | bytes 2359304 | tf_op jit(solution)/shard_map/ppermute | solution.py:329
  68.4 18.7 %collective-permute-start.15 = (bf16[16,96,256]{2,1,0:T(8,128)(2,1)}, bf16[16,96,256]{2,1,0:T(8,128)(2,1)}, u32[]{:S(2)}, u32[]{:S(2)}) collective-permute-start(bf16[16,96,256]{2,1,0:T(8,128)(2,1)} %get-tuple-element.72), channel_id=1, source_target_pairs={{0,16},{8,24},{16,0},{24,8},{1,17},{9,25},{17,1},{25,9},{2,18},{10... | collective-permute-start | bytes 2359304 | tf_op jit(solution)/shard_map/ppermute | solution.py:329
  75.2 11.7 %collective-permute-start.17 = (bf16[6,192,256]{2,1,0:T(8,128)(2,1)S(1)}, bf16[6,192,256]{2,1,0:T(8,128)(2,1)S(1)}, u32[]{:S(2)}, u32[]{:S(2)}) collective-permute-start(bf16[6,192,256]{2,1,0:T(8,128)(2,1)S(1)} %get-tuple-element.74), channel_id=1, source_target_pairs={{0,7},{1,2},{2,1},{3,4},{4,3},{5,6},{6,5},{7,0},{8,15},{9,10},{10,... | collective-permute-start | bytes 1769480 | tf_op jit(solution)/shard_map/ppermute | solution.py:373
  96.3 14.5 %collective-permute-start.19 = (bf16[12,96,256]{2,1,0:T(8,128)(2,1)}, bf16[12,96,256]{2,1,0:T(8,128)(2,1)S(1)}, u32[]{:S(2)}, u32[]{:S(2)}) collective-permute-start(bf16[12,96,256]{2,1,0:T(8,128)(2,1)} %get-tuple-element.80.refs_0_), channel_id=1, source_target_pairs={{0,8},{8,16},{16,24},{24,0},{1,9},{9,17},{17,25},{25,1},{2,10},{10... | collective-permute-start | bytes 1769480 | tf_op jit(solution)/shard_map/ppermute | solution.py:329
  97.3 13.6 %collective-permute-start.18 = (bf16[12,96,256]{2,1,0:T(8,128)(2,1)}, bf16[12,96,256]{2,1,0:T(8,128)(2,1)S(1)}, u32[]{:S(2)}, u32[]{:S(2)}) collective-permute-start(bf16[12,96,256]{2,1,0:T(8,128)(2,1)} %get-tuple-element.80.refs_0_), channel_id=1, source_target_pairs={{0,24},{8,0},{16,8},{24,16},{1,25},{9,1},{17,9},{25,17},{2,26},{10... | collective-permute-start | bytes 1769480 | tf_op jit(solution)/shard_map/ppermute | solution.py:329
  98.4 13.8 %collective-permute-start.21 = (bf16[12,96,256]{2,1,0:T(8,128)(2,1)}, bf16[12,96,256]{2,1,0:T(8,128)(2,1)S(1)}, u32[]{:S(2)}, u32[]{:S(2)}) collective-permute-start(bf16[12,96,256]{2,1,0:T(8,128)(2,1)} %get-tuple-element.77.refs_5_.refs_8_), channel_id=1, source_target_pairs={{0,32},{32,64},{64,96},{96,0},{1,33},{33,65},{65,97},{97,1},{2,34}... | collective-permute-start | bytes 1769480 | tf_op jit(solution)/shard_map/ppermute | solution.py:329
  100.7 12.9 %collective-permute-start.20 = (bf16[12,96,256]{2,1,0:T(8,128)(2,1)}, bf16[12,96,256]{2,1,0:T(8,128)(2,1)S(1)}, u32[]{:S(2)}, u32[]{:S(2)}) collective-permute-start(bf16[12,96,256]{2,1,0:T(8,128)(2,1)} %get-tuple-element.77.refs_5_.refs_8_), channel_id=1, source_target_pairs={{0,96},{32,0},{64,32},{96,64},{1,97},{33,1},{65,33},{97,65},{2,98}... | collective-permute-start | bytes 1769480 | tf_op jit(solution)/shard_map/ppermute | solution.py:329
  114.4 11.3 %collective-permute-start.26 = (bf16[6,96,256]{2,1,0:T(8,128)(2,1)S(1)}, bf16[6,96,256]{2,1,0:T(8,128)(2,1)S(1)}, u32[]{:S(2)}, u32[]{:S(2)}) collective-permute-start(bf16[6,96,256]{2,1,0:T(8,128)(2,1)S(1)} %slice.130), channel_id=1, source_target_pairs={{0,96},{32,0},{64,32},{96,64},{1,97},{33,1},{65,33},{97,65},{2,98}... | collective-permute-start | bytes 884744 | tf_op jit(solution)/shard_map/ppermute | solution.py:329
  135.6 15.9 %collective-permute-start.31 = (bf16[16,96,256]{2,1,0:T(8,128)(2,1)}, bf16[16,96,256]{2,1,0:T(8,128)(2,1)S(1)}, u32[]{:S(2)}, u32[]{:S(2)}) collective-permute-start(bf16[16,96,256]{2,1,0:T(8,128)(2,1)} %get-tuple-element.91), channel_id=1, source_target_pairs={{0,24},{8,0},{16,8},{24,16},{1,25},{9,1},{17,9},{25,17},{2,26},{10... | collective-permute-start | bytes 2359304 | tf_op jit(solution)/shard_map/ppermute | solution.py:329
  139.4 12.6 %collective-permute-start.32 = (bf16[16,96,256]{2,1,0:T(8,128)(2,1)}, bf16[16,96,256]{2,1,0:T(8,128)(2,1)S(1)}, u32[]{:S(2)}, u32[]{:S(2)}) collective-permute-start(bf16[16,96,256]{2,1,0:T(8,128)(2,1)} %get-tuple-element.93), channel_id=1, source_target_pairs={{0,8},{8,16},{16,24},{24,0},{1,9},{9,17},{17,25},{25,1},{2,10},{10... | collective-permute-start | bytes 2359304 | tf_op jit(solution)/shard_map/ppermute | solution.py:329
  139.4 14.1 %collective-permute-start.28 = (bf16[16,96,256]{2,1,0:T(8,128)(2,1)}, bf16[16,96,256]{2,1,0:T(8,128)(2,1)S(1)}, u32[]{:S(2)}, u32[]{:S(2)}) collective-permute-start(bf16[16,96,256]{2,1,0:T(8,128)(2,1)} %get-tuple-element.85), channel_id=1, source_target_pairs={{0,96},{32,0},{64,32},{96,64},{1,97},{33,1},{65,33},{97,65},{2,98}... | collective-permute-start | bytes 2359304 | tf_op jit(solution)/shard_map/ppermute | solution.py:329
  139.9 17.6 %collective-permute-start.29 = (bf16[16,96,256]{2,1,0:T(8,128)(2,1)}, bf16[16,96,256]{2,1,0:T(8,128)(2,1)S(1)}, u32[]{:S(2)}, u32[]{:S(2)}) collective-permute-start(bf16[16,96,256]{2,1,0:T(8,128)(2,1)} %get-tuple-element.87), channel_id=1, source_target_pairs={{0,32},{32,64},{64,96},{96,0},{1,33},{33,65},{65,97},{97,1},{2,34}... | collective-permute-start | bytes 2359304 | tf_op jit(solution)/shard_map/ppermute | solution.py:329
  157.5 26.7 %collective-permute-start.30 = (bf16[16,96,256]{2,1,0:T(8,128)(2,1)S(1)}, bf16[16,96,256]{2,1,0:T(8,128)(2,1)S(1)}, u32[]{:S(2)}, u32[]{:S(2)}) collective-permute-start(bf16[16,96,256]{2,1,0:T(8,128)(2,1)S(1)} %copy-done.37), channel_id=1, source_target_pairs={{0,64},{32,96},{64,0},{96,32},{1,65},{33,97},{65,1},{97,33},{2,66}... | collective-permute-start | bytes 2359304 | tf_op jit(solution)/shard_map/ppermute | solution.py:329
  165.0 19.2 %collective-permute-start.33 = (bf16[16,96,256]{2,1,0:T(8,128)(2,1)S(1)}, bf16[16,96,256]{2,1,0:T(8,128)(2,1)S(1)}, u32[]{:S(2)}, u32[]{:S(2)}) collective-permute-start(bf16[16,96,256]{2,1,0:T(8,128)(2,1)S(1)} %copy-done.36), channel_id=1, source_target_pairs={{0,16},{8,24},{16,0},{24,8},{1,17},{9,25},{17,1},{25,9},{2,18},{10... | collective-permute-start | bytes 2359304 | tf_op jit(solution)/shard_map/ppermute | solution.py:329
  170.9 13.4 %collective-permute-start.35 = (bf16[6,192,256]{2,1,0:T(8,128)(2,1)S(1)}, bf16[6,192,256]{2,1,0:T(8,128)(2,1)S(1)}, u32[]{:S(2)}, u32[]{:S(2)}) collective-permute-start(bf16[6,192,256]{2,1,0:T(8,128)(2,1)S(1)} %get-tuple-element.96), channel_id=1, source_target_pairs={{0,7},{1,2},{2,1},{3,4},{4,3},{5,6},{6,5},{7,0},{8,15},{9,10},{10,... | collective-permute-start | bytes 1769480 | tf_op jit(solution)/shard_map/ppermute | solution.py:373
  (50 other events, 448.5 us)

commit v4 on v3

--- a/solution.py
+++ b/solution.py
@@ -198,17 +198,6 @@
         pltpu.make_async_copy(core_ref, cols.at[pl.ds(0, tall)], sem.at[nblk + 2]),
         pltpu.make_async_copy(side_ref, cols.at[pl.ds(tall, tall)], sem.at[nblk + 3]),
     ]
-    for c in whole:
-        c.start()
-
-    def weight(n):
-        e = beside[n]
-        return pltpu.make_async_copy(w_ref.at[e >> 9, (e >> 6) & 7], wb.at[n], bsem.at[n])
-
-    @pl.loop(0, nbeside[0])
-    def _(n):
-        weight(n).start()
-
     for half in range(2):
         for kind in range(2 * RING):
             src = bufs[half * 2 * RING + kind]
@@ -218,6 +207,17 @@
                 e = far[half, kind, n]
                 to = got.at[e & 63, pl.ds(half * h, h)]
                 pltpu.make_async_copy(src.at[e >> 6], to, sem.at[nblk]).start()
+
+    for c in whole:
+        c.start()
+
+    def weight(n):
+        e = beside[n]
+        return pltpu.make_async_copy(w_ref.at[e >> 9, (e >> 6) & 7], wb.at[n], bsem.at[n])
+
+    @pl.loop(0, nbeside[0])
+    def _(n):
+        weight(n).start()
 
     def ins(q):
         yield pltpu.make_async_copy(own_ref.at[q], old.at[q], sem.at[q])
@@ -250,7 +250,7 @@
 
     pltpu.make_async_copy(got, got, sem.at[nblk]).wait()
 
-    group = 3
+    group = 4
     units = wl.shape[-1]
 
     @pl.loop(0, nblk // group)

time: 197 us -> 198 us (level)
    ppermute x28, starting transfers between devices: 50.2 us -> 53.7 us  [shift(): return lax.ppermute(x, axis, [(i, (i - k) % RING) for i in range(RING)])]
    ppermute x2, starting transfers between devices: 9.9 us -> 6.42 us  [second(): lax.ppermute(after(step, res[0]), gy, [(i, (i - 1 + 2 * (i % 2)) % ny) fo...]
  transfers between devices with their start and end apart: 36 -> 36, of which waited for: 18 -> 17; matrix products, arithmetic and copies ran while one was open for 7% -> 7% of each run, Pallas kernels for 13% -> 13%
where the time goes in v4:
time: 198 us; the launch traced here: 196 us
  starting transfers between devices  64.2 us (32%)
  waiting for transfers between devices  57.8 us (29%)
  Pallas kernels  54 us (27%)
  local copies, waits for them, and re-layouts  17.1 us (9%)
    ppermute x28, starting transfers between devices, shift(): return lax.ppermute(x, axis, [(i, (i - k) % RING) for i in range(RING)])  53.7 us
    ppermute x28, waiting for transfers between devices, shift(): return lax.ppermute(x, axis, [(i, (i - k) % RING) for i in range(RING)])  35.4 us
    pallas_call x2, Pallas kernels, finish(): pl.pallas_call(functools.partial(far_kernel, (nblk, h, nstencil, nlinks),...  18.5 us
    pallas_call x2, Pallas kernels, products(): pl.pallas_call(functools.partial(near_kernel, (nblk, nstencil, nsrc), nri...  16.1 us
    ppermute x2, waiting for transfers between devices, second(): lax.ppermute(after(step, res[0]), gy, [(i, (i - 1 + 2 * (i % 2)) % ny) fo...  15.2 us
    pallas_call x2, Pallas kernels, pack(): pl.pallas_call(functools.partial(pack_kernel, cap), out_shape=[jax.ShapeD...  9.72 us
    pallas_call x1, Pallas kernels, shards(): pl.pallas_call(functools.partial(plan_kernel, (rows, cols, nlinks, nstenc...  9.63 us
    unnamed x80, local copies, waits for them, and re-layouts  7.88 us
  transfers between devices with their start and end apart: 36, of which 17 were waited for; matrix products, arithmetic and copies ran while one was open for 7% of the time, Pallas kernels for 13%

profile of v4, /device:TPU:12, one launch (start us, length us, event | category | flops | bytes accessed | tf_op | source)
XLA Modules:
  0.0 196.1 jit_solution(5772781448694021153)
XLA Ops:
  10.6 9.6 %plan.1 = (s32[2,3,4,4]{3,2,1,0:T(4,128)}, s32[60]{0:T(128)}, s32[2,8,16]{2,1,0:T(8,128)}, s32[2,8]{1,0:T(2,128)}, s32[20]{0:T(128)}, /*index=5*/s32[1]{0:T(128)}) custom-call(s32[2]{0:T(128)} %pad_add_fusion.pos, s32[16,1,12,3]{3,2,1,0:T(8,128)} %copy.16.dev, s32[16,1,12,3]{3,2,1,0:T(8,128)} %copy.17.blk, s32[5,2]{1,0:T(8,128)} %copy.18.offs), custom_call_target="tpu_custom_call" | custom-call | tf_op jit(solution)/shard_map/plan/pallas_call | solution.py:306
  25.1 3.8 %collective-permute-start.6 = (bf16[6,96,256]{2,1,0:T(8,128)(2,1)S(1)}, bf16[6,96,256]{2,1,0:T(8,128)(2,1)S(1)}, u32[]{:S(2)}, u32[]{:S(2)}) collective-permute-start(bf16[6,96,256]{2,1,0:T(8,128)(2,1)S(1)} %slice.120), channel_id=1, source_target_pairs={{0,24},{8,0},{16,8},{24,16},{1,25},{9,1},{17,9},{25,17},{2,26},{10... | collective-permute-start | bytes 884744 | tf_op jit(solution)/shard_map/ppermute | solution.py:329
  30.4 4.2 %collective-permute-done.5.refs_1_ = bf16[3,192,256]{2,1,0:T(8,128)(2,1)S(1)} collective-permute-done((bf16[3,192,256]{2,1,0:T(8,128)(2,1)S(1)}, bf16[3,192,256]{2,1,0:T(8,128)(2,1)S(1)}, u32[]{:S(2)}, u32[]{:S(2)}) %collective-permute-start.5) | collective-permute-done | bytes 294944 | tf_op jit(solution)/shard_map/ppermute | solution.py:332
  34.6 3.4 %collective-permute-done.6.refs_2_ = bf16[6,96,256]{2,1,0:T(8,128)(2,1)S(1)} collective-permute-done((bf16[6,96,256]{2,1,0:T(8,128)(2,1)S(1)}, bf16[6,96,256]{2,1,0:T(8,128)(2,1)S(1)}, u32[]{:S(2)}, u32[]{:S(2)}) %collective-permute-start.6) | collective-permute-done | bytes 294944 | tf_op jit(solution)/shard_map/ppermute | solution.py:329
  39.0 4.8 %pack.2 = (bf16[16,96,256]{2,1,0:T(8,128)(2,1)}, bf16[16,96,256]{2,1,0:T(8,128)(2,1)}, bf16[16,96,256]{2,1,0:T(8,128)(2,1)}, bf16[16,96,256]{2,1,0:T(8,128)(2,1)...) custom-call(s32[2,3,4,4]{3,2,1,0:T(4,128)} %get-tuple-element.59.send, bf16[12,96,256]{2,1,0:T(8,128)(2,1)} %copy-done.3, ...), custom_call_target="tpu_custom_call" | custom-call | tf_op jit(solution)/shard_map/pack/pallas_call | solution.py:347
  48.4 7.2 %near.2.refs_20_ = f32[12,192,256]{2,1,0:T(8,128)} custom-call(s32[60]{0:T(128)} %get-tuple-element.66.near, bf16[12,192,256]{2,1,0:T(8,128)(2,1)} %bitcast.34, bf16[3,192,256]{2,1,0:T(8,128)(2,1)} %collective-permute-done.4.refs_0_, bf16[3,192,256]{2,1,0:T(8,128)(2,1)} %copy-done.19, bf16[12,9,256,256]{3,2,1,0:T(8,128)(2,1)} %bitcast.29, ...), custom_call_target="tpu_custom_call" | custom-call | tf_op jit(solution)/shard_map/near/pallas_call | solution.py:392
  56.6 5.0 %collective-permute-done.13.refs_12_ = bf16[16,96,256]{2,1,0:T(8,128)(2,1)S(1)} collective-permute-done((bf16[16,96,256]{2,1,0:T(8,128)(2,1)}, bf16[16,96,256]{2,1,0:T(8,128)(2,1)S(1)}, u32[]{:S(2)}, u32[]{:S(2)}) %collective-permute-start.13) | collective-permute-done | bytes 786464 | tf_op jit(solution)/shard_map/ppermute | solution.py:329
  61.5 3.5 %collective-permute-done.14.refs_14_ = bf16[16,96,256]{2,1,0:T(8,128)(2,1)S(1)} collective-permute-done((bf16[16,96,256]{2,1,0:T(8,128)(2,1)}, bf16[16,96,256]{2,1,0:T(8,128)(2,1)S(1)}, u32[]{:S(2)}, u32[]{:S(2)}) %collective-permute-start.14) | collective-permute-done | bytes 786464 | tf_op jit(solution)/shard_map/ppermute | solution.py:329
  68.4 4.8 %collective-permute-start.15 = (bf16[16,96,256]{2,1,0:T(8,128)(2,1)}, bf16[16,96,256]{2,1,0:T(8,128)(2,1)}, u32[]{:S(2)}, u32[]{:S(2)}) collective-permute-start(bf16[16,96,256]{2,1,0:T(8,128)(2,1)} %get-tuple-element.72), channel_id=1, source_target_pairs={{0,16},{8,24},{16,0},{24,8},{1,17},{9,25},{17,1},{25,9},{2,18},{10... | collective-permute-start | bytes 2359304 | tf_op jit(solution)/shard_map/ppermute | solution.py:329
  75.2 4.1 %collective-permute-start.17 = (bf16[6,192,256]{2,1,0:T(8,128)(2,1)S(1)}, bf16[6,192,256]{2,1,0:T(8,128)(2,1)S(1)}, u32[]{:S(2)}, u32[]{:S(2)}) collective-permute-start(bf16[6,192,256]{2,1,0:T(8,128)(2,1)S(1)} %get-tuple-element.74), channel_id=1, source_target_pairs={{0,7},{1,2},{2,1},{3,4},{4,3},{5,6},{6,5},{7,0},{8,15},{9,10},{10,... | collective-permute-start | bytes 1769480 | tf_op jit(solution)/shard_map/ppermute | solution.py:373
  79.9 6.9 %collective-permute-done.17.refs_17_ = bf16[6,192,256]{2,1,0:T(8,128)(2,1)S(1)} collective-permute-done((bf16[6,192,256]{2,1,0:T(8,128)(2,1)S(1)}, bf16[6,192,256]{2,1,0:T(8,128)(2,1)S(1)}, u32[]{:S(2)}, u32[]{:S(2)}) %collective-permute-start.17) | collective-permute-done | bytes 589856 | tf_op jit(solution)/shard_map/ppermute | solution.py:373
  87.9 8.6 %far.2 = (bf16[12,96,256]{2,1,0:T(8,128)(2,1)}, bf16[12,96,256]{2,1,0:T(8,128)(2,1)}, bf16[12,192,256]{2,1,0:T(8,128)(2,1)}) custom-call(s32[2,8,16]{2,1,0:T(8,128)} %get-tuple-element.51.far, s32[2,8]{1,0:T(2,128)} %get-tuple-element.52.count, s32[20]{0:T(128)} %get-tuple-element.53.beside, s32[1]{0:T(128)} %get-tuple-element.54.nbeside, ...), custom_call_target="tpu_custom_call" | custom-call | tf_op jit(solution)/shard_map/far/pallas_call | solution.py:425
  102.0 10.0 %collective-permute-done.19.refs_4_.refs_3_ = bf16[12,96,256]{2,1,0:T(8,128)(2,1)S(1)} collective-permute-done((bf16[12,96,256]{2,1,0:T(8,128)(2,1)}, bf16[12,96,256]{2,1,0:T(8,128)(2,1)S(1)}, u32[]{:S(2)}, u32[]{:S(2)}) %collective-permute-start.19) | collective-permute-done | bytes 589856 | tf_op jit(solution)/shard_map/ppermute | solution.py:329
  117.6 3.5 %collective-permute-start.24 = (bf16[6,96,256]{2,1,0:T(8,128)(2,1)S(1)}, bf16[6,96,256]{2,1,0:T(8,128)(2,1)S(1)}, u32[]{:S(2)}, u32[]{:S(2)}) collective-permute-start(bf16[6,96,256]{2,1,0:T(8,128)(2,1)S(1)} %slice.128), channel_id=1, source_target_pairs={{0,24},{8,0},{16,8},{24,16},{1,25},{9,1},{17,9},{25,17},{2,26},{10... | collective-permute-start | bytes 884744 | tf_op jit(solution)/shard_map/ppermute | solution.py:329
  121.1 2.9 %collective-permute-done.22.refs_0_ = bf16[3,192,256]{2,1,0:T(8,128)(2,1)S(1)} collective-permute-done((bf16[3,192,256]{2,1,0:T(8,128)(2,1)S(1)}, bf16[3,192,256]{2,1,0:T(8,128)(2,1)S(1)}, u32[]{:S(2)}, u32[]{:S(2)}) %collective-permute-start.22) | collective-permute-done | bytes 294944 | tf_op jit(solution)/shard_map/ppermute | solution.py:332
  124.0 3.6 %collective-permute-start.27 = (bf16[6,96,256]{2,1,0:T(8,128)(2,1)S(1)}, bf16[6,96,256]{2,1,0:T(8,128)(2,1)S(1)}, u32[]{:S(2)}, u32[]{:S(2)}) collective-permute-start(bf16[6,96,256]{2,1,0:T(8,128)(2,1)S(1)} %slice.131), channel_id=1, source_target_pairs={{0,32},{32,64},{64,96},{96,0},{1,33},{33,65},{65,97},{97,1},{2,34}... | collective-permute-start | bytes 884744 | tf_op jit(solution)/shard_map/ppermute | solution.py:329
  129.0 2.9 %collective-permute-done.27.refs_8_.refs_15_ = bf16[6,96,256]{2,1,0:T(8,128)(2,1)S(1)} collective-permute-done((bf16[6,96,256]{2,1,0:T(8,128)(2,1)S(1)}, bf16[6,96,256]{2,1,0:T(8,128)(2,1)S(1)}, u32[]{:S(2)}, u32[]{:S(2)}) %collective-permute-start.27) | collective-permute-done | bytes 294944 | tf_op jit(solution)/shard_map/ppermute | solution.py:329
  132.6 4.9 %pack.3 = (bf16[16,96,256]{2,1,0:T(8,128)(2,1)}, bf16[16,96,256]{2,1,0:T(8,128)(2,1)}, bf16[16,96,256]{2,1,0:T(8,128)(2,1)}, bf16[16,96,256]{2,1,0:T(8,128)(2,1)...) custom-call(s32[2,3,4,4]{3,2,1,0:T(4,128)} %get-tuple-element.59.send, ...), custom_call_target="tpu_custom_call" | custom-call | tf_op jit(solution)/shard_map/pack/pallas_call | solution.py:347
  137.5 2.8 %collective-permute-start.31 = (bf16[16,96,256]{2,1,0:T(8,128)(2,1)}, bf16[16,96,256]{2,1,0:T(8,128)(2,1)S(1)}, u32[]{:S(2)}, u32[]{:S(2)}) collective-permute-start(bf16[16,96,256]{2,1,0:T(8,128)(2,1)} %get-tuple-element.91), channel_id=1, source_target_pairs={{0,24},{8,0},{16,8},{24,16},{1,25},{9,1},{17,9},{25,17},{2,26},{10... | collective-permute-start | bytes 2359304 | tf_op jit(solution)/shard_map/ppermute | solution.py:329
  142.9 9.0 %near.3 = (f32[12,192,256]{2,1,0:T(8,128)}, f32[12,256,256]{2,1,0:T(8,128)}) custom-call(s32[60]{0:T(128)} %get-tuple-element.66.near, bf16[12,192,256]{2,1,0:T(8,128)(2,1)} %get-tuple-element.88.own_ref.refs_18_, bf16[3,192,256]{2,1,0:T(8,128)(2,1)} %copy-done.20, bf16[3,192,256]{2,1,0:T(8,128)(2,1)} %copy-done.18, bf16[12,9,256,256]{3,2,1,0:T(8,128)(2,1)} %bitcast.31, ...), custom_call_target="tpu_custom_call" | custom-call | tf_op jit(solution)/shard_map/near/pallas_call | solution.py:392
  157.8 10.4 %collective-permute-start.30 = (bf16[16,96,256]{2,1,0:T(8,128)(2,1)S(1)}, bf16[16,96,256]{2,1,0:T(8,128)(2,1)S(1)}, u32[]{:S(2)}, u32[]{:S(2)}) collective-permute-start(bf16[16,96,256]{2,1,0:T(8,128)(2,1)S(1)} %copy-done.37), channel_id=1, source_target_pairs={{0,64},{32,96},{64,0},{96,32},{1,65},{33,97},{65,1},{97,33},{2,66}... | collective-permute-start | bytes 2359304 | tf_op jit(solution)/shard_map/ppermute | solution.py:329
  168.2 4.6 %collective-permute-start.33 = (bf16[16,96,256]{2,1,0:T(8,128)(2,1)S(1)}, bf16[16,96,256]{2,1,0:T(8,128)(2,1)S(1)}, u32[]{:S(2)}, u32[]{:S(2)}) collective-permute-start(bf16[16,96,256]{2,1,0:T(8,128)(2,1)S(1)} %copy-done.36), channel_id=1, source_target_pairs={{0,16},{8,24},{16,0},{24,8},{1,17},{9,25},{17,1},{25,9},{2,18},{10... | collective-permute-start | bytes 2359304 | tf_op jit(solution)/shard_map/ppermute | solution.py:329
  176.4 8.3 %collective-permute-done.35.refs_17_ = bf16[6,192,256]{2,1,0:T(8,128)(2,1)S(1)} collective-permute-done((bf16[6,192,256]{2,1,0:T(8,128)(2,1)S(1)}, bf16[6,192,256]{2,1,0:T(8,128)(2,1)S(1)}, u32[]{:S(2)}, u32[]{:S(2)}) %collective-permute-start.35) | collective-permute-done | bytes 589856 | tf_op jit(solution)/shard_map/ppermute | solution.py:373
  186.0 9.9 %far.3 = (bf16[12,192,256]{2,1,0:T(8,128)(2,1)}, f32[12,256,256]{2,1,0:T(8,128)}) custom-call(s32[2,8,16]{2,1,0:T(8,128)} %get-tuple-element.51.far, s32[2,8]{1,0:T(2,128)} %get-tuple-element.52.count, s32[20]{0:T(128)} %get-tuple-element.53.beside, s32[1]{0:T(128)} %get-tuple-element.54.nbeside, bf16[12,96,256]{2,1,0:T(8,128)(2,1)} %get-tuple-element.80.refs_0_, ...), custom_call_target="tpu_custom_call" | custom-call | tf_op jit(solution)/shard_map/far/pallas_call | solution.py:425
  (156 shorter events, 55.9 us)
Async XLA Ops:
  2.1 18.2 %collective-permute-start.1 = (bf16[12,96,256]{2,1,0:T(8,128)(2,1)S(1)}, bf16[12,96,256]{2,1,0:T(8,128)(2,1)S(1)}, u32[]{:S(2)}, u32[]{:S(2)}) collective-permute-start(bf16[12,96,256]{2,1,0:T(8,128)(2,1)S(1)} %get-tuple-element.57.refs_0_), channel_id=1, source_target_pairs={{0,8},{8,16},{16,24},{24,0},{1,9},{9,17},{17,25},{25,1},{2,10},{10... | collective-permute-start | bytes 1769480 | tf_op jit(solution)/shard_map/ppermute | solution.py:329
  3.7 16.6 %collective-permute-start = (bf16[12,96,256]{2,1,0:T(8,128)(2,1)S(1)}, bf16[12,96,256]{2,1,0:T(8,128)(2,1)S(1)}, u32[]{:S(2)}, u32[]{:S(2)}) collective-permute-start(bf16[12,96,256]{2,1,0:T(8,128)(2,1)S(1)} %get-tuple-element.57.refs_0_), channel_id=1, source_target_pairs={{0,24},{8,0},{16,8},{24,16},{1,25},{9,1},{17,9},{25,17},{2,26},{10... | collective-permute-start | bytes 1769480 | tf_op jit(solution)/shard_map/ppermute | solution.py:329
  4.2 16.1 %collective-permute-start.3 = (bf16[12,96,256]{2,1,0:T(8,128)(2,1)S(1)}, bf16[12,96,256]{2,1,0:T(8,128)(2,1)}, u32[]{:S(2)}, u32[]{:S(2)}) collective-permute-start(bf16[12,96,256]{2,1,0:T(8,128)(2,1)S(1)} %get-tuple-element.112.refs_5_.refs_8_), channel_id=1, source_target_pairs={{0,32},{32,64},{64,96},{96,0},{1,33},{33,65},{65,97},{97,1},{2,34}... | collective-permute-start | bytes 1769480 | tf_op jit(solution)/shard_map/ppermute | solution.py:329
  5.4 15.0 %collective-permute-start.2 = (bf16[12,96,256]{2,1,0:T(8,128)(2,1)S(1)}, bf16[12,96,256]{2,1,0:T(8,128)(2,1)}, u32[]{:S(2)}, u32[]{:S(2)}) collective-permute-start(bf16[12,96,256]{2,1,0:T(8,128)(2,1)S(1)} %get-tuple-element.112.refs_5_.refs_8_), channel_id=1, source_target_pairs={{0,96},{32,0},{64,32},{96,64},{1,97},{33,1},{65,33},{97,65},{2,98}... | collective-permute-start | bytes 1769480 | tf_op jit(solution)/shard_map/ppermute | solution.py:329
  25.1 12.9 %collective-permute-start.6 = (bf16[6,96,256]{2,1,0:T(8,128)(2,1)S(1)}, bf16[6,96,256]{2,1,0:T(8,128)(2,1)S(1)}, u32[]{:S(2)}, u32[]{:S(2)}) collective-permute-start(bf16[6,96,256]{2,1,0:T(8,128)(2,1)S(1)} %slice.120), channel_id=1, source_target_pairs={{0,24},{8,0},{16,8},{24,16},{1,25},{9,1},{17,9},{25,17},{2,26},{10... | collective-permute-start | bytes 884744 | tf_op jit(solution)/shard_map/ppermute | solution.py:329
  43.9 17.7 %collective-permute-start.13 = (bf16[16,96,256]{2,1,0:T(8,128)(2,1)}, bf16[16,96,256]{2,1,0:T(8,128)(2,1)S(1)}, u32[]{:S(2)}, u32[]{:S(2)}) collective-permute-start(bf16[16,96,256]{2,1,0:T(8,128)(2,1)} %get-tuple-element.69), channel_id=1, source_target_pairs={{0,24},{8,0},{16,8},{24,16},{1,25},{9,1},{17,9},{25,17},{2,26},{10... | collective-permute-start | bytes 2359304 | tf_op jit(solution)/shard_map/ppermute | solution.py:329
  45.8 19.2 %collective-permute-start.14 = (bf16[16,96,256]{2,1,0:T(8,128)(2,1)}, bf16[16,96,256]{2,1,0:T(8,128)(2,1)S(1)}, u32[]{:S(2)}, u32[]{:S(2)}) collective-permute-start(bf16[16,96,256]{2,1,0:T(8,128)(2,1)} %get-tuple-element.71), channel_id=1, source_target_pairs={{0,8},{8,16},{16,24},{24,0},{1,9},{9,17},{17,25},{25,1},{2,10},{10... | collective-permute-start | bytes 2359304 | tf_op jit(solution)/shard_map/ppermute | solution.py:329
  46.0 19.0 %collective-permute-start.10 = (bf16[16,96,256]{2,1,0:T(8,128)(2,1)}, bf16[16,96,256]{2,1,0:T(8,128)(2,1)}, u32[]{:S(2)}, u32[]{:S(2)}) collective-permute-start(bf16[16,96,256]{2,1,0:T(8,128)(2,1)} %get-tuple-element.63), channel_id=1, source_target_pairs={{0,96},{32,0},{64,32},{96,64},{1,97},{33,1},{65,33},{97,65},{2,98}... | collective-permute-start | bytes 2359304 | tf_op jit(solution)/shard_map/ppermute | solution.py:329
  48.4 18.0 %collective-permute-start.11 = (bf16[16,96,256]{2,1,0:T(8,128)(2,1)}, bf16[16,96,256]{2,1,0:T(8,128)(2,1)}, u32[]{:S(2)}, u32[]{:S(2)}) collective-permute-start(bf16[16,96,256]{2,1,0:T(8,128)(2,1)} %get-tuple-element.65), channel_id=1, source_target_pairs={{0,32},{32,64},{64,96},{96,0},{1,33},{33,65},{65,97},{97,1},{2,34}... | collective-permute-start | bytes 2359304 | tf_op jit(solution)/shard_map/ppermute | solution.py:329
  66.3 20.5 %collective-permute-start.12 = (bf16[16,96,256]{2,1,0:T(8,128)(2,1)}, bf16[16,96,256]{2,1,0:T(8,128)(2,1)S(1)}, u32[]{:S(2)}, u32[]{:S(2)}) collective-permute-start(bf16[16,96,256]{2,1,0:T(8,128)(2,1)} %get-tuple-element.68), channel_id=1, source_target_pairs={{0,64},{32,96},{64,0},{96,32},{1,65},{33,97},{65,1},{97,33},{2,66}... | collective-permute-start | bytes 2359304 | tf_op jit(solution)/shard_map/ppermute | solution.py:329
  68.4 18.7 %collective-permute-start.15 = (bf16[16,96,256]{2,1,0:T(8,128)(2,1)}, bf16[16,96,256]{2,1,0:T(8,128)(2,1)}, u32[]{:S(2)}, u32[]{:S(2)}) collective-permute-start(bf16[16,96,256]{2,1,0:T(8,128)(2,1)} %get-tuple-element.72), channel_id=1, source_target_pairs={{0,16},{8,24},{16,0},{24,8},{1,17},{9,25},{17,1},{25,9},{2,18},{10... | collective-permute-start | bytes 2359304 | tf_op jit(solution)/shard_map/ppermute | solution.py:329
  75.2 11.7 %collective-permute-start.17 = (bf16[6,192,256]{2,1,0:T(8,128)(2,1)S(1)}, bf16[6,192,256]{2,1,0:T(8,128)(2,1)S(1)}, u32[]{:S(2)}, u32[]{:S(2)}) collective-permute-start(bf16[6,192,256]{2,1,0:T(8,128)(2,1)S(1)} %get-tuple-element.74), channel_id=1, source_target_pairs={{0,7},{1,2},{2,1},{3,4},{4,3},{5,6},{6,5},{7,0},{8,15},{9,10},{10,... | collective-permute-start | bytes 1769480 | tf_op jit(solution)/shard_map/ppermute | solution.py:373
  96.5 15.5 %collective-permute-start.19 = (bf16[12,96,256]{2,1,0:T(8,128)(2,1)}, bf16[12,96,256]{2,1,0:T(8,128)(2,1)S(1)}, u32[]{:S(2)}, u32[]{:S(2)}) collective-permute-start(bf16[12,96,256]{2,1,0:T(8,128)(2,1)} %get-tuple-element.80.refs_0_), channel_id=1, source_target_pairs={{0,8},{8,16},{16,24},{24,0},{1,9},{9,17},{17,25},{25,1},{2,10},{10... | collective-permute-start | bytes 1769480 | tf_op jit(solution)/shard_map/ppermute | solution.py:329
  97.5 14.6 %collective-permute-start.18 = (bf16[12,96,256]{2,1,0:T(8,128)(2,1)}, bf16[12,96,256]{2,1,0:T(8,128)(2,1)S(1)}, u32[]{:S(2)}, u32[]{:S(2)}) collective-permute-start(bf16[12,96,256]{2,1,0:T(8,128)(2,1)} %get-tuple-element.80.refs_0_), channel_id=1, source_target_pairs={{0,24},{8,0},{16,8},{24,16},{1,25},{9,1},{17,9},{25,17},{2,26},{10... | collective-permute-start | bytes 1769480 | tf_op jit(solution)/shard_map/ppermute | solution.py:329
  98.6 14.9 %collective-permute-start.21 = (bf16[12,96,256]{2,1,0:T(8,128)(2,1)}, bf16[12,96,256]{2,1,0:T(8,128)(2,1)S(1)}, u32[]{:S(2)}, u32[]{:S(2)}) collective-permute-start(bf16[12,96,256]{2,1,0:T(8,128)(2,1)} %get-tuple-element.77.refs_5_.refs_8_), channel_id=1, source_target_pairs={{0,32},{32,64},{64,96},{96,0},{1,33},{33,65},{65,97},{97,1},{2,34}... | collective-permute-start | bytes 1769480 | tf_op jit(solution)/shard_map/ppermute | solution.py:329
  100.9 13.9 %collective-permute-start.20 = (bf16[12,96,256]{2,1,0:T(8,128)(2,1)}, bf16[12,96,256]{2,1,0:T(8,128)(2,1)S(1)}, u32[]{:S(2)}, u32[]{:S(2)}) collective-permute-start(bf16[12,96,256]{2,1,0:T(8,128)(2,1)} %get-tuple-element.77.refs_5_.refs_8_), channel_id=1, source_target_pairs={{0,96},{32,0},{64,32},{96,64},{1,97},{33,1},{65,33},{97,65},{2,98}... | collective-permute-start | bytes 1769480 | tf_op jit(solution)/shard_map/ppermute | solution.py:329
  115.6 12.0 %collective-permute-start.26 = (bf16[6,96,256]{2,1,0:T(8,128)(2,1)S(1)}, bf16[6,96,256]{2,1,0:T(8,128)(2,1)S(1)}, u32[]{:S(2)}, u32[]{:S(2)}) collective-permute-start(bf16[6,96,256]{2,1,0:T(8,128)(2,1)S(1)} %slice.130), channel_id=1, source_target_pairs={{0,96},{32,0},{64,32},{96,64},{1,97},{33,1},{65,33},{97,65},{2,98}... | collective-permute-start | bytes 884744 | tf_op jit(solution)/shard_map/ppermute | solution.py:329
  116.1 11.6 %collective-permute-start.23 = (bf16[3,192,256]{2,1,0:T(8,128)(2,1)S(1)}, bf16[3,192,256]{2,1,0:T(8,128)(2,1)S(1)}, u32[]{:S(2)}, u32[]{:S(2)}) collective-permute-start(bf16[3,192,256]{2,1,0:T(8,128)(2,1)S(1)} %get-tuple-element.79), channel_id=1, source_target_pairs={{0,120},{8,0},{16,8},{24,16},{32,24},{40,32},{48,40},{56,48},{64,5... | collective-permute-start | bytes 884744 | tf_op jit(solution)/shard_map/ppermute | solution.py:332
  137.5 15.3 %collective-permute-start.31 = (bf16[16,96,256]{2,1,0:T(8,128)(2,1)}, bf16[16,96,256]{2,1,0:T(8,128)(2,1)S(1)}, u32[]{:S(2)}, u32[]{:S(2)}) collective-permute-start(bf16[16,96,256]{2,1,0:T(8,128)(2,1)} %get-tuple-element.91), channel_id=1, source_target_pairs={{0,24},{8,0},{16,8},{24,16},{1,25},{9,1},{17,9},{25,17},{2,26},{10... | collective-permute-start | bytes 2359304 | tf_op jit(solution)/shard_map/ppermute | solution.py:329
  140.3 15.2 %collective-permute-start.32 = (bf16[16,96,256]{2,1,0:T(8,128)(2,1)}, bf16[16,96,256]{2,1,0:T(8,128)(2,1)S(1)}, u32[]{:S(2)}, u32[]{:S(2)}) collective-permute-start(bf16[16,96,256]{2,1,0:T(8,128)(2,1)} %get-tuple-element.93), channel_id=1, source_target_pairs={{0,8},{8,16},{16,24},{24,0},{1,9},{9,17},{17,25},{25,1},{2,10},{10... | collective-permute-start | bytes 2359304 | tf_op jit(solution)/shard_map/ppermute | solution.py:329
  140.3 15.2 %collective-permute-start.28 = (bf16[16,96,256]{2,1,0:T(8,128)(2,1)}, bf16[16,96,256]{2,1,0:T(8,128)(2,1)S(1)}, u32[]{:S(2)}, u32[]{:S(2)}) collective-permute-start(bf16[16,96,256]{2,1,0:T(8,128)(2,1)} %get-tuple-element.85), channel_id=1, source_target_pairs={{0,96},{32,0},{64,32},{96,64},{1,97},{33,1},{65,33},{97,65},{2,98}... | collective-permute-start | bytes 2359304 | tf_op jit(solution)/shard_map/ppermute | solution.py:329
  140.3 17.5 %collective-permute-start.29 = (bf16[16,96,256]{2,1,0:T(8,128)(2,1)}, bf16[16,96,256]{2,1,0:T(8,128)(2,1)S(1)}, u32[]{:S(2)}, u32[]{:S(2)}) collective-permute-start(bf16[16,96,256]{2,1,0:T(8,128)(2,1)} %get-tuple-element.87), channel_id=1, source_target_pairs={{0,32},{32,64},{64,96},{96,0},{1,33},{33,65},{65,97},{97,1},{2,34}... | collective-permute-start | bytes 2359304 | tf_op jit(solution)/shard_map/ppermute | solution.py:329
  157.8 26.9 %collective-permute-start.30 = (bf16[16,96,256]{2,1,0:T(8,128)(2,1)S(1)}, bf16[16,96,256]{2,1,0:T(8,128)(2,1)S(1)}, u32[]{:S(2)}, u32[]{:S(2)}) collective-permute-start(bf16[16,96,256]{2,1,0:T(8,128)(2,1)S(1)} %copy-done.37), channel_id=1, source_target_pairs={{0,64},{32,96},{64,0},{96,32},{1,65},{33,97},{65,1},{97,33},{2,66}... | collective-permute-start | bytes 2359304 | tf_op jit(solution)/shard_map/ppermute | solution.py:329
  168.2 16.5 %collective-permute-start.33 = (bf16[16,96,256]{2,1,0:T(8,128)(2,1)S(1)}, bf16[16,96,256]{2,1,0:T(8,128)(2,1)S(1)}, u32[]{:S(2)}, u32[]{:S(2)}) collective-permute-start(bf16[16,96,256]{2,1,0:T(8,128)(2,1)S(1)} %copy-done.36), channel_id=1, source_target_pairs={{0,16},{8,24},{16,0},{24,8},{1,17},{9,25},{17,1},{25,9},{2,18},{10... | collective-permute-start | bytes 2359304 | tf_op jit(solution)/shard_map/ppermute | solution.py:329
  (50 other events, 451.5 us)
